TPU v7x, 128 devices: a whole 4x4x4 slice. The times are simulated.
128 devices in a mesh: dp: 8 (over z, x_lo), tensor: 16 (over y, x_hi, core).
Axes of the slice: x: 4 (x_hi: 2, x_lo: 2; x = x_hi * 2 + x_lo), y: 4, z: 4, core: 2. Of those that a mesh axis runs over, the one named last changes fastest.
Arguments:
- tokens: bfloat16 [8, 256, 8192], P('dp', None, 'tensor'), may hold values from -6 to 6
- gain: bfloat16 [8192], replicated, may hold values from 0.3984375 to 1.59375
- q_weight: bfloat16 [8192, 8192], P(None, 'tensor'), may hold values from -1 to 1
- kv_weight: bfloat16 [8192, 2048], P(None, 'tensor'), may hold values from -1 to 1
- o_weight: bfloat16 [8192, 8192], P('tensor'), may hold values from -0.0625 to 0.0625
- out_grad: bfloat16 [8, 256, 8192], P('dp', None, 'tensor'), may hold values from -6 to 6
Outputs:
- output: bfloat16 [8, 256, 8192], P('dp', 'tensor')
- x_grad: bfloat16 [8, 256, 8192], P('dp', 'tensor')
- gain_grad: float32 [8192], P('dp')
- q_grad: float32 [8192, 8192], P('dp', 'tensor')
- kv_grad: float32 [8192, 2048], P('dp', 'tensor')
- o_grad: float32 [8192, 8192], P('tensor', 'dp')
All inputs are finite; a program needn't handle non-finite values.
Results may differ from a plain program's by a relative error of at most 0.02.
Values may be sent and summed in bfloat16 or wider, within the bound.
No kernel may reach another device: no remote copies, remote signals or barrier semaphores. Data moves between devices by JAX's collectives and lax.ppermute only.
A program may use at most 192 MiB of HBM per device.

v0:
```python
import jax
import jax.numpy as jnp
from jax import lax
from jax.sharding import PartitionSpec as P

epsilon = 1e-05
theta = 500000.0


def swapped(array, axis, stride):
    return lax.ppermute(array, axis, [(i, i ^ 1 << stride) for i in range(lax.axis_size(axis))])


def rotary(length, head_size):
    half_dim = head_size // 2
    position = jnp.arange(length, dtype=jnp.float32)
    freq = theta ** (-(jnp.arange(half_dim, dtype=jnp.float32) * 2.0 / head_size))
    angle = position[:, None] * freq[None, :]
    return (jnp.cos(angle), jnp.sin(angle))


def rotate(vectors, cosine_table, sine_table, direction):
    half_dim = vectors.shape[-1] // 2
    first = vectors[..., :half_dim]
    second = vectors[..., half_dim:]
    cos_part = cosine_table[:, None, :]
    sin_part = sine_table[:, None, :] * direction
    return jnp.concatenate(
        [first * cos_part - second * sin_part, second * cos_part + first * sin_part], axis=-1
    )


def contract_rows(left, right):
    return lax.dot_general(
        left, right, (((0,), (0,)), ((), ())), preferred_element_type=jnp.float32
    )


def on_device(tokens, gain, q_weight, kv_weight, o_weight, out_grad):
    whole_tokens = lax.all_gather(tokens[0], "tensor", axis=1, tiled=True)
    input_tokens = whole_tokens.astype(jnp.float32)
    length = input_tokens.shape[0]
    feature_count = input_tokens.shape[1]
    row_number_total = length // lax.axis_size("tensor")
    row_offset = lax.axis_index("tensor") * row_number_total
    head_size = kv_weight.shape[1]
    local_heads = q_weight.shape[1] // head_size
    is_even = lax.axis_index("tensor") % 2 == 0
    score_scale = head_size ** (-0.5)
    cosine_table, sine_table = rotary(length, head_size)
    causal = jnp.arange(length)[:, None] >= jnp.arange(length)[None, :]
    gain_float = gain.astype(jnp.float32)
    inverse_norm = lax.rsqrt(
        jnp.mean(input_tokens * input_tokens, axis=-1, keepdims=True) + epsilon
    )
    standardized_rows = input_tokens * inverse_norm
    normalized_rows = (standardized_rows * gain_float).astype(jnp.bfloat16)
    queries = jnp.dot(normalized_rows, q_weight, preferred_element_type=jnp.float32).reshape(
        length, local_heads, head_size
    )
    qrot = rotate(queries, cosine_table, sine_table, 1.0).astype(jnp.bfloat16)
    partner = swapped(kv_weight, "tensor", 0)
    key_weight = jnp.where(is_even, kv_weight, partner)
    value_weight = jnp.where(is_even, partner, kv_weight)
    key_proj = jnp.dot(normalized_rows, key_weight, preferred_element_type=jnp.float32)[:, None, :]
    key_rows = rotate(key_proj, cosine_table, sine_table, 1.0)[:, 0].astype(jnp.bfloat16)
    value_rows = jnp.dot(normalized_rows, value_weight, preferred_element_type=jnp.float32).astype(
        jnp.bfloat16
    )
    scores = (
        jnp.einsum("qhd,kd->hqk", qrot, key_rows, preferred_element_type=jnp.float32) * score_scale
    )
    scores = jnp.where(causal[None], scores, -1e30)
    top_score = jnp.max(scores, axis=-1, keepdims=True)
    expo = jnp.exp(scores - top_score)
    probs = expo / jnp.sum(expo, axis=-1, keepdims=True)
    pbf = probs.astype(jnp.bfloat16)
    attn = jnp.einsum("hqk,kd->qhd", pbf, value_rows, preferred_element_type=jnp.float32).astype(
        jnp.bfloat16
    )
    attn = attn.reshape(length, local_heads * head_size)
    mixed = lax.psum_scatter(
        jnp.dot(attn, o_weight, preferred_element_type=jnp.float32).astype(jnp.bfloat16),
        "tensor",
        scatter_dimension=0,
        tiled=True,
    ).astype(jnp.float32)
    own_inputs = lax.dynamic_slice_in_dim(input_tokens, row_offset, row_number_total, 0)
    result = (own_inputs + mixed).astype(jnp.bfloat16)
    cotangent = lax.all_gather(out_grad[0], "tensor", axis=1, tiled=True)
    o_term = contract_rows(attn, cotangent)
    dattn = jnp.dot(cotangent, o_weight.T, preferred_element_type=jnp.float32).astype(jnp.bfloat16)
    dattn = dattn.reshape(length, local_heads, head_size)
    dprobs = jnp.einsum("qhd,kd->hqk", dattn, value_rows, preferred_element_type=jnp.float32)
    delta = jnp.sum(dprobs * probs, axis=-1, keepdims=True)
    dscores = (probs * (dprobs - delta) * score_scale).astype(jnp.bfloat16)
    dqrot = jnp.einsum("hqk,kd->qhd", dscores, key_rows, preferred_element_type=jnp.float32)
    dkey_part = jnp.einsum("hqk,qhd->kd", dscores, qrot, preferred_element_type=jnp.float32)
    dvalue_part = jnp.einsum("hqk,qhd->kd", pbf, dattn, preferred_element_type=jnp.float32)
    outgoing = jnp.where(is_even, dvalue_part, dkey_part)
    incoming = swapped(outgoing.astype(jnp.bfloat16), "tensor", 0).astype(outgoing.dtype)
    own_total = jnp.where(is_even, dkey_part, dvalue_part) + incoming
    unrotated = rotate(own_total[:, None, :], cosine_table, sine_table, -1.0)[:, 0]
    own_grad = jnp.where(is_even, unrotated, own_total).astype(jnp.bfloat16)
    dq_rows = (
        rotate(dqrot, cosine_table, sine_table, -1.0)
        .astype(jnp.bfloat16)
        .reshape(length, local_heads * head_size)
    )
    q_part = jnp.dot(dq_rows, q_weight.T, preferred_element_type=jnp.float32)
    kv_part = jnp.dot(own_grad, kv_weight.T, preferred_element_type=jnp.float32)
    normalized_gradient = lax.psum_scatter(
        (q_part + kv_part).astype(jnp.bfloat16), "tensor", scatter_dimension=0, tiled=True
    ).astype(jnp.float32)
    local_standardized = lax.dynamic_slice_in_dim(
        standardized_rows, row_offset, row_number_total, 0
    )
    own_inverse = lax.dynamic_slice_in_dim(inverse_norm, row_offset, row_number_total, 0)
    own_cot = lax.dynamic_slice_in_dim(cotangent, row_offset, row_number_total, 0)
    scaled_gradient = normalized_gradient * gain_float
    input_gradient = own_inverse * (
        scaled_gradient
        - local_standardized
        * jnp.mean(scaled_gradient * local_standardized, axis=-1, keepdims=True)
    )
    input_grad = (own_cot.astype(jnp.float32) + input_gradient).astype(jnp.bfloat16)
    gain_partial = jnp.sum(normalized_gradient * local_standardized, axis=0)
    gain_whole = lax.psum(gain_partial, ("dp", "tensor"))
    block_size = feature_count // lax.axis_size("dp")
    gain_grad = lax.dynamic_slice_in_dim(
        gain_whole, lax.axis_index("dp") * block_size, block_size, 0
    )
    q_term = contract_rows(normalized_rows, dq_rows).astype(jnp.bfloat16).astype(jnp.float32)
    kv_term = contract_rows(normalized_rows, own_grad).astype(jnp.bfloat16).astype(jnp.float32)
    q_grad, kv_grad = (
        lax.psum_scatter(q_term.astype(jnp.bfloat16), "dp", scatter_dimension=0, tiled=True).astype(
            jnp.float32
        ),
        lax.psum_scatter(
            kv_term.astype(jnp.bfloat16), "dp", scatter_dimension=0, tiled=True
        ).astype(jnp.float32),
    )
    o_grad = lax.psum_scatter(
        o_term.astype(jnp.bfloat16), "dp", scatter_dimension=1, tiled=True
    ).astype(jnp.float32)
    return (result[None], input_grad[None], gain_grad, q_grad, kv_grad, o_grad)


def solution(mesh):
    in_specs = (
        P("dp", None, "tensor"),
        P(),
        P(None, "tensor"),
        P(None, "tensor"),
        P("tensor", None),
        P("dp", None, "tensor"),
    )
    out_specs = (
        P("dp", "tensor", None),
        P("dp", "tensor", None),
        P("dp"),
        P("dp", "tensor"),
        P("dp", "tensor"),
        P("tensor", "dp"),
    )
    return jax.shard_map(
        on_device, mesh=mesh, in_specs=in_specs, out_specs=out_specs, check_vma=False
    )
```

profile of v0, /device:TPU:6, one launch (start us, length us, event | category | flops | bytes accessed | tf_op | source)
XLA Modules:
  0.0 728.6 jit_solution(1122185537018087064)
XLA Ops:
  7.2 0.7 all-gather.5.cloned.1.call-update
  7.9 0.7 all-gather.7.cloned.1.call-update
  8.8 0.7 convert_element_type.90
  9.5 0.7 iota_compare_fusion
  10.2 1.2 broadcast_multiply_fusion
  11.4 56.4 %all-gather.5.cloned.1.call-done = bf16[1,256,8192]{2,1,0:T(8,128)(2,1)} async-done(((bf16[1,256,512]{2,1,0:T(8,128)(2,1)}), bf16[1,256,8192]{2,1,0:T(8,128)(2,1)}) %all-gather.5.cloned.1.call-update) | async-done | bytes 4194320 | tf_op jit(solution)/shard_map/all_gather | solution.py:40
  67.8 3.1 fusion.3
  70.9 7.2 fusion.71
  78.0 0.2 reshape.165
  78.3 4.1 fusion.24
  82.4 1.0 subtract_convert_fusion.2
  83.4 1.1 fusion.72
  84.5 40.0 %all-gather.7.cloned.1.call-done = bf16[1,256,8192]{2,1,0:T(8,128)(2,1)} async-done(((bf16[1,256,512]{2,1,0:T(8,128)(2,1)}), bf16[1,256,8192]{2,1,0:T(8,128)(2,1)}) %all-gather.7.cloned.1.call-update) | async-done | bytes 4194320 | tf_op jit(solution)/shard_map/all_gather | solution.py:90
  124.5 7.7 %fusion.21 = bf16[256,512]{1,0:T(8,128)(2,1)} fusion(bf16[512,8192]{1,0:T(8,128)(2,1)} %param.10, bf16[1,256,8192]{2,1,0:T(8,128)(2,1)} %all-gather.7.cloned.1.call-done), kind=kOutput, calls=%fused_computation.33 | convolution fusion | flops 2147614720 | bytes 12845056 | tf_op jit(solution)/shard_map/dot_general | solution.py:92
  132.2 1.1 copy.49
  133.4 4.4 fusion.30
  137.8 1.3 convolution_bitcast_fusion
  139.1 0.9 subtract_convert_fusion.1
  140.0 2.6 fusion.73
  142.6 3.0 convolution_bitcast_fusion.3
  145.6 2.1 select_convert_fusion
  147.8 1.2 collective-permute-done.1
  149.1 0.3 multiply_subtract_fusion
  149.5 5.1 convolution_convert_fusion.3
  154.7 1.7 convolution_convert_fusion.4
  156.4 7.8 %convolution_convert_fusion.2 = bf16[256,8192]{1,0:T(8,128)(2,1)} fusion(bf16[256,512]{0,1:T(8,128)(2,1)S(1)} %bitcast.118, bf16[512,8192]{1,0:T(8,128)(2,1)} %param.10), kind=kOutput, calls=%fused_computation.5 | convolution fusion | flops 2149580800 | bytes 12845056 | tf_op jit(solution)/shard_map/dot_general | solution.py:83
  164.2 2.7 convolution_bitcast_fusion.1
  167.0 0.3 subtract_convert_fusion
  167.5 5.8 fusion.74
  173.4 3.2 fusion.2
  176.6 0.3 reduce-scatter.10.cloned.1.call-start
  176.9 7.9 %convolution_convert_fusion.1 = bf16[8192,512]{1,0:T(8,128)(2,1)} fusion(bf16[256,512]{0,1:T(8,128)(2,1)S(1)} %bitcast.117, f32[8192]{0:T(1024)S(1)} %copy-done.6, f32[256]{0:T(256)S(1)} %add_rsqrt_fusion, bf16[1,256,8192]{2,1,0:T(8,128)(2,1)} %all-gather.5.cloned.1.call-done), kind=kOutput, calls=%fused_computation.3 | convolution fusion | flops 2160066560 | bytes 12878848 | tf_op jit(solution)/shard_map/dot_general | solution.py:34
  184.9 7.8 %convolution_convert_fusion = bf16[512,8192]{1,0:T(8,128)(2,1)} fusion(bf16[256,512]{0,1:T(8,128)(2,1)S(1)} %bitcast.119, bf16[1,256,8192]{2,1,0:T(8,128)(2,1)} %all-gather.7.cloned.1.call-done), kind=kOutput, calls=%fused_computation.2 | convolution fusion | flops 2151677952 | bytes 12845056 | tf_op jit(solution)/shard_map/dot_general | solution.py:34
  192.8 6.6 convert_element_type.116
  199.4 4.3 bitcast_multiply_fusion.1
  203.7 1.5 reduce-scatter.12.cloned.1.call-done
  205.2 1.8 convert_element_type.113
  207.0 82.1 %reduce-scatter.6.cloned.1.call-done = bf16[16,8192]{1,0:T(8,128)(2,1)} async-done(((bf16[256,8192]{1,0:T(8,128)(2,1)}), bf16[16,8192]{1,0:T(8,128)(2,1)}) %reduce-scatter.6.cloned.1.call-update) | async-done | bytes 262160 | tf_op jit(solution)/shard_map/reduce_scatter | solution.py:82
  289.0 1.9 fusion.48
  290.9 81.8 %reduce-scatter.8.cloned.1.call-done = bf16[16,8192]{1,0:T(8,128)(2,1)} async-done(((bf16[256,8192]{1,0:T(8,128)(2,1)}), bf16[16,8192]{1,0:T(8,128)(2,1)}) %reduce-scatter.8.cloned.1.call-update) | async-done | bytes 262160 | tf_op jit(solution)/shard_map/reduce_scatter | solution.py:112
  372.8 1.4 fusion.44
  374.1 67.3 %psum.7 = f32[8192]{0:T(1024)S(1)} all-reduce(f32[8192]{0:T(1024)S(1)} %get-tuple-element.6), channel_id=1, replica_groups=mesh['dp'=8,'tensor'=16] {'dp','tensor'}, use_global_device_ids=true, to_apply=%region_8.9 | all-reduce | flops 8192 | bytes 65536 | tf_op jit(solution)/shard_map/psum | solution.py:128
  441.4 0.6 dynamic_slice.16
  442.0 2.1 fusion.49
  444.1 102.2 %reduce-scatter.10.cloned.1.call-done = bf16[1024,512]{1,0:T(8,128)(2,1)} async-done(((bf16[8192,512]{1,0:T(8,128)(2,1)}), bf16[1024,512]{1,0:T(8,128)(2,1)}) %reduce-scatter.10.cloned.1.call-update) | async-done | bytes 1048592 | tf_op jit(solution)/shard_map/reduce_scatter | solution.py:136
  546.3 2.8 convert_element_type.111
  549.2 169.8 %reduce-scatter.14.cloned.1.call-done = bf16[512,1024]{1,0:T(8,128)(2,1)} async-done(((bf16[512,8192]{1,0:T(8,128)(2,1)}), bf16[512,1024]{1,0:T(8,128)(2,1)}) %reduce-scatter.14.cloned.1.call-update) | async-done | bytes 1048592 | tf_op jit(solution)/shard_map/reduce_scatter | solution.py:143
  719.0 2.8 convert_element_type.115
  (48 shorter events, 1.0 us)
Async XLA Ops:
  7.2 60.6 %all-gather.5.cloned.1.call-start = ((), (), s32[]{:S(2)}) async-start(), calls=%async_computation.10 | async-start | bytes 4456448 | tf_op jit(solution)/shard_map/all_gather | solution.py:40
  7.9 116.6 %all-gather.7.cloned.1.call-start = ((), (), s32[]{:S(2)}) async-start(), calls=%async_computation.11 | async-start | bytes 4456448 | tf_op jit(solution)/shard_map/all_gather | solution.py:90
  8.7 196.5 %reduce-scatter.12.cloned.1.call-start = ((), (), s32[]{:S(2)}) async-start(), calls=%async_computation.8 | async-start | bytes 2359296 | tf_op jit(solution)/shard_map/reduce_scatter | solution.py:139
  8.7 69.5 %collective-permute-start = (bf16[8192,128]{1,0:T(8,128)(2,1)}, bf16[8192,128]{1,0:T(8,128)(2,1)}, u32[]{:S(2)}, u32[]{:S(2)}) collective-permute-start(bf16[8192,128]{1,0:T(8,128)(2,1)} %param.9), channel_id=1, source_target_pairs={{0,1},{1,0},{2,3},{3,2},{4,5},{5,4},{6,7},{7,6},{8,9},{9,8},{10,11... | collective-permute-start | bytes 6291464 | tf_op jit(solution)/shard_map/ppermute | solution.py:11
  9.5 68.7 %copy-start.5 = (f32[8192]{0:T(1024)}, f32[8192]{0:T(1024)S(1)}, u32[]{:S(2)}) copy-start(f32[8192]{0:T(1024)S(1)} %convert_element_type.90) | copy-start | bytes 98308
  70.9 7.4 %copy-start.1 = (bf16[8192,128]{1,0:T(8,128)(2,1)S(1)}, bf16[8192,128]{1,0:T(8,128)(2,1)}, u32[]{:S(2)}) copy-start(bf16[8192,128]{1,0:T(8,128)(2,1)} %param.9) | copy-start | bytes 6291460
  132.2 6.8 copy-start.2
  133.4 5.7 copy-start.4
  137.8 2.2 copy-start.9
  147.7 7.0 copy-start.7
  147.7 7.0 copy-start.8
  147.7 7.0 copy-start.10
  147.7 7.0 copy-start.11
  147.7 7.0 copy-start.12
  147.7 1.3 collective-permute-start.1
  154.6 134.4 %reduce-scatter.6.cloned.1.call-start = ((), (), s32[]{:S(2)}) async-start(), calls=%async_computation.5 | async-start | bytes 4456448 | tf_op jit(solution)/shard_map/reduce_scatter | solution.py:82
  156.4 10.6 %copy-start.3 = (f32[256,64]{1,0:T(8,128)S(1)}, f32[256,64]{1,0:T(8,128)}, u32[]{:S(2)}) copy-start(f32[256,64]{1,0:T(8,128)} %get-tuple-element.18) | copy-start | bytes 196612
  164.2 208.6 %reduce-scatter.8.cloned.1.call-start = ((), (), s32[]{:S(2)}) async-start(), calls=%async_computation.6 | async-start | bytes 4456448 | tf_op jit(solution)/shard_map/reduce_scatter | solution.py:112
  173.4 3.5 copy-start.6
  176.6 369.7 %reduce-scatter.10.cloned.1.call-start = ((), (), s32[]{:S(2)}) async-start(), calls=%async_computation.7 | async-start | bytes 9437184 | tf_op jit(solution)/shard_map/reduce_scatter | solution.py:136
  184.9 534.1 %reduce-scatter.14.cloned.1.call-start = ((), (), s32[]{:S(2)}) async-start(), calls=%async_computation.9 | async-start | bytes 9437184 | tf_op jit(solution)/shard_map/reduce_scatter | solution.py:143
  192.8 6.7 copy-start
Sparse Core Ops, SparseCore 0:
  10.3 57.3 all-gather.4
  70.1 54.3 all-gather.6
  154.7 50.4 reduce-scatter.11
  209.1 79.9 reduce-scatter.5
  293.4 79.2 reduce-scatter.7
  375.0 171.2 reduce-scatter.9
  548.7 170.2 reduce-scatter.13
where the time goes:
time: 730 us; the launch traced here: 729 us
  waiting for transfers between devices  537 us (74%)
  matrix products  74.4 us (10%)
  blocking collectives  67.3 us (9%)
  other arithmetic  32 us (4%)
  between operations  14.5 us (2%)
    reduce_scatter x1, waiting for transfers between devices, on_device(): lax.psum_scatter(o_term.astype(jnp.bfloat16), 'dp', scatter_dimension=1,...  170 us
    reduce_scatter x1, waiting for transfers between devices, on_device(): lax.psum_scatter(q_term.astype(jnp.bfloat16), 'dp', scatter_dimension=0,...  102 us
    reduce_scatter x1, waiting for transfers between devices, on_device(): lax.psum_scatter(jnp.dot(attn, o_weight, preferred_element_type=jnp.float...  82.1 us
    reduce_scatter x1, waiting for transfers between devices, on_device(): lax.psum_scatter((q_part + kv_part).astype(jnp.bfloat16), 'tensor', scatt...  81.8 us
    psum x1, blocking collectives, on_device(): gain_whole = lax.psum(gain_partial, ('dp', 'tensor'))  67.3 us
    all_gather x1, waiting for transfers between devices, on_device(): whole_tokens = lax.all_gather(tokens[0], 'tensor', axis=1, tiled=True)  56.4 us
    all_gather x1, waiting for transfers between devices, on_device(): cotangent = lax.all_gather(out_grad[0], 'tensor', axis=1, tiled=True)  40 us
    dot_general x3, matrix products, contract_rows(): lax.dot_general(left, right, (((0,), (0,)), ((), ())), preferred_element_...  20.8 us
  transfers between devices with their start and end apart: 9, of which 8 were waited for; matrix products, arithmetic and copies ran while one was open for 11% of the time, Pallas kernels for 0%

commit v1 on v0

v1 whole, which is shorter than its diff:
```python
import jax
import jax.numpy as jnp
import numpy as np
from jax import lax
from jax.experimental import pallas as pl
from jax.experimental.pallas import tpu as pltpu
from jax.sharding import PartitionSpec as P

epsilon = 1e-05
theta = 500000.0
f32 = jnp.float32
bf16 = jnp.bfloat16
VMEM = 20 * 1024 * 1024
ANY = pl.BlockSpec(memory_space=pl.ANY)
T, CHIP, CORE, Y, X, Z, XL = range(7)


def partner(array, axis, bits):
    return lax.ppermute(array, axis, [(i, i ^ bits) for i in range(lax.axis_size(axis))])


class Order:
    def __init__(self, at):
        self.at, self.last = at, []

    def wait(self, *arrays):
        self.last = self.last + list(arrays)


def call(kernel, name, order, operands, outputs, grid=(1,), scratch=()):
    arrays = [array for array, _ in operands]
    after = [a for a in order.last if not any(a is b for b in arrays)]
    count, extra = len(arrays), len(after)

    def body(at_ref, *refs):
        kernel(at_ref, *refs[:count], *refs[count + extra :])

    results = pl.pallas_call(
        body,
        grid_spec=pltpu.PrefetchScalarGridSpec(
            num_scalar_prefetch=1,
            grid=grid,
            in_specs=[spec for _, spec in operands] + [ANY] * extra,
            out_specs=[spec for _, spec in outputs],
            scratch_shapes=list(scratch),
        ),
        out_shape=[shape for shape, _ in outputs],
        compiler_params=pltpu.CompilerParams(vmem_limit_bytes=VMEM),
        cost_estimate=pl.CostEstimate(flops=1, bytes_accessed=1, transcendentals=0),
        name=name,
    )(order.at, *arrays, *after)
    order.last = [results[0]]
    return results


def whole(array):
    rank = len(array.shape)
    return (array, pl.BlockSpec(tuple(array.shape), lambda *_: (0,) * rank))


def shape(dims, dtype=bf16):
    return jax.ShapeDtypeStruct(tuple(dims), dtype)


def nt(left, right):
    return lax.dot_general(left, right, (((1,), (1,)), ((), ())), preferred_element_type=f32)


def tn(left, right):
    return lax.dot_general(left, right, (((0,), (0,)), ((), ())), preferred_element_type=f32)


def nn(left, right):
    return jnp.dot(left, right, preferred_element_type=f32)


def move(name, order, sources, out_shapes, plan):
    count, outs_count = len(sources), len(out_shapes)

    def kernel(at_ref, *refs):
        ins, outs = refs[:count], refs[count : count + outs_count]
        held, sems, out_sems = refs[count + outs_count : -2], refs[-2], refs[-1]
        copies = [
            pltpu.make_async_copy(source, target, sems.at[number])
            for number, (source, target) in enumerate(plan(at_ref, ins, held))
        ]
        for copy in copies:
            copy.start()
        for copy in copies:
            copy.wait()
        copies = [
            pltpu.make_async_copy(source, target, out_sems.at[number])
            for number, (source, target) in enumerate(zip(held, outs))
        ]
        for copy in copies:
            copy.start()
        for copy in copies:
            copy.wait()

    return call(
        kernel,
        name,
        order,
        [(source, ANY) for source in sources],
        [(s, ANY) for s in out_shapes],
        scratch=[pltpu.VMEM(s.shape, s.dtype) for s in out_shapes]
        + [pltpu.SemaphoreType.DMA((16,))] * 2,
    )


def stack(name, order, *groups):
    groups = [[p if p.ndim == 3 else p[None] for p in group] for group in groups]
    sources = [p for group in groups for p in group]

    def plan(at_ref, ins, outs):
        pairs, number = [], 0
        for group, out in zip(groups, outs):
            row = 0
            for p in group:
                pairs.append((ins[number], out.at[pl.ds(row, p.shape[0])]))
                row += p.shape[0]
                number += 1
        return pairs

    outs = [shape((sum(p.shape[0] for p in g),) + g[0].shape[1:]) for g in groups]
    return move(name, order, sources, outs, plan)


def norm(order, gain_row, own, other):
    chips, length, width = own.shape
    tile = 64
    full = 2 * chips * width

    def kernel(at_ref, gain_ref, own_ref, other_ref, normed_ref, inverse_ref, rows_ref):
        chip, core = at_ref[CHIP], at_ref[CORE]

        def columns(pair, half):
            return pl.ds(pl.multiple_of((2 * pair + half) * width, width), width)

        @pl.loop(0, tile // 16)
        def _(step):
            here = pl.ds(pl.multiple_of(step * 16, 16), 16)
            squares = jnp.zeros((16, width), f32)
            for j in range(chips):
                for ref in (own_ref, other_ref):
                    value = ref[j, here, :].astype(f32)
                    squares += value * value
            mean = jnp.sum(squares, axis=-1, keepdims=True) / full
            inverse = lax.rsqrt(mean + epsilon)
            inverse_ref[here, :] = inverse
            for j in range(chips):
                for ref, half in ((own_ref, core), (other_ref, 1 - core)):
                    place = columns(chip ^ j, half)
                    value = ref[j, here, :].astype(f32)
                    normed_ref[here, place] = (value * inverse * gain_ref[:, place]).astype(bf16)

            @pl.when(pl.program_id(0) * (tile // 16) + step == at_ref[T])
            def _():
                for j in range(chips):
                    for ref, half in ((own_ref, core), (other_ref, 1 - core)):
                        rows_ref[:, columns(chip ^ j, half)] = ref[j, here, :]

    block = pl.BlockSpec((chips, tile, width), lambda i, at: (0, i, 0))
    return call(
        kernel,
        "norm",
        order,
        [whole(gain_row), (own, block), (other, block)],
        [
            (shape((length, full)), pl.BlockSpec((tile, full), lambda i, at: (i, 0))),
            (shape((length, 1), f32), pl.BlockSpec((tile, 1), lambda i, at: (i, 0))),
            (shape((16, full)), pl.BlockSpec((16, full), lambda i, at: (0, 0))),
        ],
        grid=(length // tile,),
    )


def pick_tokens(order, own):
    chips, length, width = own.shape

    def kernel(at_ref, own_ref, *out):
        for k in range(4):
            for x in range(2):
                block = own_ref[at_ref[CHIP] ^ (2 * (at_ref[Z] ^ k) + x)]
                out[k][x] = block.T

    return call(
        kernel, "pick_tokens", order, [whole(own)], [whole_out((2, width, length))] * 4
    )


def turned(value, cos_ref, sin_ref, direction):
    swapped = pltpu.roll(value, value.shape[-1] // 2, 1)
    return value * cos_ref[...] + swapped * (sin_ref[...] * direction)


def project(order, normed, q_weight, kv_weight, tables):
    length, full = normed.shape
    q_width, head = q_weight.shape[1], kv_weight.shape[1]
    tile = 1024

    def kernel(at_ref, x_ref, q_ref, kv_ref, cos_ref, sin_ref, rot_ref, own_ref, qacc, kvacc):
        step = pl.program_id(0)

        @pl.when(step == 0)
        def _():
            qacc[...] = jnp.zeros_like(qacc)
            kvacc[...] = jnp.zeros_like(kvacc)

        qacc[...] += nn(x_ref[...], q_ref[...])
        kvacc[...] += nn(x_ref[...], kv_ref[...])

        @pl.when(step == pl.num_programs(0) - 1)
        def _():
            for h in range(q_width // head):
                place = slice(h * head, (h + 1) * head)
                rot_ref[:, place] = turned(qacc[:, place], cos_ref, sin_ref, 1.0).astype(bf16)
            plain = kvacc[...]
            rotated = turned(plain, cos_ref, sin_ref, 1.0)
            own_ref[...] = jnp.where(at_ref[CORE] == 0, rotated, plain).astype(bf16)

    return call(
        kernel,
        "project",
        order,
        [
            (normed, pl.BlockSpec((length, tile), lambda i, at: (0, i))),
            (q_weight, pl.BlockSpec((tile, q_width), lambda i, at: (i, 0))),
            (kv_weight, pl.BlockSpec((tile, head), lambda i, at: (i, 0))),
            whole(tables[0]),
            whole(tables[1]),
        ],
        [whole_out((length, q_width)), whole_out((length, head))],
        grid=(full // tile,),
        scratch=[pltpu.VMEM((length, q_width), f32), pltpu.VMEM((length, head), f32)],
    )


def whole_out(dims, dtype=bf16):
    return whole(shape(dims, dtype))


def attend(order, rot, own, other):
    length, q_width = rot.shape
    head = own.shape[1]
    heads = q_width // head
    scale = head ** (-0.5)

    def kernel(at_ref, rot_ref, own_ref, other_ref, attn_ref, probs_ref, turned_ref):
        even = at_ref[CORE] == 0
        key = jnp.where(even, own_ref[...], other_ref[...])
        value = jnp.where(even, other_ref[...], own_ref[...])
        row = lax.broadcasted_iota(jnp.int32, (length, length), 0)
        column = lax.broadcasted_iota(jnp.int32, (length, length), 1)
        for h in range(heads):
            place = slice(h * head, (h + 1) * head)
            scores = jnp.where(row >= column, nt(rot_ref[:, place], key) * scale, -1e30)
            expo = jnp.exp(scores - jnp.max(scores, axis=-1, keepdims=True))
            probs = expo / jnp.sum(expo, axis=-1, keepdims=True)
            probs_ref[h] = probs
            attn = nn(probs.astype(bf16), value)
            attn_ref[:, place] = attn.astype(bf16)
            turned_ref[place, :] = attn.T.astype(bf16)

    return call(
        kernel,
        "attend",
        order,
        [whole(rot), whole(own), whole(other)],
        [
            whole_out((length, q_width)),
            whole_out((heads, length, length), f32),
            whole_out((q_width, length)),
        ],
    )


def split_rows(at_ref, product, rows_ref, send_ref, keep_ref):
    rows_ref[...] = product.reshape(rows_ref.shape)
    send_ref[...] = rows_ref[:, 1 - at_ref[CORE]].astype(bf16)
    keep_ref[...] = rows_ref[:, at_ref[CORE]].astype(bf16)


def mix(order, attn, o_weight):
    length, q_width = attn.shape
    full = o_weight.shape[1]
    tile = 1024

    def kernel(at_ref, attn_ref, w_ref, send_ref, keep_ref, rows_ref):
        split_rows(at_ref, nn(attn_ref[...], w_ref[...]), rows_ref, send_ref, keep_ref)

    out = (shape((length // 32, 16, full)), pl.BlockSpec((length // 32, 16, tile), lambda i, at: (0, 0, i)))
    return call(
        kernel,
        "mix",
        order,
        [whole(attn), (o_weight, pl.BlockSpec((q_width, tile), lambda i, at: (0, i)))],
        [out, out],
        grid=(full // tile,),
        scratch=[pltpu.VMEM((length // 32, 2, 16, tile), f32)],
    )


def pair_sum(order, keep, arrived, groups, index):
    chips, _, full = keep.shape
    each = chips // groups
    tile = 2048

    def kernel(at_ref, keep_ref, arrived_ref, *out):
        for k in range(groups):
            here = pl.ds((at_ref[index] ^ k) * each, each) if groups > 1 else slice(None)
            out[k][...] = (keep_ref[here].astype(f32) + arrived_ref[here].astype(f32)).astype(bf16)

    block = pl.BlockSpec((chips, 16, tile), lambda i, at: (0, 0, i))
    out = (shape((each, 16, full)), pl.BlockSpec((each, 16, tile), lambda i, at: (0, 0, i)))
    return call(
        kernel,
        "pair_sum",
        order,
        [(keep, block), (arrived, block)],
        [out] * groups,
        grid=(full // tile,),
    )


def ring_sum(order, parts):
    _, _, full = parts[0].shape
    tile = 2048

    def kernel(at_ref, *refs):
        parts, keep_ref, send_ref = refs[:4], refs[4], refs[5]
        for target, x in ((keep_ref, at_ref[X]), (send_ref, 1 - at_ref[X])):
            total = parts[0][x].astype(f32)
            for part in parts[1:]:
                total += part[x].astype(f32)
            target[...] = total.astype(target.dtype)

    block = pl.BlockSpec((2, 16, tile), lambda i, at: (0, 0, i))
    out = pl.BlockSpec((16, tile), lambda i, at: (0, i))
    return call(
        kernel,
        "ring_sum",
        order,
        [(part, block) for part in parts],
        [(shape((16, full), f32), out), (shape((16, full)), out)],
        grid=(full // tile,),
    )


def out_gradient(order, own, other, o_weight):
    chips, length, width = own.shape
    q_width, full = o_weight.shape

    def kernel(at_ref, own_ref, other_ref, w_ref, dattn_ref, rows_ref, acc):
        step = pl.program_id(0)
        core = at_ref[CORE]

        @pl.when(step == 0)
        def _():
            acc[...] = jnp.zeros_like(acc)

        mine = pl.ds(pl.multiple_of(at_ref[T] * 16, 16), 16)
        for ref, half in ((own_ref, core), (other_ref, 1 - core)):
            place = pl.ds(pl.multiple_of(half * width, width), width)
            acc[...] += nt(ref[0], w_ref[:, place])
            rows_ref[:, place] = ref[0, mine, :]

        @pl.when(step == pl.num_programs(0) - 1)
        def _():
            dattn_ref[...] = acc[...].astype(bf16)

    block = pl.BlockSpec((1, length, width), lambda i, at: (i, 0, 0))
    return call(
        kernel,
        "out_gradient",
        order,
        [
            (own, block),
            (other, block),
            (o_weight, pl.BlockSpec((q_width, 2 * width), lambda i, at: (0, at[CHIP] ^ i))),
        ],
        [
            whole_out((length, q_width)),
            (shape((16, full)), pl.BlockSpec((16, 2 * width), lambda i, at: (0, at[CHIP] ^ i))),
        ],
        grid=(chips,),
        scratch=[pltpu.VMEM((length, q_width), f32)],
    )


def attend_gradient(order, dattn, probs, rot, own, other, tables):
    length, q_width = rot.shape
    head = own.shape[1]
    scale = head ** (-0.5)

    def kernel(
        at_ref, dattn_ref, probs_ref, rot_ref, own_ref, other_ref, cos_ref, sin_ref,
        dq_ref, keep_ref, send_ref,
    ):
        even = at_ref[CORE] == 0
        key = jnp.where(even, own_ref[...], other_ref[...])
        value = jnp.where(even, other_ref[...], own_ref[...])
        dkey = jnp.zeros((length, head), f32)
        dvalue = jnp.zeros((length, head), f32)
        for h in range(q_width // head):
            place = slice(h * head, (h + 1) * head)
            probs = probs_ref[h]
            dattn = dattn_ref[:, place]
            dprobs = nt(dattn, value)
            delta = jnp.sum(dprobs * probs, axis=-1, keepdims=True)
            dscores = (probs * (dprobs - delta) * scale).astype(bf16)
            dq_ref[:, place] = turned(nn(dscores, key), cos_ref, sin_ref, -1.0).astype(bf16)
            dkey += tn(dscores, rot_ref[:, place])
            dvalue += tn(probs.astype(bf16), dattn)
        keep_ref[...] = jnp.where(even, dkey, dvalue)
        send_ref[...] = jnp.where(even, dvalue, dkey).astype(bf16)

    return call(
        kernel,
        "attend_gradient",
        order,
        [whole(a) for a in (dattn, probs, rot, own, other, *tables)],
        [whole_out((length, q_width)), whole_out((length, head), f32), whole_out((length, head))],
    )


def join_gradient(order, dq, keep, arrived, inverse, tables):
    length, q_width = dq.shape
    head = keep.shape[1]

    def kernel(
        at_ref, dq_ref, keep_ref, arrived_ref, inverse_ref, cos_ref, sin_ref, out_ref, scaled_ref
    ):
        inverse = inverse_ref[...]
        dq = dq_ref[...]
        out_ref[:, :q_width] = dq
        scaled_ref[:, :q_width] = (dq.astype(f32) * inverse).astype(bf16)
        plain = keep_ref[...] + arrived_ref[...].astype(f32)
        back = turned(plain, cos_ref, sin_ref, -1.0)
        own = jnp.where(at_ref[CORE] == 0, back, plain).astype(bf16)
        out_ref[:, q_width:] = own
        scaled_ref[:, q_width:] = (own.astype(f32) * inverse).astype(bf16)

    return call(
        kernel,
        "join_gradient",
        order,
        [whole(a) for a in (dq, keep, arrived, inverse, *tables)],
        [whole_out((length, q_width + head))] * 2,
    )


def norm_gradient(order, dqkv, q_weight, kv_weight, normed, gain_row):
    length, full = normed.shape
    q_width, head = q_weight.shape[1], kv_weight.shape[1]
    tile = 1024

    def kernel(
        at_ref, d_ref, q_ref, kv_ref, normed_ref, gain_ref, send_ref, keep_ref, part_ref, rows_ref
    ):
        product = nt(d_ref[:, :q_width], q_ref[...]) + nt(d_ref[:, q_width:], kv_ref[...])
        part = jnp.sum(product * normed_ref[...].astype(f32), axis=0, keepdims=True)
        part_ref[0] = part / gain_ref[...]
        split_rows(at_ref, product, rows_ref, send_ref, keep_ref)

    out = (shape((length // 32, 16, full)), pl.BlockSpec((length // 32, 16, tile), lambda i, at: (0, 0, i)))
    return call(
        kernel,
        "norm_gradient",
        order,
        [
            whole(dqkv),
            (q_weight, pl.BlockSpec((tile, q_width), lambda i, at: (i, 0))),
            (kv_weight, pl.BlockSpec((tile, head), lambda i, at: (i, 0))),
            (normed, pl.BlockSpec((length, tile), lambda i, at: (0, i))),
            (gain_row, pl.BlockSpec((1, tile), lambda i, at: (0, i))),
        ],
        [out, out, (shape((full // tile, 1, tile), f32), pl.BlockSpec((1, 1, tile), lambda i, at: (i, 0, 0)))],
        grid=(full // tile,),
        scratch=[pltpu.VMEM((length // 32, 2, 16, tile), f32)],
    )


def input_gradient(order, keep, arrived, tokens, inverse, cotangent, gain_row):
    rows, full = tokens.shape

    def kernel(
        at_ref, keep_ref, arrived_ref, tokens_ref, inverse_ref, cot_ref, gain_ref, out_ref,
        xhat_ref, scaled_ref,
    ):
        inverse = inverse_ref[pl.ds(pl.multiple_of(at_ref[T] * 16, 16), 16), :]
        tile = 1024
        dots = jnp.zeros((rows, tile), f32)
        for i in range(full // tile):
            place = slice(i * tile, (i + 1) * tile)
            total = keep_ref[:, place] + arrived_ref[:, place].astype(f32)
            xhat = tokens_ref[:, place].astype(f32) * inverse
            scaled = total * gain_ref[:, place]
            xhat_ref[:, place] = xhat
            scaled_ref[:, place] = scaled
            dots += scaled * xhat
        mean = jnp.sum(dots, axis=-1, keepdims=True) / full
        for i in range(full // tile):
            place = slice(i * tile, (i + 1) * tile)
            change = inverse * (scaled_ref[:, place] - xhat_ref[:, place] * mean)
            out_ref[:, place] = (cot_ref[:, place].astype(f32) + change).astype(bf16)

    return call(
        kernel,
        "input_gradient",
        order,
        [whole(a) for a in (keep, arrived, tokens, inverse, cotangent, gain_row)],
        [whole_out((rows, full))],
        scratch=[pltpu.VMEM((rows, full), f32)] * 2,
    )[0]


def out_terms(order, own, other, rows):
    _, length, width = own.shape
    total = rows[0].shape[0]

    def kernel(at_ref, own_ref, other_ref, *refs):
        rows, (send_ref, keep_ref, acc) = refs[:4], refs[4:]
        step = pl.program_id(0)

        def add(ref):
            acc[...] = nn(rows[0][...], ref[0, 0])
            for k in range(1, 4):
                acc[...] += nn(rows[k][...], ref[k, 0])

        pl.when(step % 2 == 0)(lambda: add(own_ref))
        pl.when(step % 2 == 1)(lambda: add(other_ref))

        @pl.when(step < 2)
        def _():
            send_ref[...] = acc[...].astype(bf16)

        @pl.when(step >= 2)
        def _():
            keep_ref[...] = acc[...]

    def x_of(i, at):
        return jnp.where(i < 2, 1 - at[XL], at[XL])

    def side(half, at):
        return jnp.where(half == 0, at[CORE], 1 - at[CORE])

    block = pl.BlockSpec((4, 1, length, width), lambda i, at: (0, x_of(i, at), 0, 0))
    dims = (4, 2, length, width)
    return call(
        kernel,
        "out_terms",
        order,
        [(own.reshape(dims), block), (other.reshape(dims), block)] + [whole(a) for a in rows],
        [
            (
                shape((total, 2 * width)),
                pl.BlockSpec((total, width), lambda i, at: (0, side(jnp.minimum(i, 1), at))),
            ),
            (
                shape((total, 2 * width), f32),
                pl.BlockSpec((total, width), lambda i, at: (0, side(jnp.maximum(i - 2, 0), at))),
            ),
        ],
        grid=(4,),
        scratch=[pltpu.VMEM((total, width), f32)],
    )


def q_gradient(order, own, other, rows, gain_column, q_width):
    _, width, length = own[0].shape
    total = rows[0].shape[2]

    def kernel(at_ref, *refs):
        blocks, row_refs, gain_ref, q_ref, kv_ref, acc = refs[:4], refs[4:8], *refs[8:]
        half, k = pl.program_id(0), pl.program_id(1)

        def add(pair):
            for number in range(4):

                @pl.when(k == number)
                def _():
                    term = nn(pair[0][0], row_refs[number][0]) + nn(pair[1][0], row_refs[number][1])
                    if number == 0:
                        acc[...] = term
                    else:
                        acc[...] += term

        pl.when(half == 0)(lambda: add(blocks[:2]))
        pl.when(half == 1)(lambda: add(blocks[2:]))

        @pl.when(k == 3)
        def _():
            product = acc[...] * gain_ref[...]
            q_ref[...] = product[:, :q_width]
            kv_ref[...] = product[:, q_width:]

    first = pl.BlockSpec((1, width, length), lambda h, k, at: (jnp.where(h == 0, k, 3), 0, 0))
    second = pl.BlockSpec((1, width, length), lambda h, k, at: (jnp.where(h == 0, 0, k), 0, 0))

    def side(h, at):
        return jnp.where(h == 0, at[CORE], 1 - at[CORE])

    return call(
        kernel,
        "q_gradient",
        order,
        [(a, first) for a in own]
        + [(a, second) for a in other]
        + [whole(a) for a in rows]
        + [(gain_column, pl.BlockSpec((width, 1), lambda h, k, at: (side(h, at), 0)))],
        [
            (
                shape((2 * width, size), f32),
                pl.BlockSpec((width, size), lambda h, k, at: (side(h, at), 0)),
            )
            for size in (q_width, total - q_width)
        ],
        grid=(2, 4),
        scratch=[pltpu.VMEM((width, total), f32)],
    )


def near(parts):
    return {k: partner(parts[k], "dp", 2 * k) for k in (1, 3)}


def far(parts):
    return {2: partner(parts[2], "dp", 4)}


def in_order(*found):
    merged = {}
    for part in found:
        merged.update(part)
    return [merged[k] for k in sorted(merged)]


def split_x(name, order, parts):
    def plan(at_ref, ins, outs):
        pairs = []
        for k, ref in enumerate(ins):
            pairs.append((ref.at[at_ref[XL]], outs[0].at[k]))
            pairs.append((ref.at[1 - at_ref[XL]], outs[1].at[k]))
        return pairs

    dims = (len(parts),) + parts[0].shape[1:]
    return move(name, order, parts, [shape(dims)] * 2, plan)


def rotary(length, head):
    freq = theta ** (-(np.arange(head // 2, dtype=np.float64) * 2.0 / head))
    angle = np.arange(length, dtype=np.float64)[:, None] * freq[None, :]
    cosine, sine = np.cos(angle), np.sin(angle)
    return (
        np.concatenate([cosine, cosine], 1).astype(np.float32),
        np.concatenate([-sine, sine], 1).astype(np.float32),
    )


def on_device(tokens, gain, q_weight, kv_weight, o_weight, out_grad):
    t_at = lax.axis_index("tensor")
    dp_at = lax.axis_index("dp")
    at = jnp.stack(
        [t_at, t_at // 2, t_at % 2, t_at // 4, t_at // 2 % 2, dp_at // 2, dp_at % 2]
    ).astype(jnp.int32)
    order = Order(at)
    length, width = tokens.shape[1:]
    q_width, head = q_weight.shape[1], kv_weight.shape[1]
    tables = [jnp.asarray(table) for table in rotary(length, head)]
    gain_float = gain.astype(f32)
    gain_row = gain_float[None, :]
    gain_column = lax.dynamic_slice_in_dim(gain_float, dp_at * 2 * width, 2 * width)[:, None]

    def y_near(parts):
        return {k: partner(parts[k], "tensor", 4 * k) for k in (1, 3)}

    def y_far(parts):
        return {2: partner(parts[2], "tensor", 8)}

    shard, cot = tokens[0], out_grad[0]
    shards = {0: shard, 1: partner(shard, "tensor", 2)}
    for j in (2, 6, 4):
        shards[j] = partner(shard, "tensor", 2 * j)
    for j in (2, 6, 4):
        shards[j ^ 1] = partner(shards[1], "tensor", 2 * j)
    cot_other = partner(cot, "tensor", 2)
    own, cot_pair = stack("stack_tokens", order, [shards[j] for j in range(8)], [cot, cot_other])
    other = partner(own, "tensor", 1)
    cot_near = y_near([cot_pair] * 4)

    blocks = pick_tokens(order, own)
    token_near = near(blocks)
    normed, inverse, own_tokens = norm(order, gain_row, own, other)
    order.wait(*cot_near.values())
    rot, kv_own = project(order, normed, q_weight, kv_weight, tables)
    cot_far = y_far([cot_pair] * 4)
    kv_other = partner(kv_own, "tensor", 1)
    order.wait(*token_near.values())
    attn, probs, attn_turned = attend(order, rot, kv_own, kv_other)
    token_far = far(blocks)
    send, keep = mix(order, attn, o_weight)
    arrived = partner(send, "tensor", 1)

    (cot_own,) = stack("stack_cot", order, in_order({0: cot_pair}, cot_near, cot_far))
    cot_other = partner(cot_own, "tensor", 1)

    def cot_plan(at_ref, ins, outs):
        return [
            (ins[0].at[at_ref[CHIP] ^ (2 * (at_ref[Z] ^ k) + x)], outs[k].at[x])
            for k in range(4)
            for x in range(2)
        ]

    cot_blocks = move(
        "pick_cot", order, [cot_own], [shape((2, length, width))] * 4, cot_plan
    )
    b_near = near(cot_blocks)
    a_keep, a_send = split_x(
        "split_tokens", order, in_order({0: blocks[0]}, token_near, token_far)
    )
    a_cross = partner(a_send, "dp", 1)
    out_parts = pair_sum(order, keep, arrived, 4, Y)
    out_near = y_near(out_parts)

    dattn, own_cot = out_gradient(order, cot_own, cot_other, o_weight)
    order.wait(*b_near.values())
    dq, dkv_keep, send = attend_gradient(order, dattn, probs, rot, kv_own, kv_other, tables)
    b_far = far(cot_blocks)
    arrived = partner(send, "tensor", 1)
    order.wait(*out_near.values())
    dqkv, scaled = join_gradient(order, dq, dkv_keep, arrived, inverse, tables)
    scaled_other = partner(scaled, "dp", 1)
    out_far = y_far(out_parts)
    attn_near = near([attn_turned] * 4)
    order.wait(a_cross)

    send, keep, gain_part = norm_gradient(order, dqkv, q_weight, kv_weight, normed, gain_row)
    arrived = partner(send, "tensor", 1)
    order.wait(*attn_near.values())
    (pair,) = stack("stack_dqkv", order, [scaled, scaled_other])
    dqkv_near = near([pair] * 4)
    out_keep, out_send = ring_sum(order, in_order({0: out_parts[0]}, out_near, out_far))
    out_arrived = partner(out_send, "tensor", 2)
    x_parts = pair_sum(order, keep, arrived, 4, Y)
    x_near = y_near(x_parts)

    gain_part = lax.all_to_all(gain_part, "dp", 0, 0, tiled=True)
    gain_part = jnp.broadcast_to(jnp.sum(gain_part, axis=0)[None], (16, 1, 2 * width))
    gain_grad = jnp.sum(lax.all_to_all(gain_part, "tensor", 0, 0, tiled=True), axis=0)
    result = (own_tokens.astype(f32) + (out_keep + out_arrived.astype(f32))).astype(bf16)

    attn_far = far([attn_turned] * 4)
    (b_own,) = stack("stack_b", order, in_order({0: cot_blocks[0]}, b_near, b_far))
    b_other = partner(b_own, "tensor", 1)
    a_other = [partner(a, "tensor", 1) for a in (a_keep, a_cross)]
    order.wait(*dqkv_near.values())
    send, keep = out_terms(
        order, b_own, b_other, in_order({0: attn_turned}, attn_near, attn_far)
    )
    dqkv_far = far([pair] * 4)
    o_arrived = partner(send, "dp", 1)
    x_far = y_far(x_parts)
    x_keep, x_send = ring_sum(order, in_order({0: x_parts[0]}, x_near, x_far))
    x_arrived = partner(x_send, "tensor", 2)
    o_grad = keep + o_arrived.astype(f32)

    q_grad, kv_grad = q_gradient(
        order,
        [a_keep, a_cross],
        a_other,
        in_order({0: pair}, dqkv_near, dqkv_far),
        gain_column,
        q_width,
    )
    x_grad = input_gradient(order, x_keep, x_arrived, own_tokens, inverse, own_cot, gain_row)
    return (result[None], x_grad[None], gain_grad.reshape(-1), q_grad, kv_grad, o_grad)


def solution(mesh):
    in_specs = (
        P("dp", None, "tensor"),
        P(),
        P(None, "tensor"),
        P(None, "tensor"),
        P("tensor", None),
        P("dp", None, "tensor"),
    )
    out_specs = (
        P("dp", "tensor", None),
        P("dp", "tensor", None),
        P("dp"),
        P("dp", "tensor"),
        P("dp", "tensor"),
        P("tensor", "dp"),
    )
    return jax.shard_map(
        on_device, mesh=mesh, in_specs=in_specs, out_specs=out_specs, check_vma=False
    )
```

time: 730 us -> 267 us (0.37)
  waiting for transfers between devices: 537 us -> 110 us
  matrix products: 74.4 us -> 0 us
  Pallas kernels: 0 us -> 63.7 us
  starting transfers between devices: 0.68 us -> 63.3 us
  blocking collectives: 67.3 us -> 10.4 us
  other arithmetic: 32 us -> 4.2 us
  between operations: 14.5 us -> 1.12 us
  local copies, waits for them, and re-layouts: 3.33 us -> 13.6 us
    reduce_scatter x5 -> x0, waiting for transfers between devices: 437 us -> none  [the longest x1 170 us: on_device(): lax.psum_scatter(o_term.astype(jnp.bfloat16), 'dp', scatter_dimension=1,...]
    ppermute x2 -> x43, waiting for transfers between devices: 1.24 us -> 106 us  [partner(): lax.ppermute(array, axis, [(i, i ^ bits) for i in range(lax.axis_size(axi...]
    all_gather x2 -> x0, waiting for transfers between devices: 96.4 us -> none  [the longest x1 56.4 us: on_device(): whole_tokens = lax.all_gather(tokens[0], 'tensor', axis=1, tiled=True)]
    dot_general x15 -> x0, matrix products: 71.8 us -> none  [the longest x3 20.8 us: contract_rows(): lax.dot_general(left, right, (((0,), (0,)), ((), ())), preferred_element_...]
    psum x1 -> x0, blocking collectives: 67.3 us -> none  [on_device(): gain_whole = lax.psum(gain_partial, ('dp', 'tensor'))]
    pallas_call x0 -> x22, Pallas kernels: none -> 63.7 us  [call(): pl.pallas_call(body, grid_spec=pltpu.PrefetchScalarGridSpec(num_scalar_pr...]
    ppermute x2 -> x43, starting transfers between devices: 0.17 us -> 58.2 us  [partner(): lax.ppermute(array, axis, [(i, i ^ bits) for i in range(lax.axis_size(axi...]
    convert_element_type x6 -> x1, other arithmetic: 14.7 us -> 0.01 us  [on_device(): gain_float = gain.astype(f32)]
  transfers between devices with their start and end apart: 9 -> 44, of which waited for: 8 -> 21; matrix products, arithmetic and copies ran while one was open for 11% -> 2% of each run, Pallas kernels for 0% -> 21%
where the time goes in v1:
time: 267 us; the launch traced here: 266 us
  waiting for transfers between devices  110 us (41%)
  Pallas kernels  63.7 us (24%)
  starting transfers between devices  63.3 us (24%)
  local copies, waits for them, and re-layouts  13.6 us (5%)
  blocking collectives  10.4 us (4%)
  other arithmetic  4.2 us (2%)
    ppermute x43, waiting for transfers between devices, partner(): lax.ppermute(array, axis, [(i, i ^ bits) for i in range(lax.axis_size(axi...  106 us
    pallas_call x22, Pallas kernels, call(): pl.pallas_call(body, grid_spec=pltpu.PrefetchScalarGridSpec(num_scalar_pr...  63.7 us
    ppermute x43, starting transfers between devices, partner(): lax.ppermute(array, axis, [(i, i ^ bits) for i in range(lax.axis_size(axi...  58.2 us
    unnamed x74, local copies, waits for them, and re-layouts  11.8 us
    all_to_all x1, blocking collectives, on_device(): gain_part = lax.all_to_all(gain_part, 'dp', 0, 0, tiled=True)  10.4 us
  transfers between devices with their start and end apart: 44, of which 21 were waited for; matrix products, arithmetic and copies ran while one was open for 2% of the time, Pallas kernels for 21%

profile of v1, /device:TPU:6, one launch (start us, length us, event | category | flops | bytes accessed | tf_op | source)
XLA Modules:
  0.0 266.3 jit_solution(11187788015025223927)
XLA Ops:
  3.7 2.9 %collective-permute-start.3 = (bf16[256,512]{1,0:T(8,128)(2,1)}, bf16[256,512]{1,0:T(8,128)(2,1)S(1)}, u32[]{:S(2)}, u32[]{:S(2)}) collective-permute-start(bf16[256,512]{1,0:T(8,128)(2,1)} %bitcast.36), channel_id=1, source_target_pairs={{0,8},{1,9},{2,10},{3,11},{4,12},{5,13},{6,14},{7,15},{8,0},{9,1},... | collective-permute-start | bytes 786440 | tf_op jit(solution)/shard_map/ppermute | solution.py:19
  6.8 2.1 collective-permute-start.7
  8.9 2.0 collective-permute-done
  11.0 2.2 collective-permute-start.2
  13.2 2.3 collective-permute-start.4
  15.5 4.2 %collective-permute-done.3 = bf16[256,512]{1,0:T(8,128)(2,1)S(1)} collective-permute-done((bf16[256,512]{1,0:T(8,128)(2,1)}, bf16[256,512]{1,0:T(8,128)(2,1)S(1)}, u32[]{:S(2)}, u32[]{:S(2)}) %collective-permute-start.3) | collective-permute-done | bytes 262176 | tf_op jit(solution)/shard_map/ppermute | solution.py:19
  21.0 1.9 collective-permute-done.2
  22.8 6.7 %collective-permute-done.4 = bf16[256,512]{1,0:T(8,128)(2,1)S(1)} collective-permute-done((bf16[256,512]{1,0:T(8,128)(2,1)S(1)}, bf16[256,512]{1,0:T(8,128)(2,1)S(1)}, u32[]{:S(2)}, u32[]{:S(2)}) %collective-permute-start.4) | collective-permute-done | bytes 262176 | tf_op jit(solution)/shard_map/ppermute | solution.py:19
  29.5 2.5 collective-permute-done.6
  36.9 2.0 collective-permute-start.12
  38.9 2.5 collective-permute-start.13
  41.4 3.7 %collective-permute-start.16 = (bf16[2,256,512]{2,1,0:T(8,128)(2,1)S(1)}, bf16[2,256,512]{2,1,0:T(8,128)(2,1)S(1)}, u32[]{:S(2)}, u32[]{:S(2)}) collective-permute-start(bf16[2,256,512]{2,1,0:T(8,128)(2,1)S(1)} %get-tuple-element.58.refs_0_), channel_id=1, source_target_pairs={{0,8},{1,9},{2,10},{3,11},{4,12},{5,13},{6,14},{7,15},{8,0},{9,1},... | collective-permute-start | bytes 1572872 | tf_op jit(solution)/shard_map/ppermute | solution.py:19
  45.1 3.7 %norm.1 = (bf16[256,8192]{1,0:T(8,128)(2,1)S(1)}, f32[256,1]{1,0:T(8,128)S(1)}, bf16[16,8192]{1,0:T(8,128)(2,1)S(1)}) custom-call(s32[7]{0:T(128)S(1)} %stack.31.at_ref, f32[1,8192]{1,0:T(1,128)S(1)} %bitcast.29, bf16[8,256,512]{2,1,0:T(8,128)(2,1)S(1)} %get-tuple-element.54.refs_0_.refs_1_, bf16[8,256,512]{2,1,0:T(8,128)(2,1)S(1)} %collective-permute-done.8.refs_2_, ...), custom_call_target="tpu_custom_call" | custom-call | flops 1 | bytes 1 | tf_op jit(solution)/shard_map/norm/pallas_call | solution.py:38
  50.1 12.0 %collective-permute-done.10.refs_6_.refs_3_ = bf16[2,256,512]{2,1,0:T(8,128)(2,1)S(1)} collective-permute-done((bf16[2,256,512]{2,1,0:T(8,128)(2,1)S(1)}, bf16[2,256,512]{2,1,0:T(8,128)(2,1)S(1)}, u32[]{:S(2)}, u32[]{:S(2)}) %collective-permute-start.10) | collective-permute-done | bytes 524320 | tf_op jit(solution)/shard_map/ppermute | solution.py:19
  62.1 1.7 copy-done.1
  63.8 5.9 %project.1 = (bf16[256,512]{1,0:T(8,128)(2,1)S(1)}, bf16[256,128]{1,0:T(8,128)(2,1)S(1)}) custom-call(s32[7]{0:T(128)S(1)} %stack.31.at_ref, bf16[256,8192]{1,0:T(8,128)(2,1)S(1)} %get-tuple-element.57.refs_0_.refs_3_, bf16[8192,512]{1,0:T(8,128)(2,1)S(1)} %copy-done, bf16[8192,128]{1,0:T(8,128)(2,1)S(1)} %copy-done.1, f32[256,128]{1,0:T(8,128)S(1)} %copy-done.16, ...), custom_call_target="tpu_custom_call" | custom-call | flops 1 | bytes 1 | tf_op jit(solution)/shard_map/project/pallas_call | solution.py:38
  71.1 1.8 attend.1
  72.9 5.5 %mix.1 = (bf16[8,16,8192]{2,1,0:T(8,128)(2,1)S(1)}, bf16[8,16,8192]{2,1,0:T(8,128)(2,1)S(1)}) custom-call(s32[7]{0:T(128)S(1)} %stack.31.at_ref, bf16[256,512]{1,0:T(8,128)(2,1)S(1)} %get-tuple-element.63.refs_0_, bf16[512,8192]{1,0:T(8,128)(2,1)S(1)} %bitcast.27), custom_call_target="tpu_custom_call" | custom-call | flops 1 | bytes 1 | tf_op jit(solution)/shard_map/mix/pallas_call | solution.py:38
  80.2 3.9 %collective-permute-start.15 = (bf16[2,512,256]{2,1,0:T(8,128)(2,1)S(1)}, bf16[2,512,256]{2,1,0:T(8,128)(2,1)S(1)}, u32[]{:S(2)}, u32[]{:S(2)}) collective-permute-start(bf16[2,512,256]{2,1,0:T(8,128)(2,1)S(1)} %get-tuple-element.66), channel_id=1, source_target_pairs={{0,64},{16,80},{32,96},{48,112},{64,0},{80,16},{96,32},{112,48},{1... | collective-permute-start | bytes 1572872 | tf_op jit(solution)/shard_map/ppermute | solution.py:19
  85.2 11.1 %collective-permute-done.15.refs_2_ = bf16[2,512,256]{2,1,0:T(8,128)(2,1)S(1)} collective-permute-done((bf16[2,512,256]{2,1,0:T(8,128)(2,1)S(1)}, bf16[2,512,256]{2,1,0:T(8,128)(2,1)S(1)}, u32[]{:S(2)}, u32[]{:S(2)}) %collective-permute-start.15) | collective-permute-done | bytes 524320 | tf_op jit(solution)/shard_map/ppermute | solution.py:19
  98.9 2.5 collective-permute-start.22
  104.5 5.2 %out_gradient.1 = (bf16[256,512]{1,0:T(8,128)(2,1)S(1)}, bf16[16,8192]{1,0:T(8,128)(2,1)S(1)}) custom-call(s32[7]{0:T(128)S(1)} %stack.31.at_ref, bf16[8,256,512]{2,1,0:T(8,128)(2,1)S(1)} %stack_cot.1.refs_0_, bf16[8,256,512]{2,1,0:T(8,128)(2,1)S(1)} %collective-permute-done.20.refs_1_, bf16[512,8192]{1,0:T(8,128)(2,1)S(1)} %bitcast.27, ...), custom_call_target="tpu_custom_call" | custom-call | flops 1 | bytes 1 | tf_op jit(solution)/shard_map/out_gradient/pallas_call | solution.py:38
  111.1 1.9 collective-permute-done.22.refs_8_.refs_3_
  113.0 2.3 attend_gradient.1
  117.9 4.4 %collective-permute-done.25.refs_5_.refs_1_ = bf16[4,512,256]{2,1,0:T(8,128)(2,1)S(1)} collective-permute-done((bf16[4,512,256]{2,1,0:T(8,128)(2,1)S(1)}, bf16[4,512,256]{2,1,0:T(8,128)(2,1)S(1)}, u32[]{:S(2)}, u32[]{:S(2)}) %collective-permute-start.25) | collective-permute-done | bytes 1048608 | tf_op jit(solution)/shard_map/ppermute | solution.py:19
  122.3 6.3 %norm_gradient.1 = (bf16[8,16,8192]{2,1,0:T(8,128)(2,1)S(1)}, bf16[8,16,8192]{2,1,0:T(8,128)(2,1)S(1)}, f32[8,1,1024]{2,1,0:T(1,128)S(1)}) custom-call(s32[7]{0:T(128)S(1)} %stack.31.at_ref, bf16[256,640]{1,0:T(8,128)(2,1)S(1)} %get-tuple-element.82.refs_0_, bf16[8192,512]{1,0:T(8,128)(2,1)S(1)} %copy-done, bf16[8192,128]{1,0:T(8,128)(2,1)S(1)} %copy-done.2, ...), custom_call_target="tpu_custom_call" | custom-call | flops 1 | bytes 1 | tf_op jit(solution)/shard_map/norm_gradient/pallas_call | solution.py:38
  130.6 3.6 %collective-permute-start.33 = (bf16[2,256,512]{2,1,0:T(8,128)(2,1)S(1)}, bf16[2,256,512]{2,1,0:T(8,128)(2,1)S(1)}, u32[]{:S(2)}, u32[]{:S(2)}) collective-permute-start(bf16[2,256,512]{2,1,0:T(8,128)(2,1)S(1)} %get-tuple-element.93), channel_id=1, source_target_pairs={{0,64},{16,80},{32,96},{48,112},{64,0},{80,16},{96,32},{112,48},{1... | collective-permute-start | bytes 1572872 | tf_op jit(solution)/shard_map/ppermute | solution.py:19
  134.4 3.4 %collective-permute-done.26.refs_3_ = bf16[512,256]{1,0:T(8,128)(2,1)S(1)} collective-permute-done((bf16[512,256]{1,0:T(8,128)(2,1)S(1)}, bf16[512,256]{1,0:T(8,128)(2,1)S(1)}, u32[]{:S(2)}, u32[]{:S(2)}) %collective-permute-start.26) | collective-permute-done | bytes 262176 | tf_op jit(solution)/shard_map/ppermute | solution.py:19
  137.8 3.1 %collective-permute-start.27 = (bf16[512,256]{1,0:T(8,128)(2,1)S(1)}, bf16[512,256]{1,0:T(8,128)(2,1)S(1)}, u32[]{:S(2)}, u32[]{:S(2)}) collective-permute-start(bf16[512,256]{1,0:T(8,128)(2,1)S(1)} %get-tuple-element.85.refs_2_), channel_id=1, source_target_pairs={{0,96},{16,112},{32,64},{48,80},{64,32},{80,48},{96,0},{112,16},{1... | collective-permute-start | bytes 786440 | tf_op jit(solution)/shard_map/ppermute | solution.py:19
  140.9 15.8 %collective-permute-done.27.refs_4_.refs_5_ = bf16[512,256]{1,0:T(8,128)(2,1)S(1)} collective-permute-done((bf16[512,256]{1,0:T(8,128)(2,1)S(1)}, bf16[512,256]{1,0:T(8,128)(2,1)S(1)}, u32[]{:S(2)}, u32[]{:S(2)}) %collective-permute-start.27) | collective-permute-done | bytes 262176 | tf_op jit(solution)/shard_map/ppermute | solution.py:19
  158.0 2.2 ring_sum.2
  160.2 2.8 %pair_sum.3 = (bf16[2,16,8192]{2,1,0:T(8,128)(2,1)S(1)}, bf16[2,16,8192]{2,1,0:T(8,128)(2,1)}, bf16[2,16,8192]{2,1,0:T(8,128)(2,1)}, bf16[2,16,8192]{2,1,0:T(8,128)(2,1)}) custom-call(s32[7]{0:T(128)S(1)} %stack.31.at_ref, bf16[8,16,8192]{2,1,0:T(8,128)(2,1)S(1)} %get-tuple-element.88.refs_0_, bf16[8,16,8192]{2,1,0:T(8,128)(2,1)S(1)} %collective-permute-done.29.refs_1_, ...), custom_call_target="tpu_custom_call" | custom-call | flops 1 | bytes 1 | tf_op jit(solution)/shard_map/pair_sum/pallas_call | solution.py:38
  164.9 3.6 %collective-permute-start.35 = (bf16[512,256]{1,0:T(8,128)(2,1)S(1)}, bf16[512,256]{1,0:T(8,128)(2,1)S(1)}, u32[]{:S(2)}, u32[]{:S(2)}) collective-permute-start(bf16[512,256]{1,0:T(8,128)(2,1)S(1)} %get-tuple-element.85.refs_2_), channel_id=1, source_target_pairs={{0,64},{16,80},{32,96},{48,112},{64,0},{80,16},{96,32},{112,48},{1... | collective-permute-start | bytes 786440 | tf_op jit(solution)/shard_map/ppermute | solution.py:19
  169.0 17.7 %collective-permute-done.35.refs_4_ = bf16[512,256]{1,0:T(8,128)(2,1)S(1)} collective-permute-done((bf16[512,256]{1,0:T(8,128)(2,1)S(1)}, bf16[512,256]{1,0:T(8,128)(2,1)S(1)}, u32[]{:S(2)}, u32[]{:S(2)}) %collective-permute-start.35) | collective-permute-done | bytes 262176 | tf_op jit(solution)/shard_map/ppermute | solution.py:19
  188.3 2.3 collective-permute-start.32
  191.5 2.1 collective-permute-start.28
  193.6 10.4 %all_to_all.10 = f32[8,1,1024]{2,1,0:T(1,128)S(1)} all-to-all(f32[8,1,1024]{2,1,0:T(1,128)S(1)} %get-tuple-element.99), channel_id=1, replica_groups=mesh['dp'=8,'tensor'=16] {'dp'}, dimensions={0} | all-to-all | bytes 65536 | tf_op jit(solution)/shard_map/all_to_all | solution.py:748
  204.7 5.1 %all-to-all-start.1 = ((f32[16,1,1024]{2,1,0:T(1,128)}), f32[16,1,1024]{2,1,0:T(1,128)S(1)}, u32[]{:S(2)}, u32[]{:S(2)}) async-start(f32[16,1,1024]{2,1,0:T(1,128)} %broadcast_in_dim.62), calls=%async_computation.1 | async-start | bytes 131072 | tf_op jit(solution)/shard_map/all_to_all | solution.py:750
  210.9 3.8 %all-to-all-done.1 = f32[16,1,1024]{2,1,0:T(1,128)S(1)} async-done(((f32[16,1,1024]{2,1,0:T(1,128)}), f32[16,1,1024]{2,1,0:T(1,128)S(1)}, u32[]{:S(2)}, u32[]{:S(2)}) %all-to-all-start.1) | async-done | bytes 65568 | tf_op jit(solution)/shard_map/all_to_all | solution.py:750
  220.4 5.8 %out_terms.1 = (bf16[512,1024]{1,0:T(8,128)(2,1)S(1)}, f32[512,1024]{1,0:T(8,128)S(1)}) custom-call(s32[7]{0:T(128)S(1)} %stack.31.at_ref, bf16[4,2,256,512]{3,2,1,0:T(8,128)(2,1)S(1)} %bitcast.28, bf16[4,2,256,512]{3,2,1,0:T(8,128)(2,1)} %bitcast.22.refs_1_, bf16[512,256]{1,0:T(8,128)(2,1)S(1)} %copy-done.29, bf16[512,256]{1,0:T(8,128)(2,1)S(1)} %copy-done.21, ...), custom_call_target="tpu_custom_call" | custom-call | flops 1 | bytes 1 | tf_op jit(solution)/shard_map/out_terms/pallas_call | solution.py:38
  226.8 2.2 collective-permute-start.41
  229.4 3.0 %ring_sum.3 = (f32[16,8192]{1,0:T(8,128)S(1)}, bf16[16,8192]{1,0:T(8,128)(2,1)S(1)}) custom-call(s32[7]{0:T(128)S(1)} %stack.31.at_ref, bf16[2,16,8192]{2,1,0:T(8,128)(2,1)S(1)} %copy-done.15, bf16[2,16,8192]{2,1,0:T(8,128)(2,1)} %collective-permute-done.30.refs_1_, bf16[2,16,8192]{2,1,0:T(8,128)(2,1)} %collective-permute-done.31.refs_2_, ...), custom_call_target="tpu_custom_call" | custom-call | flops 1 | bytes 1 | tf_op jit(solution)/shard_map/ring_sum/pallas_call | solution.py:38
  232.5 3.8 %collective-permute-start.38 = (bf16[16,8192]{1,0:T(8,128)(2,1)S(1)}, bf16[16,8192]{1,0:T(8,128)(2,1)S(1)}, u32[]{:S(2)}, u32[]{:S(2)}) collective-permute-start(bf16[16,8192]{1,0:T(8,128)(2,1)S(1)} %get-tuple-element.96), channel_id=1, source_target_pairs={{0,2},{1,3},{2,0},{3,1},{4,6},{5,7},{6,4},{7,5},{8,10},{9,11},{10,... | collective-permute-start | bytes 786440 | tf_op jit(solution)/shard_map/ppermute | solution.py:19
  236.3 1.7 fusion
  238.0 7.0 %collective-permute-done.41.refs_6_ = bf16[2,256,640]{2,1,0:T(8,128)(2,1)S(1)} collective-permute-done((bf16[2,256,640]{2,1,0:T(8,128)(2,1)S(1)}, bf16[2,256,640]{2,1,0:T(8,128)(2,1)S(1)}, u32[]{:S(2)}, u32[]{:S(2)}) %collective-permute-start.41) | collective-permute-done | bytes 655392 | tf_op jit(solution)/shard_map/ppermute | solution.py:19
  245.0 7.4 %q_gradient.1 = (f32[1024,512]{1,0:T(8,128)}, f32[1024,128]{1,0:T(8,128)}) custom-call(s32[7]{0:T(128)S(1)} %stack.31.at_ref, bf16[4,512,256]{2,1,0:T(8,128)(2,1)S(1)} %copy-done.6, bf16[4,512,256]{2,1,0:T(8,128)(2,1)S(1)} %copy-done.4, bf16[4,512,256]{2,1,0:T(8,128)(2,1)S(1)} %collective-permute-done.39.refs_2_, ...), custom_call_target="tpu_custom_call" | custom-call | flops 1 | bytes 1 | tf_op jit(solution)/shard_map/q_gradient/pallas_call | solution.py:38
  252.5 8.9 %collective-permute-done.38.refs_1_ = bf16[16,8192]{1,0:T(8,128)(2,1)S(1)} collective-permute-done((bf16[16,8192]{1,0:T(8,128)(2,1)S(1)}, bf16[16,8192]{1,0:T(8,128)(2,1)S(1)}, u32[]{:S(2)}, u32[]{:S(2)}) %collective-permute-start.38) | collective-permute-done | bytes 262176 | tf_op jit(solution)/shard_map/ppermute | solution.py:19
  264.5 1.8 convert_add_fusion
  (147 shorter events, 44.4 us)
Async XLA Ops:
  0.6 10.3 %collective-permute-start = (bf16[256,512]{1,0:T(8,128)(2,1)}, bf16[256,512]{1,0:T(8,128)(2,1)S(1)}, u32[]{:S(2)}, u32[]{:S(2)}) collective-permute-start(bf16[256,512]{1,0:T(8,128)(2,1)} %bitcast.34), channel_id=1, source_target_pairs={{0,2},{1,3},{2,0},{3,1},{4,6},{5,7},{6,4},{7,5},{8,10},{9,11},{10,... | collective-permute-start | bytes 786440 | tf_op jit(solution)/shard_map/ppermute | solution.py:19
  2.1 11.1 %collective-permute-start.1 = (bf16[256,512]{1,0:T(8,128)(2,1)}, bf16[256,512]{1,0:T(8,128)(2,1)S(1)}, u32[]{:S(2)}, u32[]{:S(2)}) collective-permute-start(bf16[256,512]{1,0:T(8,128)(2,1)} %bitcast.35), channel_id=1, source_target_pairs={{0,4},{1,5},{2,6},{3,7},{4,0},{5,1},{6,2},{7,3},{8,12},{9,13},{10,... | collective-permute-start | bytes 786440 | tf_op jit(solution)/shard_map/ppermute | solution.py:19
  3.7 16.0 %collective-permute-start.3 = (bf16[256,512]{1,0:T(8,128)(2,1)}, bf16[256,512]{1,0:T(8,128)(2,1)S(1)}, u32[]{:S(2)}, u32[]{:S(2)}) collective-permute-start(bf16[256,512]{1,0:T(8,128)(2,1)} %bitcast.36), channel_id=1, source_target_pairs={{0,8},{1,9},{2,10},{3,11},{4,12},{5,13},{6,14},{7,15},{8,0},{9,1},... | collective-permute-start | bytes 786440 | tf_op jit(solution)/shard_map/ppermute | solution.py:19
  6.6 14.4 %collective-permute-start.5 = (bf16[256,512]{1,0:T(8,128)(2,1)}, bf16[256,512]{1,0:T(8,128)(2,1)S(1)}, u32[]{:S(2)}, u32[]{:S(2)}) collective-permute-start(bf16[256,512]{1,0:T(8,128)(2,1)} %bitcast.37), channel_id=1, source_target_pairs={{0,12},{1,13},{2,14},{3,15},{4,8},{5,9},{6,10},{7,11},{8,4},{9,5},... | collective-permute-start | bytes 786440 | tf_op jit(solution)/shard_map/ppermute | solution.py:19
  6.8 14.1 %collective-permute-start.7 = (bf16[256,512]{1,0:T(8,128)(2,1)}, bf16[256,512]{1,0:T(8,128)(2,1)S(1)}, u32[]{:S(2)}, u32[]{:S(2)}) collective-permute-start(bf16[256,512]{1,0:T(8,128)(2,1)} %bitcast.38), channel_id=1, source_target_pairs={{0,2},{1,3},{2,0},{3,1},{4,6},{5,7},{6,4},{7,5},{8,10},{9,11},{10,... | collective-permute-start | bytes 786440 | tf_op jit(solution)/shard_map/ppermute | solution.py:19
  11.0 11.9 %collective-permute-start.2 = (bf16[256,512]{1,0:T(8,128)(2,1)S(1)}, bf16[256,512]{1,0:T(8,128)(2,1)S(1)}, u32[]{:S(2)}, u32[]{:S(2)}) collective-permute-start(bf16[256,512]{1,0:T(8,128)(2,1)S(1)} %collective-permute-done), channel_id=1, source_target_pairs={{0,4},{1,5},{2,6},{3,7},{4,0},{5,1},{6,2},{7,3},{8,12},{9,13},{10,... | collective-permute-start | bytes 786440 | tf_op jit(solution)/shard_map/ppermute | solution.py:19
  13.2 16.3 %collective-permute-start.4 = (bf16[256,512]{1,0:T(8,128)(2,1)S(1)}, bf16[256,512]{1,0:T(8,128)(2,1)S(1)}, u32[]{:S(2)}, u32[]{:S(2)}) collective-permute-start(bf16[256,512]{1,0:T(8,128)(2,1)S(1)} %collective-permute-done), channel_id=1, source_target_pairs={{0,8},{1,9},{2,10},{3,11},{4,12},{5,13},{6,14},{7,15},{8,0},{9,1},... | collective-permute-start | bytes 786440 | tf_op jit(solution)/shard_map/ppermute | solution.py:19
  19.7 12.4 %collective-permute-start.6 = (bf16[256,512]{1,0:T(8,128)(2,1)S(1)}, bf16[256,512]{1,0:T(8,128)(2,1)S(1)}, u32[]{:S(2)}, u32[]{:S(2)}) collective-permute-start(bf16[256,512]{1,0:T(8,128)(2,1)S(1)} %collective-permute-done), channel_id=1, source_target_pairs={{0,12},{1,13},{2,14},{3,15},{4,8},{5,9},{6,10},{7,11},{8,4},{9,5},... | collective-permute-start | bytes 786440 | tf_op jit(solution)/shard_map/ppermute | solution.py:19
  19.9 25.2 %copy-start.34 = (bf16[8192]{0:T(1024)(128)(2,1)S(1)}, bf16[8192]{0:T(1024)(128)(2,1)}, u32[]{:S(2)}) copy-start(bf16[8192]{0:T(1024)(128)(2,1)} %param.9) | copy-start | bytes 49156
  34.0 28.1 %copy-start = (bf16[8192,512]{1,0:T(8,128)(2,1)S(1)}, bf16[8192,512]{1,0:T(8,128)(2,1)}, u32[]{:S(2)}) copy-start(bf16[8192,512]{1,0:T(8,128)(2,1)} %refs_1_.5) | copy-start | bytes 25165828
  35.2 6.2 %collective-permute-start.8 = (bf16[8,256,512]{2,1,0:T(8,128)(2,1)S(1)}, bf16[8,256,512]{2,1,0:T(8,128)(2,1)S(1)}, u32[]{:S(2)}, u32[]{:S(2)}) collective-permute-start(bf16[8,256,512]{2,1,0:T(8,128)(2,1)S(1)} %get-tuple-element.54.refs_0_.refs_1_), channel_id=1, source_target_pairs={{0,1},{1,0},{2,3},{3,2},{4,5},{5,4},{6,7},{7,6},{8,9},{9,8},{10,11... | collective-permute-start | bytes 6291464 | tf_op jit(solution)/shard_map/ppermute | solution.py:19
  35.3 14.8 %collective-permute-start.9 = (bf16[2,256,512]{2,1,0:T(8,128)(2,1)S(1)}, bf16[2,256,512]{2,1,0:T(8,128)(2,1)S(1)}, u32[]{:S(2)}, u32[]{:S(2)}) collective-permute-start(bf16[2,256,512]{2,1,0:T(8,128)(2,1)S(1)} %get-tuple-element.58.refs_0_), channel_id=1, source_target_pairs={{0,4},{1,5},{2,6},{3,7},{4,0},{5,1},{6,2},{7,3},{8,12},{9,13},{10,... | collective-permute-start | bytes 1572872 | tf_op jit(solution)/shard_map/ppermute | solution.py:19
  35.4 26.7 %collective-permute-start.10 = (bf16[2,256,512]{2,1,0:T(8,128)(2,1)S(1)}, bf16[2,256,512]{2,1,0:T(8,128)(2,1)S(1)}, u32[]{:S(2)}, u32[]{:S(2)}) collective-permute-start(bf16[2,256,512]{2,1,0:T(8,128)(2,1)S(1)} %get-tuple-element.58.refs_0_), channel_id=1, source_target_pairs={{0,12},{1,13},{2,14},{3,15},{4,8},{5,9},{6,10},{7,11},{8,4},{9,5},... | collective-permute-start | bytes 1572872 | tf_op jit(solution)/shard_map/ppermute | solution.py:19
  36.9 32.9 %collective-permute-start.12 = (bf16[2,512,256]{2,1,0:T(8,128)(2,1)S(1)}, bf16[2,512,256]{2,1,0:T(8,128)(2,1)S(1)}, u32[]{:S(2)}, u32[]{:S(2)}) collective-permute-start(bf16[2,512,256]{2,1,0:T(8,128)(2,1)S(1)} %get-tuple-element.61), channel_id=1, source_target_pairs={{0,32},{16,48},{32,0},{48,16},{64,96},{80,112},{96,64},{112,80},{1... | collective-permute-start | bytes 1572872 | tf_op jit(solution)/shard_map/ppermute | solution.py:19
  38.9 31.0 %collective-permute-start.13 = (bf16[2,512,256]{2,1,0:T(8,128)(2,1)S(1)}, bf16[2,512,256]{2,1,0:T(8,128)(2,1)S(1)}, u32[]{:S(2)}, u32[]{:S(2)}) collective-permute-start(bf16[2,512,256]{2,1,0:T(8,128)(2,1)S(1)} %get-tuple-element.62), channel_id=1, source_target_pairs={{0,96},{16,112},{32,64},{48,80},{64,32},{80,48},{96,0},{112,16},{1... | collective-permute-start | bytes 1572872 | tf_op jit(solution)/shard_map/ppermute | solution.py:19
  41.4 37.2 %collective-permute-start.16 = (bf16[2,256,512]{2,1,0:T(8,128)(2,1)S(1)}, bf16[2,256,512]{2,1,0:T(8,128)(2,1)S(1)}, u32[]{:S(2)}, u32[]{:S(2)}) collective-permute-start(bf16[2,256,512]{2,1,0:T(8,128)(2,1)S(1)} %get-tuple-element.58.refs_0_), channel_id=1, source_target_pairs={{0,8},{1,9},{2,10},{3,11},{4,12},{5,13},{6,14},{7,15},{8,0},{9,1},... | collective-permute-start | bytes 1572872 | tf_op jit(solution)/shard_map/ppermute | solution.py:19
  48.9 68.3 %copy-start.24 = (f32[256,1]{1,0:T(8,128)}, f32[256,1]{1,0:T(8,128)S(1)}, u32[]{:S(2)}) copy-start(f32[256,1]{1,0:T(8,128)S(1)} %get-tuple-element.80.refs_3_) | copy-start | bytes 3076
  69.8 1.3 collective-permute-start.11
  72.9 92.0 %copy-start.28 = (bf16[512,256]{1,0:T(8,128)(2,1)}, bf16[512,256]{1,0:T(8,128)(2,1)S(1)}, u32[]{:S(2)}) copy-start(bf16[512,256]{1,0:T(8,128)(2,1)S(1)} %get-tuple-element.85.refs_2_) | copy-start | bytes 786436
  78.4 23.1 %collective-permute-start.14 = (bf16[8,16,8192]{2,1,0:T(8,128)(2,1)S(1)}, bf16[8,16,8192]{2,1,0:T(8,128)(2,1)S(1)}, u32[]{:S(2)}, u32[]{:S(2)}) collective-permute-start(bf16[8,16,8192]{2,1,0:T(8,128)(2,1)S(1)} %get-tuple-element.65.refs_4_), channel_id=1, source_target_pairs={{0,1},{1,0},{2,3},{3,2},{4,5},{5,4},{6,7},{7,6},{8,9},{9,8},{10,11... | collective-permute-start | bytes 6291464 | tf_op jit(solution)/shard_map/ppermute | solution.py:19
  79.8 23.9 %collective-permute-start.20 = (bf16[8,256,512]{2,1,0:T(8,128)(2,1)S(1)}, bf16[8,256,512]{2,1,0:T(8,128)(2,1)S(1)}, u32[]{:S(2)}, u32[]{:S(2)}) collective-permute-start(bf16[8,256,512]{2,1,0:T(8,128)(2,1)S(1)} %stack_cot.1.refs_0_), channel_id=1, source_target_pairs={{0,1},{1,0},{2,3},{3,2},{4,5},{5,4},{6,7},{7,6},{8,9},{9,8},{10,11... | collective-permute-start | bytes 6291464 | tf_op jit(solution)/shard_map/ppermute | solution.py:19
  80.2 16.1 %collective-permute-start.15 = (bf16[2,512,256]{2,1,0:T(8,128)(2,1)S(1)}, bf16[2,512,256]{2,1,0:T(8,128)(2,1)S(1)}, u32[]{:S(2)}, u32[]{:S(2)}) collective-permute-start(bf16[2,512,256]{2,1,0:T(8,128)(2,1)S(1)} %get-tuple-element.66), channel_id=1, source_target_pairs={{0,64},{16,80},{32,96},{48,112},{64,0},{80,16},{96,32},{112,48},{1... | collective-permute-start | bytes 1572872 | tf_op jit(solution)/shard_map/ppermute | solution.py:19
  97.5 24.8 %collective-permute-start.25 = (bf16[4,512,256]{2,1,0:T(8,128)(2,1)S(1)}, bf16[4,512,256]{2,1,0:T(8,128)(2,1)S(1)}, u32[]{:S(2)}, u32[]{:S(2)}) collective-permute-start(bf16[4,512,256]{2,1,0:T(8,128)(2,1)S(1)} %get-tuple-element.83), channel_id=1, source_target_pairs={{0,16},{16,0},{32,48},{48,32},{64,80},{80,64},{96,112},{112,96},{1... | collective-permute-start | bytes 3145736 | tf_op jit(solution)/shard_map/ppermute | solution.py:19
  97.6 13.6 %collective-permute-start.21 = (bf16[2,256,512]{2,1,0:T(8,128)(2,1)S(1)}, bf16[2,256,512]{2,1,0:T(8,128)(2,1)S(1)}, u32[]{:S(2)}, u32[]{:S(2)}) collective-permute-start(bf16[2,256,512]{2,1,0:T(8,128)(2,1)S(1)} %get-tuple-element.75), channel_id=1, source_target_pairs={{0,32},{16,48},{32,0},{48,16},{64,96},{80,112},{96,64},{112,80},{1... | collective-permute-start | bytes 1572872 | tf_op jit(solution)/shard_map/ppermute | solution.py:19
  98.9 14.1 %collective-permute-start.22 = (bf16[2,256,512]{2,1,0:T(8,128)(2,1)S(1)}, bf16[2,256,512]{2,1,0:T(8,128)(2,1)S(1)}, u32[]{:S(2)}, u32[]{:S(2)}) collective-permute-start(bf16[2,256,512]{2,1,0:T(8,128)(2,1)S(1)} %get-tuple-element.76), channel_id=1, source_target_pairs={{0,96},{16,112},{32,64},{48,80},{64,32},{80,48},{96,0},{112,16},{1... | collective-permute-start | bytes 1572872 | tf_op jit(solution)/shard_map/ppermute | solution.py:19
  103.0 13.6 %collective-permute-start.17 = (bf16[2,16,8192]{2,1,0:T(8,128)(2,1)S(1)}, bf16[2,16,8192]{2,1,0:T(8,128)(2,1)S(1)}, u32[]{:S(2)}, u32[]{:S(2)}) collective-permute-start(bf16[2,16,8192]{2,1,0:T(8,128)(2,1)S(1)} %get-tuple-element.70), channel_id=1, source_target_pairs={{0,4},{1,5},{2,6},{3,7},{4,0},{5,1},{6,2},{7,3},{8,12},{9,13},{10,... | collective-permute-start | bytes 1572872 | tf_op jit(solution)/shard_map/ppermute | solution.py:19
  103.6 13.5 %collective-permute-start.19 = (bf16[2,16,8192]{2,1,0:T(8,128)(2,1)S(1)}, bf16[2,16,8192]{2,1,0:T(8,128)(2,1)S(1)}, u32[]{:S(2)}, u32[]{:S(2)}) collective-permute-start(bf16[2,16,8192]{2,1,0:T(8,128)(2,1)S(1)} %get-tuple-element.72), channel_id=1, source_target_pairs={{0,12},{1,13},{2,14},{3,15},{4,8},{5,9},{6,10},{7,11},{8,4},{9,5},... | collective-permute-start | bytes 1572872 | tf_op jit(solution)/shard_map/ppermute | solution.py:19
  115.3 1.3 collective-permute-start.23
  128.6 31.6 %collective-permute-start.29 = (bf16[8,16,8192]{2,1,0:T(8,128)(2,1)S(1)}, bf16[8,16,8192]{2,1,0:T(8,128)(2,1)S(1)}, u32[]{:S(2)}, u32[]{:S(2)}) collective-permute-start(bf16[8,16,8192]{2,1,0:T(8,128)(2,1)S(1)} %get-tuple-element.84.refs_2_), channel_id=1, source_target_pairs={{0,1},{1,0},{2,3},{3,2},{4,5},{5,4},{6,7},{7,6},{8,9},{9,8},{10,11... | collective-permute-start | bytes 6291464 | tf_op jit(solution)/shard_map/ppermute | solution.py:19
  128.6 9.2 %collective-permute-start.26 = (bf16[512,256]{1,0:T(8,128)(2,1)S(1)}, bf16[512,256]{1,0:T(8,128)(2,1)S(1)}, u32[]{:S(2)}, u32[]{:S(2)}) collective-permute-start(bf16[512,256]{1,0:T(8,128)(2,1)S(1)} %get-tuple-element.85.refs_2_), channel_id=1, source_target_pairs={{0,32},{16,48},{32,0},{48,16},{64,96},{80,112},{96,64},{112,80},{1... | collective-permute-start | bytes 786440 | tf_op jit(solution)/shard_map/ppermute | solution.py:19
  129.7 28.3 %collective-permute-start.18 = (bf16[2,16,8192]{2,1,0:T(8,128)(2,1)S(1)}, bf16[2,16,8192]{2,1,0:T(8,128)(2,1)S(1)}, u32[]{:S(2)}, u32[]{:S(2)}) collective-permute-start(bf16[2,16,8192]{2,1,0:T(8,128)(2,1)S(1)} %get-tuple-element.71), channel_id=1, source_target_pairs={{0,8},{1,9},{2,10},{3,11},{4,12},{5,13},{6,14},{7,15},{8,0},{9,1},... | collective-permute-start | bytes 1572872 | tf_op jit(solution)/shard_map/ppermute | solution.py:19
  130.6 32.5 %collective-permute-start.33 = (bf16[2,256,512]{2,1,0:T(8,128)(2,1)S(1)}, bf16[2,256,512]{2,1,0:T(8,128)(2,1)S(1)}, u32[]{:S(2)}, u32[]{:S(2)}) collective-permute-start(bf16[2,256,512]{2,1,0:T(8,128)(2,1)S(1)} %get-tuple-element.93), channel_id=1, source_target_pairs={{0,64},{16,80},{32,96},{48,112},{64,0},{80,16},{96,32},{112,48},{1... | collective-permute-start | bytes 1572872 | tf_op jit(solution)/shard_map/ppermute | solution.py:19
  134.1 22.6 %collective-permute-start.24 = (bf16[256,640]{1,0:T(8,128)(2,1)S(1)}, bf16[256,640]{1,0:T(8,128)(2,1)S(1)}, u32[]{:S(2)}, u32[]{:S(2)}) collective-permute-start(bf16[256,640]{1,0:T(8,128)(2,1)S(1)} %get-tuple-element.81), channel_id=1, source_target_pairs={{0,16},{16,0},{32,48},{48,32},{64,80},{80,64},{96,112},{112,96},{1... | collective-permute-start | bytes 983048 | tf_op jit(solution)/shard_map/ppermute | solution.py:19
  137.8 18.9 %collective-permute-start.27 = (bf16[512,256]{1,0:T(8,128)(2,1)S(1)}, bf16[512,256]{1,0:T(8,128)(2,1)S(1)}, u32[]{:S(2)}, u32[]{:S(2)}) collective-permute-start(bf16[512,256]{1,0:T(8,128)(2,1)S(1)} %get-tuple-element.85.refs_2_), channel_id=1, source_target_pairs={{0,96},{16,112},{32,64},{48,80},{64,32},{80,48},{96,0},{112,16},{1... | collective-permute-start | bytes 786440 | tf_op jit(solution)/shard_map/ppermute | solution.py:19
  164.2 51.2 %collective-permute-start.34 = (bf16[8,256,512]{2,1,0:T(8,128)(2,1)S(1)}, bf16[8,256,512]{2,1,0:T(8,128)(2,1)}, u32[]{:S(2)}, u32[]{:S(2)}) collective-permute-start(bf16[8,256,512]{2,1,0:T(8,128)(2,1)S(1)} %stack_b.1.refs_6_), channel_id=1, source_target_pairs={{0,1},{1,0},{2,3},{3,2},{4,5},{5,4},{6,7},{7,6},{8,9},{9,8},{10,11... | collective-permute-start | bytes 6291464 | tf_op jit(solution)/shard_map/ppermute | solution.py:19
  164.3 24.0 %collective-permute-start.36 = (bf16[2,256,640]{2,1,0:T(8,128)(2,1)S(1)}, bf16[2,256,640]{2,1,0:T(8,128)(2,1)S(1)}, u32[]{:S(2)}, u32[]{:S(2)}) collective-permute-start(bf16[2,256,640]{2,1,0:T(8,128)(2,1)S(1)} %stack_dqkv.1.refs_4_), channel_id=1, source_target_pairs={{0,32},{16,48},{32,0},{48,16},{64,96},{80,112},{96,64},{112,80},{1... | collective-permute-start | bytes 1966088 | tf_op jit(solution)/shard_map/ppermute | solution.py:19
  164.4 26.3 %collective-permute-start.37 = (bf16[2,256,640]{2,1,0:T(8,128)(2,1)S(1)}, bf16[2,256,640]{2,1,0:T(8,128)(2,1)S(1)}, u32[]{:S(2)}, u32[]{:S(2)}) collective-permute-start(bf16[2,256,640]{2,1,0:T(8,128)(2,1)S(1)} %stack_dqkv.1.refs_4_), channel_id=1, source_target_pairs={{0,96},{16,112},{32,64},{48,80},{64,32},{80,48},{96,0},{112,16},{1... | collective-permute-start | bytes 1966088 | tf_op jit(solution)/shard_map/ppermute | solution.py:19
  164.9 21.9 %collective-permute-start.35 = (bf16[512,256]{1,0:T(8,128)(2,1)S(1)}, bf16[512,256]{1,0:T(8,128)(2,1)S(1)}, u32[]{:S(2)}, u32[]{:S(2)}) collective-permute-start(bf16[512,256]{1,0:T(8,128)(2,1)S(1)} %get-tuple-element.85.refs_2_), channel_id=1, source_target_pairs={{0,64},{16,80},{32,96},{48,112},{64,0},{80,16},{96,32},{112,48},{1... | collective-permute-start | bytes 786440 | tf_op jit(solution)/shard_map/ppermute | solution.py:19
  168.4 57.8 %collective-permute-start.30 = (bf16[2,16,8192]{2,1,0:T(8,128)(2,1)}, bf16[2,16,8192]{2,1,0:T(8,128)(2,1)}, u32[]{:S(2)}, u32[]{:S(2)}) collective-permute-start(bf16[2,16,8192]{2,1,0:T(8,128)(2,1)} %get-tuple-element.90), channel_id=1, source_target_pairs={{0,4},{1,5},{2,6},{3,7},{4,0},{5,1},{6,2},{7,3},{8,12},{9,13},{10,... | collective-permute-start | bytes 1572872 | tf_op jit(solution)/shard_map/ppermute | solution.py:19
  187.4 39.3 %collective-permute-start.31 = (bf16[2,16,8192]{2,1,0:T(8,128)(2,1)}, bf16[2,16,8192]{2,1,0:T(8,128)(2,1)}, u32[]{:S(2)}, u32[]{:S(2)}) collective-permute-start(bf16[2,16,8192]{2,1,0:T(8,128)(2,1)} %get-tuple-element.91), channel_id=1, source_target_pairs={{0,8},{1,9},{2,10},{3,11},{4,12},{5,13},{6,14},{7,15},{8,0},{9,1},... | collective-permute-start | bytes 1572872 | tf_op jit(solution)/shard_map/ppermute | solution.py:19
  188.3 40.6 %collective-permute-start.32 = (bf16[2,16,8192]{2,1,0:T(8,128)(2,1)}, bf16[2,16,8192]{2,1,0:T(8,128)(2,1)}, u32[]{:S(2)}, u32[]{:S(2)}) collective-permute-start(bf16[2,16,8192]{2,1,0:T(8,128)(2,1)} %get-tuple-element.92), channel_id=1, source_target_pairs={{0,12},{1,13},{2,14},{3,15},{4,8},{5,9},{6,10},{7,11},{8,4},{9,5},... | collective-permute-start | bytes 1572872 | tf_op jit(solution)/shard_map/ppermute | solution.py:19
  191.5 41.0 %collective-permute-start.28 = (bf16[16,8192]{1,0:T(8,128)(2,1)}, bf16[16,8192]{1,0:T(8,128)(2,1)}, u32[]{:S(2)}, u32[]{:S(2)}) collective-permute-start(bf16[16,8192]{1,0:T(8,128)(2,1)} %get-tuple-element.87), channel_id=1, source_target_pairs={{0,2},{1,3},{2,0},{3,1},{4,6},{5,7},{6,4},{7,5},{8,10},{9,11},{10,... | collective-permute-start | bytes 786440 | tf_op jit(solution)/shard_map/ppermute | solution.py:19
  204.7 10.0 %all-to-all-start.1 = ((f32[16,1,1024]{2,1,0:T(1,128)}), f32[16,1,1024]{2,1,0:T(1,128)S(1)}, u32[]{:S(2)}, u32[]{:S(2)}) async-start(f32[16,1,1024]{2,1,0:T(1,128)} %broadcast_in_dim.62), calls=%async_computation.1 | async-start | bytes 131072 | tf_op jit(solution)/shard_map/all_to_all | solution.py:750
  215.4 22.6 %collective-permute-start.39 = (bf16[4,512,256]{2,1,0:T(8,128)(2,1)}, bf16[4,512,256]{2,1,0:T(8,128)(2,1)S(1)}, u32[]{:S(2)}, u32[]{:S(2)}) collective-permute-start(bf16[4,512,256]{2,1,0:T(8,128)(2,1)} %copy-done.5), channel_id=1, source_target_pairs={{0,1},{1,0},{2,3},{3,2},{4,5},{5,4},{6,7},{7,6},{8,9},{9,8},{10,11... | collective-permute-start | bytes 3145736 | tf_op jit(solution)/shard_map/ppermute | solution.py:19
  226.3 11.7 %collective-permute-start.40 = (bf16[4,512,256]{2,1,0:T(8,128)(2,1)S(1)}, bf16[4,512,256]{2,1,0:T(8,128)(2,1)S(1)}, u32[]{:S(2)}, u32[]{:S(2)}) collective-permute-start(bf16[4,512,256]{2,1,0:T(8,128)(2,1)S(1)} %copy-done.4), channel_id=1, source_target_pairs={{0,1},{1,0},{2,3},{3,2},{4,5},{5,4},{6,7},{7,6},{8,9},{9,8},{10,11... | collective-permute-start | bytes 3145736 | tf_op jit(solution)/shard_map/ppermute | solution.py:19
  226.8 18.3 %collective-permute-start.41 = (bf16[2,256,640]{2,1,0:T(8,128)(2,1)S(1)}, bf16[2,256,640]{2,1,0:T(8,128)(2,1)S(1)}, u32[]{:S(2)}, u32[]{:S(2)}) collective-permute-start(bf16[2,256,640]{2,1,0:T(8,128)(2,1)S(1)} %stack_dqkv.1.refs_4_), channel_id=1, source_target_pairs={{0,64},{16,80},{32,96},{48,112},{64,0},{80,16},{96,32},{112,48},{1... | collective-permute-start | bytes 1966088 | tf_op jit(solution)/shard_map/ppermute | solution.py:19
  228.9 35.6 %collective-permute-start.42 = (bf16[512,1024]{1,0:T(8,128)(2,1)S(1)}, bf16[512,1024]{1,0:T(8,128)(2,1)S(1)}, u32[]{:S(2)}, u32[]{:S(2)}) collective-permute-start(bf16[512,1024]{1,0:T(8,128)(2,1)S(1)} %get-tuple-element.94.refs_4_), channel_id=1, source_target_pairs={{0,16},{16,0},{32,48},{48,32},{64,80},{80,64},{96,112},{112,96},{1... | collective-permute-start | bytes 3145736 | tf_op jit(solution)/shard_map/ppermute | solution.py:19
  232.5 28.9 %collective-permute-start.38 = (bf16[16,8192]{1,0:T(8,128)(2,1)S(1)}, bf16[16,8192]{1,0:T(8,128)(2,1)S(1)}, u32[]{:S(2)}, u32[]{:S(2)}) collective-permute-start(bf16[16,8192]{1,0:T(8,128)(2,1)S(1)} %get-tuple-element.96), channel_id=1, source_target_pairs={{0,2},{1,3},{2,0},{3,1},{4,6},{5,7},{6,4},{7,5},{8,10},{9,11},{10,... | collective-permute-start | bytes 786440 | tf_op jit(solution)/shard_map/ppermute | solution.py:19
  (33 other events, 259.1 us)

commit v2 on v1

--- a/solution.py
+++ b/solution.py
@@ -122,7 +122,7 @@
                 number += 1
         return pairs
 
-    outs = [shape((sum(p.shape[0] for p in g),) + g[0].shape[1:]) for g in groups]
+    outs = [shape((sum(p.shape[0] for p in g),) + g[0].shape[1:], g[0].dtype) for g in groups]
     return move(name, order, sources, outs, plan)
 
 
@@ -175,17 +175,24 @@
     )
 
 
-def pick_tokens(order, own):
+def pick_tokens(name, order, own, partners, *copied):
     chips, length, width = own.shape
-
-    def kernel(at_ref, own_ref, *out):
-        for k in range(4):
+    count = len(partners)
+
+    def kernel(at_ref, own_ref, *refs):
+        ins, out, copies = refs[: len(copied)], refs[len(copied) :][:count], refs[len(copied) + count :]
+        for number, k in enumerate(partners):
             for x in range(2):
-                block = own_ref[at_ref[CHIP] ^ (2 * (at_ref[Z] ^ k) + x)]
-                out[k][x] = block.T
-
-    return call(
-        kernel, "pick_tokens", order, [whole(own)], [whole_out((2, width, length))] * 4
+                out[number][x] = own_ref[at_ref[CHIP] ^ (2 * (at_ref[Z] ^ k) + x)].T
+        for source, target in zip(ins, copies):
+            target[...] = source[...]
+
+    return call(
+        kernel,
+        name,
+        order,
+        [whole(own)] + [whole(c) for c in copied],
+        [whole_out((2, width, length))] * count + [whole_out(c.shape) for c in copied],
     )
 
 
@@ -246,7 +253,7 @@
     heads = q_width // head
     scale = head ** (-0.5)
 
-    def kernel(at_ref, rot_ref, own_ref, other_ref, attn_ref, probs_ref, turned_ref):
+    def kernel(at_ref, rot_ref, own_ref, other_ref, attn_ref, probs_ref):
         even = at_ref[CORE] == 0
         key = jnp.where(even, own_ref[...], other_ref[...])
         value = jnp.where(even, other_ref[...], own_ref[...])
@@ -258,9 +265,7 @@
             expo = jnp.exp(scores - jnp.max(scores, axis=-1, keepdims=True))
             probs = expo / jnp.sum(expo, axis=-1, keepdims=True)
             probs_ref[h] = probs
-            attn = nn(probs.astype(bf16), value)
-            attn_ref[:, place] = attn.astype(bf16)
-            turned_ref[place, :] = attn.T.astype(bf16)
+            attn_ref[:, place] = nn(probs.astype(bf16), value).astype(bf16)
 
     return call(
         kernel,
@@ -270,7 +275,6 @@
         [
             whole_out((length, q_width)),
             whole_out((heads, length, length), f32),
-            whole_out((q_width, length)),
         ],
     )
 
@@ -517,16 +521,20 @@
 
 def out_terms(order, own, other, rows):
     _, length, width = own.shape
-    total = rows[0].shape[0]
-
-    def kernel(at_ref, own_ref, other_ref, *refs):
-        rows, (send_ref, keep_ref, acc) = refs[:4], refs[4:]
+    total = rows.shape[2]
+
+    def kernel(at_ref, own_ref, other_ref, rows_ref, send_ref, keep_ref, acc, turned_ref):
         step = pl.program_id(0)
 
+        @pl.when(step == 0)
+        def _():
+            for k in range(4):
+                turned_ref[k] = rows_ref[k].T
+
         def add(ref):
-            acc[...] = nn(rows[0][...], ref[0, 0])
+            acc[...] = nn(turned_ref[0], ref[0, 0])
             for k in range(1, 4):
-                acc[...] += nn(rows[k][...], ref[k, 0])
+                acc[...] += nn(turned_ref[k], ref[k, 0])
 
         pl.when(step % 2 == 0)(lambda: add(own_ref))
         pl.when(step % 2 == 1)(lambda: add(other_ref))
@@ -551,7 +559,7 @@
         kernel,
         "out_terms",
         order,
-        [(own.reshape(dims), block), (other.reshape(dims), block)] + [whole(a) for a in rows],
+        [(own.reshape(dims), block), (other.reshape(dims), block), whole(rows)],
         [
             (
                 shape((total, 2 * width)),
@@ -563,7 +571,7 @@
             ),
         ],
         grid=(4,),
-        scratch=[pltpu.VMEM((total, width), f32)],
+        scratch=[pltpu.VMEM((total, width), f32), pltpu.VMEM((4, total, length), bf16)],
     )
 
 
@@ -648,6 +656,18 @@
     return move(name, order, parts, [shape(dims)] * 2, plan)
 
 
+def stack_b(order, parts):
+    _, length, width = parts[0].shape
+
+    def plan(at_ref, ins, outs):
+        pairs = [(ref.at[pl.ds(0, 2)], outs[0].at[pl.ds(2 * k, 2)]) for k, ref in enumerate(ins)]
+        return pairs + [(ref.at[2], outs[1].at[k]) for k, ref in enumerate(ins)]
+
+    return move(
+        "stack_b", order, parts, [shape((8, length, width)), shape((4, length, width))], plan
+    )
+
+
 def rotary(length, head):
     freq = theta ** (-(np.arange(head // 2, dtype=np.float64) * 2.0 / head))
     angle = np.arange(length, dtype=np.float64)[:, None] * freq[None, :]
@@ -689,19 +709,20 @@
     other = partner(own, "tensor", 1)
     cot_near = y_near([cot_pair] * 4)
 
-    blocks = pick_tokens(order, own)
+    blocks = dict(zip((0, 1, 3), pick_tokens("pick_near", order, own, (0, 1, 3))))
     token_near = near(blocks)
     normed, inverse, own_tokens = norm(order, gain_row, own, other)
-    order.wait(*cot_near.values())
     rot, kv_own = project(order, normed, q_weight, kv_weight, tables)
-    cot_far = y_far([cot_pair] * 4)
+    blocks[2], cot_copy = pick_tokens("pick_far", order, own, (2,), cot_pair)
+    cot_far = y_far([cot_copy] * 4)
     kv_other = partner(kv_own, "tensor", 1)
-    order.wait(*token_near.values())
-    attn, probs, attn_turned = attend(order, rot, kv_own, kv_other)
     token_far = far(blocks)
+    order.wait(*token_near.values(), *cot_near.values())
+    attn, probs = attend(order, rot, kv_own, kv_other)
     send, keep = mix(order, attn, o_weight)
     arrived = partner(send, "tensor", 1)
 
+    order.wait(*token_far.values())
     (cot_own,) = stack("stack_cot", order, in_order({0: cot_pair}, cot_near, cot_far))
     cot_other = partner(cot_own, "tensor", 1)
 
@@ -710,10 +731,10 @@
             (ins[0].at[at_ref[CHIP] ^ (2 * (at_ref[Z] ^ k) + x)], outs[k].at[x])
             for k in range(4)
             for x in range(2)
-        ]
+        ] + [(ins[1], outs[k].at[2]) for k in range(4)]
 
     cot_blocks = move(
-        "pick_cot", order, [cot_own], [shape((2, length, width))] * 4, cot_plan
+        "pick_cot", order, [cot_own, attn], [shape((3, length, width))] * 4, cot_plan
     )
     b_near = near(cot_blocks)
     a_keep, a_send = split_x(
@@ -724,47 +745,44 @@
     out_near = y_near(out_parts)
 
     dattn, own_cot = out_gradient(order, cot_own, cot_other, o_weight)
-    order.wait(*b_near.values())
     dq, dkv_keep, send = attend_gradient(order, dattn, probs, rot, kv_own, kv_other, tables)
     b_far = far(cot_blocks)
     arrived = partner(send, "tensor", 1)
-    order.wait(*out_near.values())
+    order.wait(*b_near.values(), *out_near.values(), a_cross)
     dqkv, scaled = join_gradient(order, dq, dkv_keep, arrived, inverse, tables)
     scaled_other = partner(scaled, "dp", 1)
     out_far = y_far(out_parts)
-    attn_near = near([attn_turned] * 4)
-    order.wait(a_cross)
 
     send, keep, gain_part = norm_gradient(order, dqkv, q_weight, kv_weight, normed, gain_row)
     arrived = partner(send, "tensor", 1)
-    order.wait(*attn_near.values())
+    x_parts = pair_sum(order, keep, arrived, 4, Y)
+    x_near = y_near(x_parts)
+    gain_part = jnp.sum(lax.all_to_all(gain_part, "dp", 0, 0, tiled=True), axis=0)
+    order.wait(*b_far.values(), *out_far.values(), *x_near.values(), gain_part)
     (pair,) = stack("stack_dqkv", order, [scaled, scaled_other])
     dqkv_near = near([pair] * 4)
+    (b_own, attn_all) = stack_b(order, in_order({0: cot_blocks[0]}, b_near, b_far))
+    b_other = partner(b_own, "tensor", 1)
+    gain_part = lax.all_to_all(
+        jnp.broadcast_to(gain_part[None], (16, 1, 2 * width)), "tensor", 0, 0, tiled=True
+    )
+    gain_grad = jnp.sum(gain_part, axis=0)
+    x_far = y_far(x_parts)
+    order.wait(gain_grad)
     out_keep, out_send = ring_sum(order, in_order({0: out_parts[0]}, out_near, out_far))
     out_arrived = partner(out_send, "tensor", 2)
-    x_parts = pair_sum(order, keep, arrived, 4, Y)
-    x_near = y_near(x_parts)
-
-    gain_part = lax.all_to_all(gain_part, "dp", 0, 0, tiled=True)
-    gain_part = jnp.broadcast_to(jnp.sum(gain_part, axis=0)[None], (16, 1, 2 * width))
-    gain_grad = jnp.sum(lax.all_to_all(gain_part, "tensor", 0, 0, tiled=True), axis=0)
-    result = (own_tokens.astype(f32) + (out_keep + out_arrived.astype(f32))).astype(bf16)
-
-    attn_far = far([attn_turned] * 4)
-    (b_own,) = stack("stack_b", order, in_order({0: cot_blocks[0]}, b_near, b_far))
-    b_other = partner(b_own, "tensor", 1)
     a_other = [partner(a, "tensor", 1) for a in (a_keep, a_cross)]
     order.wait(*dqkv_near.values())
-    send, keep = out_terms(
-        order, b_own, b_other, in_order({0: attn_turned}, attn_near, attn_far)
-    )
+    send, keep = out_terms(order, b_own, b_other, attn_all)
     dqkv_far = far([pair] * 4)
     o_arrived = partner(send, "dp", 1)
-    x_far = y_far(x_parts)
+    result = (own_tokens.astype(f32) + (out_keep + out_arrived.astype(f32))).astype(bf16)
+
     x_keep, x_send = ring_sum(order, in_order({0: x_parts[0]}, x_near, x_far))
     x_arrived = partner(x_send, "tensor", 2)
     o_grad = keep + o_arrived.astype(f32)
 
+    order.wait(o_arrived)
     q_grad, kv_grad = q_gradient(
         order,
         [a_keep, a_cross],

time: 267 us -> 226 us (0.85)
  waiting for transfers between devices: 110 us -> 59.6 us
  starting transfers between devices: 63.3 us -> 46.5 us
  blocking collectives: 10.4 us -> 22.6 us
  local copies, waits for them, and re-layouts: 13.6 us -> 22.3 us
  Pallas kernels: 63.7 us -> 68.8 us
    ppermute x43 -> x40, waiting for transfers between devices: 106 us -> 59.6 us  [partner(): lax.ppermute(array, axis, [(i, i ^ bits) for i in range(lax.axis_size(axi...]
    all_to_all x1 -> x2, blocking collectives: 10.4 us -> 22.6 us  [the longest x1 11.3 us: on_device(): lax.all_to_all(gain_part, 'dp', 0, 0, tiled=True)]
    ppermute x43 -> x40, starting transfers between devices: 58.2 us -> 46.5 us  [partner(): lax.ppermute(array, axis, [(i, i ^ bits) for i in range(lax.axis_size(axi...]
    unnamed x74 -> x98, local copies, waits for them, and re-layouts: 11.8 us -> 20.4 us
    all_to_all x1 -> x0, starting transfers between devices: 5.15 us -> none  [on_device(): lax.all_to_all(gain_part, 'tensor', 0, 0, tiled=True)]
    pallas_call x22 -> x23, Pallas kernels: 63.7 us -> 68.8 us  [call(): pl.pallas_call(body, grid_spec=pltpu.PrefetchScalarGridSpec(num_scalar_pr...]
    all_to_all x1 -> x0, waiting for transfers between devices: 3.8 us -> none  [on_device(): lax.all_to_all(gain_part, 'tensor', 0, 0, tiled=True)]
  transfers between devices with their start and end apart: 44 -> 40, of which waited for: 21 -> 15; matrix products, arithmetic and copies ran while one was open for 2% -> 3% of each run, Pallas kernels for 21% -> 25%
where the time goes in v2:
time: 226 us; the launch traced here: 225 us
  Pallas kernels  68.8 us (30%)
  waiting for transfers between devices  59.6 us (26%)
  starting transfers between devices  46.5 us (21%)
  blocking collectives  22.6 us (10%)
  local copies, waits for them, and re-layouts  22.3 us (10%)
  other arithmetic  3.76 us (2%)
    pallas_call x23, Pallas kernels, call(): pl.pallas_call(body, grid_spec=pltpu.PrefetchScalarGridSpec(num_scalar_pr...  68.8 us
    ppermute x40, waiting for transfers between devices, partner(): lax.ppermute(array, axis, [(i, i ^ bits) for i in range(lax.axis_size(axi...  59.6 us
    ppermute x40, starting transfers between devices, partner(): lax.ppermute(array, axis, [(i, i ^ bits) for i in range(lax.axis_size(axi...  46.5 us
    unnamed x98, local copies, waits for them, and re-layouts  20.4 us
    all_to_all x1, blocking collectives, on_device(): lax.all_to_all(gain_part, 'dp', 0, 0, tiled=True)  11.3 us
    all_to_all x1, blocking collectives, on_device(): lax.all_to_all(jnp.broadcast_to(gain_part[None], (16, 1, 2 * width)), 'te...  11.2 us
  transfers between devices with their start and end apart: 40, of which 15 were waited for; matrix products, arithmetic and copies ran while one was open for 3% of the time, Pallas kernels for 25%

profile of v2, /device:TPU:6, one launch (start us, length us, event | category | flops | bytes accessed | tf_op | source)
XLA Modules:
  0.0 224.6 jit_solution(8585557197012265865)
XLA Ops:
  2.1 1.6 collective-permute-start.1
  3.7 2.9 %collective-permute-start.3 = (bf16[256,512]{1,0:T(8,128)(2,1)}, bf16[256,512]{1,0:T(8,128)(2,1)S(1)}, u32[]{:S(2)}, u32[]{:S(2)}) collective-permute-start(bf16[256,512]{1,0:T(8,128)(2,1)} %bitcast.36), channel_id=1, source_target_pairs={{0,8},{1,9},{2,10},{3,11},{4,12},{5,13},{6,14},{7,15},{8,0},{9,1},... | collective-permute-start | bytes 786440 | tf_op jit(solution)/shard_map/ppermute | solution.py:19
  6.8 2.1 collective-permute-start.7
  8.9 2.0 collective-permute-done
  11.0 2.2 collective-permute-start.2
  13.2 2.3 %collective-permute-start.4 = (bf16[256,512]{1,0:T(8,128)(2,1)S(1)}, bf16[256,512]{1,0:T(8,128)(2,1)S(1)}, u32[]{:S(2)}, u32[]{:S(2)}) collective-permute-start(bf16[256,512]{1,0:T(8,128)(2,1)S(1)} %collective-permute-done), channel_id=1, source_target_pairs={{0,8},{1,9},{2,10},{3,11},{4,12},{5,13},{6,14},{7,15},{8,0},{9,1},... | collective-permute-start | bytes 786440 | tf_op jit(solution)/shard_map/ppermute | solution.py:19
  15.5 4.2 %collective-permute-done.3 = bf16[256,512]{1,0:T(8,128)(2,1)S(1)} collective-permute-done((bf16[256,512]{1,0:T(8,128)(2,1)}, bf16[256,512]{1,0:T(8,128)(2,1)S(1)}, u32[]{:S(2)}, u32[]{:S(2)}) %collective-permute-start.3) | collective-permute-done | bytes 262176 | tf_op jit(solution)/shard_map/ppermute | solution.py:19
  21.0 1.9 collective-permute-done.2
  22.8 6.7 %collective-permute-done.4 = bf16[256,512]{1,0:T(8,128)(2,1)S(1)} collective-permute-done((bf16[256,512]{1,0:T(8,128)(2,1)S(1)}, bf16[256,512]{1,0:T(8,128)(2,1)S(1)}, u32[]{:S(2)}, u32[]{:S(2)}) %collective-permute-start.4) | collective-permute-done | bytes 262176 | tf_op jit(solution)/shard_map/ppermute | solution.py:19
  29.5 2.5 %collective-permute-done.6 = bf16[256,512]{1,0:T(8,128)(2,1)S(1)} collective-permute-done((bf16[256,512]{1,0:T(8,128)(2,1)S(1)}, bf16[256,512]{1,0:T(8,128)(2,1)S(1)}, u32[]{:S(2)}, u32[]{:S(2)}) %collective-permute-start.6) | collective-permute-done | bytes 262176 | tf_op jit(solution)/shard_map/ppermute | solution.py:19
  36.3 2.0 collective-permute-start.10
  38.3 2.5 %collective-permute-start.11 = (bf16[2,512,256]{2,1,0:T(8,128)(2,1)S(1)}, bf16[2,512,256]{2,1,0:T(8,128)(2,1)S(1)}, u32[]{:S(2)}, u32[]{:S(2)}) collective-permute-start(bf16[2,512,256]{2,1,0:T(8,128)(2,1)S(1)} %get-tuple-element.65), channel_id=1, source_target_pairs={{0,96},{16,112},{32,64},{48,80},{64,32},{80,48},{96,0},{112,16},{1... | collective-permute-start | bytes 1572872 | tf_op jit(solution)/shard_map/ppermute | solution.py:19
  41.3 3.7 %norm.1 = (bf16[256,8192]{1,0:T(8,128)(2,1)S(1)}, f32[256,1]{1,0:T(8,128)S(1)}, bf16[16,8192]{1,0:T(8,128)(2,1)S(1)}) custom-call(s32[7]{0:T(128)S(1)} %stack.31.at_ref, f32[1,8192]{1,0:T(1,128)S(1)} %bitcast.31, bf16[8,256,512]{2,1,0:T(8,128)(2,1)S(1)} %get-tuple-element.56.refs_0_.refs_1_, bf16[8,256,512]{2,1,0:T(8,128)(2,1)S(1)} %collective-permute-done.8.refs_2_, ...), custom_call_target="tpu_custom_call" | custom-call | flops 1 | bytes 1 | tf_op jit(solution)/shard_map/norm/pallas_call | solution.py:38
  45.8 1.7 copy-done.1
  47.5 5.9 %project.1 = (bf16[256,512]{1,0:T(8,128)(2,1)S(1)}, bf16[256,128]{1,0:T(8,128)(2,1)S(1)}) custom-call(s32[7]{0:T(128)S(1)} %stack.31.at_ref, bf16[256,8192]{1,0:T(8,128)(2,1)S(1)} %get-tuple-element.59.refs_0_.refs_3_, bf16[8192,512]{1,0:T(8,128)(2,1)S(1)} %copy-done, bf16[8192,128]{1,0:T(8,128)(2,1)S(1)} %copy-done.1, f32[256,128]{1,0:T(8,128)S(1)} %copy-done.30, ...), custom_call_target="tpu_custom_call" | custom-call | flops 1 | bytes 1 | tf_op jit(solution)/shard_map/project/pallas_call | solution.py:38
  54.2 2.1 collective-permute-start.15
  56.3 2.8 %collective-permute-start.16 = (bf16[2,256,512]{2,1,0:T(8,128)(2,1)S(1)}, bf16[2,256,512]{2,1,0:T(8,128)(2,1)S(1)}, u32[]{:S(2)}, u32[]{:S(2)}) collective-permute-start(bf16[2,256,512]{2,1,0:T(8,128)(2,1)S(1)} %get-tuple-element.69), channel_id=1, source_target_pairs={{0,8},{1,9},{2,10},{3,11},{4,12},{5,13},{6,14},{7,15},{8,0},{9,1},... | collective-permute-start | bytes 1572872 | tf_op jit(solution)/shard_map/ppermute | solution.py:19
  60.3 1.7 attend.1
  62.0 5.5 %mix.1 = (bf16[8,16,8192]{2,1,0:T(8,128)(2,1)S(1)}, bf16[8,16,8192]{2,1,0:T(8,128)(2,1)S(1)}) custom-call(s32[7]{0:T(128)S(1)} %stack.31.at_ref, bf16[256,512]{1,0:T(8,128)(2,1)S(1)} %get-tuple-element.66.refs_0_.refs_1_, bf16[512,8192]{1,0:T(8,128)(2,1)S(1)} %bitcast.29), custom_call_target="tpu_custom_call" | custom-call | flops 1 | bytes 1 | tf_op jit(solution)/shard_map/mix/pallas_call | solution.py:38
  67.7 1.5 collective-permute-done.15.refs_5_.refs_2_
  69.3 2.2 collective-permute-done.16.refs_2_
  72.7 2.1 pick_cot.1
  77.9 2.5 %pair_sum.2 = (bf16[2,16,8192]{2,1,0:T(8,128)(2,1)S(1)}, bf16[2,16,8192]{2,1,0:T(8,128)(2,1)S(1)}, bf16[2,16,8192]{2,1,0:T(8,128)(2,1)}, bf16[2,16,8192]{2,1,0:T(8,128)(2,1)S(1)}) custom-call(s32[7]{0:T(128)S(1)} %stack.31.at_ref, bf16[8,16,8192]{2,1,0:T(8,128)(2,1)S(1)} %get-tuple-element.67.refs_0_, ...), custom_call_target="tpu_custom_call" | custom-call | flops 1 | bytes 1 | tf_op jit(solution)/shard_map/pair_sum/pallas_call | solution.py:38
  81.9 2.3 %collective-permute-start.19 = (bf16[2,16,8192]{2,1,0:T(8,128)(2,1)S(1)}, bf16[2,16,8192]{2,1,0:T(8,128)(2,1)S(1)}, u32[]{:S(2)}, u32[]{:S(2)}) collective-permute-start(bf16[2,16,8192]{2,1,0:T(8,128)(2,1)S(1)} %get-tuple-element.75), channel_id=1, source_target_pairs={{0,12},{1,13},{2,14},{3,15},{4,8},{5,9},{6,10},{7,11},{8,4},{9,5},... | collective-permute-start | bytes 1572872 | tf_op jit(solution)/shard_map/ppermute | solution.py:19
  84.2 5.2 %out_gradient.1 = (bf16[256,512]{1,0:T(8,128)(2,1)S(1)}, bf16[16,8192]{1,0:T(8,128)(2,1)S(1)}) custom-call(s32[7]{0:T(128)S(1)} %stack.31.at_ref, bf16[8,256,512]{2,1,0:T(8,128)(2,1)S(1)} %stack_cot.1.refs_0_, bf16[8,256,512]{2,1,0:T(8,128)(2,1)S(1)} %collective-permute-done.23.refs_1_, bf16[512,8192]{1,0:T(8,128)(2,1)S(1)} %bitcast.29, ...), custom_call_target="tpu_custom_call" | custom-call | flops 1 | bytes 1 | tf_op jit(solution)/shard_map/out_gradient/pallas_call | solution.py:38
  89.4 2.3 %attend_gradient.1 = (bf16[256,512]{1,0:T(8,128)(2,1)S(1)}, f32[256,128]{1,0:T(8,128)S(1)}, bf16[256,128]{1,0:T(8,128)(2,1)S(1)}) custom-call(s32[7]{0:T(128)S(1)} %stack.31.at_ref, bf16[256,512]{1,0:T(8,128)(2,1)S(1)} %get-tuple-element.79.refs_0_, f32[4,256,256]{2,1,0:T(8,128)S(1)} %get-tuple-element.80.refs_1_, ...), custom_call_target="tpu_custom_call" | custom-call | flops 1 | bytes 1 | tf_op jit(solution)/shard_map/attend_gradient/pallas_call | solution.py:38
  91.7 4.3 %collective-permute-done.20.refs_6_.refs_1_ = bf16[3,256,512]{2,1,0:T(8,128)(2,1)S(1)} collective-permute-done((bf16[3,256,512]{2,1,0:T(8,128)(2,1)S(1)}, bf16[3,256,512]{2,1,0:T(8,128)(2,1)S(1)}, u32[]{:S(2)}, u32[]{:S(2)}) %collective-permute-start.20) | collective-permute-done | bytes 786464 | tf_op jit(solution)/shard_map/ppermute | solution.py:19
  96.0 1.9 collective-permute-done.22.refs_7_.refs_3_
  98.0 3.6 %collective-permute-done.25.refs_10_.refs_1_ = bf16[4,512,256]{2,1,0:T(8,128)(2,1)S(1)} collective-permute-done((bf16[4,512,256]{2,1,0:T(8,128)(2,1)S(1)}, bf16[4,512,256]{2,1,0:T(8,128)(2,1)S(1)}, u32[]{:S(2)}, u32[]{:S(2)}) %collective-permute-start.25) | collective-permute-done | bytes 1048608 | tf_op jit(solution)/shard_map/ppermute | solution.py:19
  104.0 6.3 %norm_gradient.1 = (bf16[8,16,8192]{2,1,0:T(8,128)(2,1)S(1)}, bf16[8,16,8192]{2,1,0:T(8,128)(2,1)S(1)}, f32[8,1,1024]{2,1,0:T(1,128)S(1)}) custom-call(s32[7]{0:T(128)S(1)} %stack.31.at_ref, bf16[256,640]{1,0:T(8,128)(2,1)S(1)} %get-tuple-element.87.refs_0_, bf16[8192,512]{1,0:T(8,128)(2,1)S(1)} %copy-done, bf16[8192,128]{1,0:T(8,128)(2,1)S(1)} %copy-done.2, ...), custom_call_target="tpu_custom_call" | custom-call | flops 1 | bytes 1 | tf_op jit(solution)/shard_map/norm_gradient/pallas_call | solution.py:38
  111.7 3.2 %collective-permute-start.18 = (bf16[2,16,8192]{2,1,0:T(8,128)(2,1)}, bf16[2,16,8192]{2,1,0:T(8,128)(2,1)S(1)}, u32[]{:S(2)}, u32[]{:S(2)}) collective-permute-start(bf16[2,16,8192]{2,1,0:T(8,128)(2,1)} %get-tuple-element.74), channel_id=1, source_target_pairs={{0,8},{1,9},{2,10},{3,11},{4,12},{5,13},{6,14},{7,15},{8,0},{9,1},... | collective-permute-start | bytes 1572872 | tf_op jit(solution)/shard_map/ppermute | solution.py:19
  114.9 2.6 %pair_sum.3 = (bf16[2,16,8192]{2,1,0:T(8,128)(2,1)S(1)}, bf16[2,16,8192]{2,1,0:T(8,128)(2,1)}, bf16[2,16,8192]{2,1,0:T(8,128)(2,1)S(1)}, bf16[2,16,8192]{2,1,0:T(8,128)(2,1)}) custom-call(s32[7]{0:T(128)S(1)} %stack.31.at_ref, bf16[8,16,8192]{2,1,0:T(8,128)(2,1)S(1)} %get-tuple-element.88.refs_0_, bf16[8,16,8192]{2,1,0:T(8,128)(2,1)S(1)} %collective-permute-done.27.refs_1_, ...), custom_call_target="tpu_custom_call" | custom-call | flops 1 | bytes 1 | tf_op jit(solution)/shard_map/pair_sum/pallas_call | solution.py:38
  118.7 2.1 collective-permute-start.29
  121.1 11.3 %all_to_all.10 = f32[8,1,1024]{2,1,0:T(1,128)S(1)} all-to-all(f32[8,1,1024]{2,1,0:T(1,128)S(1)} %get-tuple-element.93), channel_id=1, replica_groups=mesh['dp'=8,'tensor'=16] {'dp'}, dimensions={0} | all-to-all | bytes 65536 | tf_op jit(solution)/shard_map/all_to_all | solution.py:760
  132.5 6.3 %collective-permute-done.28.refs_5_.refs_1_ = bf16[2,16,8192]{2,1,0:T(8,128)(2,1)S(1)} collective-permute-done((bf16[2,16,8192]{2,1,0:T(8,128)(2,1)}, bf16[2,16,8192]{2,1,0:T(8,128)(2,1)S(1)}, u32[]{:S(2)}, u32[]{:S(2)}) %collective-permute-start.28) | collective-permute-done | bytes 524320 | tf_op jit(solution)/shard_map/ppermute | solution.py:19
  140.7 2.1 stack_dqkv.1.refs_4_
  150.7 11.2 %all_to_all.11 = f32[16,1,1024]{2,1,0:T(1,128)S(1)} all-to-all(f32[16,1,1024]{2,1,0:T(1,128)S(1)} %broadcast_in_dim.59), channel_id=1, replica_groups=mesh['dp'=8,'tensor'=16] {'tensor'}, dimensions={0} | all-to-all | bytes 131072 | tf_op jit(solution)/shard_map/all_to_all | solution.py:766
  166.2 2.2 ring_sum.2
  169.1 2.9 %collective-permute-start.30 = (bf16[16,8192]{1,0:T(8,128)(2,1)}, bf16[16,8192]{1,0:T(8,128)(2,1)}, u32[]{:S(2)}, u32[]{:S(2)}) collective-permute-start(bf16[16,8192]{1,0:T(8,128)(2,1)} %get-tuple-element.96), channel_id=1, source_target_pairs={{0,2},{1,3},{2,0},{3,1},{4,6},{5,7},{6,4},{7,5},{8,10},{9,11},{10,... | collective-permute-start | bytes 786440 | tf_op jit(solution)/shard_map/ppermute | solution.py:19
  175.5 2.2 collective-permute-start.38
  179.9 6.2 %out_terms.1 = (bf16[512,1024]{1,0:T(8,128)(2,1)S(1)}, f32[512,1024]{1,0:T(8,128)S(1)}) custom-call(s32[7]{0:T(128)S(1)} %stack.31.at_ref, bf16[4,2,256,512]{3,2,1,0:T(8,128)(2,1)S(1)} %bitcast.30, bf16[4,2,256,512]{3,2,1,0:T(8,128)(2,1)} %bitcast.24.refs_1_, bf16[4,256,512]{2,1,0:T(8,128)(2,1)S(1)} %copy-done.33, f32[16,8192]{1,0:T(8,128)S(1)} %copy-done.14, ...), custom_call_target="tpu_custom_call" | custom-call | flops 1 | bytes 1 | tf_op jit(solution)/shard_map/out_terms/pallas_call | solution.py:38
  186.5 1.9 fusion
  188.4 1.5 collective-permute-done.31.refs_2_
  189.9 2.7 %ring_sum.3 = (f32[16,8192]{1,0:T(8,128)S(1)}, bf16[16,8192]{1,0:T(8,128)(2,1)S(1)}) custom-call(s32[7]{0:T(128)S(1)} %stack.31.at_ref, bf16[2,16,8192]{2,1,0:T(8,128)(2,1)S(1)} %copy-done.26, bf16[2,16,8192]{2,1,0:T(8,128)(2,1)S(1)} %copy-done.29, bf16[2,16,8192]{2,1,0:T(8,128)(2,1)S(1)} %collective-permute-done.31.refs_2_, ...), custom_call_target="tpu_custom_call" | custom-call | flops 1 | bytes 1 | tf_op jit(solution)/shard_map/ring_sum/pallas_call | solution.py:38
  193.6 18.6 %collective-permute-done.39.refs_10_ = bf16[512,1024]{1,0:T(8,128)(2,1)S(1)} collective-permute-done((bf16[512,1024]{1,0:T(8,128)(2,1)S(1)}, bf16[512,1024]{1,0:T(8,128)(2,1)S(1)}, u32[]{:S(2)}, u32[]{:S(2)}) %collective-permute-start.39) | collective-permute-done | bytes 1048608 | tf_op jit(solution)/shard_map/ppermute | solution.py:19
  212.3 8.5 %q_gradient.1 = (f32[1024,512]{1,0:T(8,128)}, f32[1024,128]{1,0:T(8,128)}) custom-call(s32[7]{0:T(128)S(1)} %stack.31.at_ref, bf16[4,512,256]{2,1,0:T(8,128)(2,1)S(1)} %copy-done.6, bf16[4,512,256]{2,1,0:T(8,128)(2,1)S(1)} %copy-done.4, bf16[4,512,256]{2,1,0:T(8,128)(2,1)S(1)} %collective-permute-done.36.refs_2_, ...), custom_call_target="tpu_custom_call" | custom-call | flops 1 | bytes 1 | tf_op jit(solution)/shard_map/q_gradient/pallas_call | solution.py:38
  220.8 1.8 convert_add_fusion
  223.1 1.5 input_gradient.1
  (165 shorter events, 44.1 us)
Async XLA Ops:
  0.6 10.3 %collective-permute-start = (bf16[256,512]{1,0:T(8,128)(2,1)}, bf16[256,512]{1,0:T(8,128)(2,1)S(1)}, u32[]{:S(2)}, u32[]{:S(2)}) collective-permute-start(bf16[256,512]{1,0:T(8,128)(2,1)} %bitcast.34), channel_id=1, source_target_pairs={{0,2},{1,3},{2,0},{3,1},{4,6},{5,7},{6,4},{7,5},{8,10},{9,11},{10,... | collective-permute-start | bytes 786440 | tf_op jit(solution)/shard_map/ppermute | solution.py:19
  2.1 11.1 %collective-permute-start.1 = (bf16[256,512]{1,0:T(8,128)(2,1)}, bf16[256,512]{1,0:T(8,128)(2,1)S(1)}, u32[]{:S(2)}, u32[]{:S(2)}) collective-permute-start(bf16[256,512]{1,0:T(8,128)(2,1)} %bitcast.35), channel_id=1, source_target_pairs={{0,4},{1,5},{2,6},{3,7},{4,0},{5,1},{6,2},{7,3},{8,12},{9,13},{10,... | collective-permute-start | bytes 786440 | tf_op jit(solution)/shard_map/ppermute | solution.py:19
  3.7 16.0 %collective-permute-start.3 = (bf16[256,512]{1,0:T(8,128)(2,1)}, bf16[256,512]{1,0:T(8,128)(2,1)S(1)}, u32[]{:S(2)}, u32[]{:S(2)}) collective-permute-start(bf16[256,512]{1,0:T(8,128)(2,1)} %bitcast.36), channel_id=1, source_target_pairs={{0,8},{1,9},{2,10},{3,11},{4,12},{5,13},{6,14},{7,15},{8,0},{9,1},... | collective-permute-start | bytes 786440 | tf_op jit(solution)/shard_map/ppermute | solution.py:19
  6.6 14.4 %collective-permute-start.5 = (bf16[256,512]{1,0:T(8,128)(2,1)}, bf16[256,512]{1,0:T(8,128)(2,1)S(1)}, u32[]{:S(2)}, u32[]{:S(2)}) collective-permute-start(bf16[256,512]{1,0:T(8,128)(2,1)} %bitcast.37), channel_id=1, source_target_pairs={{0,12},{1,13},{2,14},{3,15},{4,8},{5,9},{6,10},{7,11},{8,4},{9,5},... | collective-permute-start | bytes 786440 | tf_op jit(solution)/shard_map/ppermute | solution.py:19
  6.8 14.1 %collective-permute-start.7 = (bf16[256,512]{1,0:T(8,128)(2,1)}, bf16[256,512]{1,0:T(8,128)(2,1)S(1)}, u32[]{:S(2)}, u32[]{:S(2)}) collective-permute-start(bf16[256,512]{1,0:T(8,128)(2,1)} %bitcast.38), channel_id=1, source_target_pairs={{0,2},{1,3},{2,0},{3,1},{4,6},{5,7},{6,4},{7,5},{8,10},{9,11},{10,... | collective-permute-start | bytes 786440 | tf_op jit(solution)/shard_map/ppermute | solution.py:19
  11.0 11.9 %collective-permute-start.2 = (bf16[256,512]{1,0:T(8,128)(2,1)S(1)}, bf16[256,512]{1,0:T(8,128)(2,1)S(1)}, u32[]{:S(2)}, u32[]{:S(2)}) collective-permute-start(bf16[256,512]{1,0:T(8,128)(2,1)S(1)} %collective-permute-done), channel_id=1, source_target_pairs={{0,4},{1,5},{2,6},{3,7},{4,0},{5,1},{6,2},{7,3},{8,12},{9,13},{10,... | collective-permute-start | bytes 786440 | tf_op jit(solution)/shard_map/ppermute | solution.py:19
  13.2 16.3 %collective-permute-start.4 = (bf16[256,512]{1,0:T(8,128)(2,1)S(1)}, bf16[256,512]{1,0:T(8,128)(2,1)S(1)}, u32[]{:S(2)}, u32[]{:S(2)}) collective-permute-start(bf16[256,512]{1,0:T(8,128)(2,1)S(1)} %collective-permute-done), channel_id=1, source_target_pairs={{0,8},{1,9},{2,10},{3,11},{4,12},{5,13},{6,14},{7,15},{8,0},{9,1},... | collective-permute-start | bytes 786440 | tf_op jit(solution)/shard_map/ppermute | solution.py:19
  19.7 12.4 %collective-permute-start.6 = (bf16[256,512]{1,0:T(8,128)(2,1)S(1)}, bf16[256,512]{1,0:T(8,128)(2,1)S(1)}, u32[]{:S(2)}, u32[]{:S(2)}) collective-permute-start(bf16[256,512]{1,0:T(8,128)(2,1)S(1)} %collective-permute-done), channel_id=1, source_target_pairs={{0,12},{1,13},{2,14},{3,15},{4,8},{5,9},{6,10},{7,11},{8,4},{9,5},... | collective-permute-start | bytes 786440 | tf_op jit(solution)/shard_map/ppermute | solution.py:19
  19.9 20.9 %copy-start.46 = (bf16[8192]{0:T(1024)(128)(2,1)S(1)}, bf16[8192]{0:T(1024)(128)(2,1)}, u32[]{:S(2)}) copy-start(bf16[8192]{0:T(1024)(128)(2,1)} %param.9) | copy-start | bytes 49156
  35.2 6.1 %collective-permute-start.8 = (bf16[8,256,512]{2,1,0:T(8,128)(2,1)S(1)}, bf16[8,256,512]{2,1,0:T(8,128)(2,1)S(1)}, u32[]{:S(2)}, u32[]{:S(2)}) collective-permute-start(bf16[8,256,512]{2,1,0:T(8,128)(2,1)S(1)} %get-tuple-element.56.refs_0_.refs_1_), channel_id=1, source_target_pairs={{0,1},{1,0},{2,3},{3,2},{4,5},{5,4},{6,7},{7,6},{8,9},{9,8},{10,11... | collective-permute-start | bytes 6291464 | tf_op jit(solution)/shard_map/ppermute | solution.py:19
  36.3 20.0 %collective-permute-start.10 = (bf16[2,512,256]{2,1,0:T(8,128)(2,1)S(1)}, bf16[2,512,256]{2,1,0:T(8,128)(2,1)S(1)}, u32[]{:S(2)}, u32[]{:S(2)}) collective-permute-start(bf16[2,512,256]{2,1,0:T(8,128)(2,1)S(1)} %get-tuple-element.64), channel_id=1, source_target_pairs={{0,32},{16,48},{32,0},{48,16},{64,96},{80,112},{96,64},{112,80},{1... | collective-permute-start | bytes 1572872 | tf_op jit(solution)/shard_map/ppermute | solution.py:19
  38.3 20.7 %collective-permute-start.11 = (bf16[2,512,256]{2,1,0:T(8,128)(2,1)S(1)}, bf16[2,512,256]{2,1,0:T(8,128)(2,1)S(1)}, u32[]{:S(2)}, u32[]{:S(2)}) collective-permute-start(bf16[2,512,256]{2,1,0:T(8,128)(2,1)S(1)} %get-tuple-element.65), channel_id=1, source_target_pairs={{0,96},{16,112},{32,64},{48,80},{64,32},{80,48},{96,0},{112,16},{1... | collective-permute-start | bytes 1572872 | tf_op jit(solution)/shard_map/ppermute | solution.py:19
  40.8 62.3 %copy-start.36 = (f32[8192]{0:T(1024)}, f32[8192]{0:T(1024)S(1)}, u32[]{:S(2)}) copy-start(f32[8192]{0:T(1024)S(1)} %convert_element_type.15) | copy-start | bytes 98308
  40.8 18.2 %collective-permute-start.12 = (bf16[2,256,512]{2,1,0:T(8,128)(2,1)S(1)}, bf16[2,256,512]{2,1,0:T(8,128)(2,1)S(1)}, u32[]{:S(2)}, u32[]{:S(2)}) collective-permute-start(bf16[2,256,512]{2,1,0:T(8,128)(2,1)S(1)} %get-tuple-element.62.refs_1_.refs_0_), channel_id=1, source_target_pairs={{0,4},{1,5},{2,6},{3,7},{4,0},{5,1},{6,2},{7,3},{8,12},{9,13},{10,... | collective-permute-start | bytes 1572872 | tf_op jit(solution)/shard_map/ppermute | solution.py:19
  40.9 18.1 %collective-permute-start.13 = (bf16[2,256,512]{2,1,0:T(8,128)(2,1)S(1)}, bf16[2,256,512]{2,1,0:T(8,128)(2,1)S(1)}, u32[]{:S(2)}, u32[]{:S(2)}) collective-permute-start(bf16[2,256,512]{2,1,0:T(8,128)(2,1)S(1)} %get-tuple-element.62.refs_1_.refs_0_), channel_id=1, source_target_pairs={{0,12},{1,13},{2,14},{3,15},{4,8},{5,9},{6,10},{7,11},{8,4},{9,5},... | collective-permute-start | bytes 1572872 | tf_op jit(solution)/shard_map/ppermute | solution.py:19
  45.8 55.8 %copy-start.38 = (f32[256,1]{1,0:T(8,128)}, f32[256,1]{1,0:T(8,128)S(1)}, u32[]{:S(2)}) copy-start(f32[256,1]{1,0:T(8,128)S(1)} %get-tuple-element.84.refs_3_) | copy-start | bytes 3076
  45.8 16.2 %slice-start = ((s8[8388608]{0:T(1024)(128)(4,1)}), s8[4194304]{0:T(1024)(128)(4,1)S(1)}, s32[]{:S(2)}) async-start(s8[8388608]{0:T(1024)(128)(4,1)} %bitcast.28), calls=%async_computation.2 | async-start | bytes 8388608
  47.5 14.4 %slice-start.1 = ((s8[8388608]{0:T(1024)(128)(4,1)}), s8[4194304]{0:T(1024)(128)(4,1)S(1)}, s32[]{:S(2)}) async-start(s8[8388608]{0:T(1024)(128)(4,1)} %bitcast.28), calls=%async_computation.3 | async-start | bytes 8388608
  54.2 15.1 %collective-permute-start.15 = (bf16[2,512,256]{2,1,0:T(8,128)(2,1)S(1)}, bf16[2,512,256]{2,1,0:T(8,128)(2,1)S(1)}, u32[]{:S(2)}, u32[]{:S(2)}) collective-permute-start(bf16[2,512,256]{2,1,0:T(8,128)(2,1)S(1)} %get-tuple-element.63.refs_3_), channel_id=1, source_target_pairs={{0,64},{16,80},{32,96},{48,112},{64,0},{80,16},{96,32},{112,48},{1... | collective-permute-start | bytes 1572872 | tf_op jit(solution)/shard_map/ppermute | solution.py:19
  56.3 15.2 %collective-permute-start.16 = (bf16[2,256,512]{2,1,0:T(8,128)(2,1)S(1)}, bf16[2,256,512]{2,1,0:T(8,128)(2,1)S(1)}, u32[]{:S(2)}, u32[]{:S(2)}) collective-permute-start(bf16[2,256,512]{2,1,0:T(8,128)(2,1)S(1)} %get-tuple-element.69), channel_id=1, source_target_pairs={{0,8},{1,9},{2,10},{3,11},{4,12},{5,13},{6,14},{7,15},{8,0},{9,1},... | collective-permute-start | bytes 1572872 | tf_op jit(solution)/shard_map/ppermute | solution.py:19
  59.0 1.3 collective-permute-start.9
  67.5 10.4 %collective-permute-start.14 = (bf16[8,16,8192]{2,1,0:T(8,128)(2,1)S(1)}, bf16[8,16,8192]{2,1,0:T(8,128)(2,1)S(1)}, u32[]{:S(2)}, u32[]{:S(2)}) collective-permute-start(bf16[8,16,8192]{2,1,0:T(8,128)(2,1)S(1)} %get-tuple-element.68.refs_4_), channel_id=1, source_target_pairs={{0,1},{1,0},{2,3},{3,2},{4,5},{5,4},{6,7},{7,6},{8,9},{9,8},{10,11... | collective-permute-start | bytes 6291464 | tf_op jit(solution)/shard_map/ppermute | solution.py:19
  72.6 9.3 %collective-permute-start.23 = (bf16[8,256,512]{2,1,0:T(8,128)(2,1)S(1)}, bf16[8,256,512]{2,1,0:T(8,128)(2,1)S(1)}, u32[]{:S(2)}, u32[]{:S(2)}) collective-permute-start(bf16[8,256,512]{2,1,0:T(8,128)(2,1)S(1)} %stack_cot.1.refs_0_), channel_id=1, source_target_pairs={{0,1},{1,0},{2,3},{3,2},{4,5},{5,4},{6,7},{7,6},{8,9},{9,8},{10,11... | collective-permute-start | bytes 6291464 | tf_op jit(solution)/shard_map/ppermute | solution.py:19
  75.9 25.6 %collective-permute-start.25 = (bf16[4,512,256]{2,1,0:T(8,128)(2,1)S(1)}, bf16[4,512,256]{2,1,0:T(8,128)(2,1)S(1)}, u32[]{:S(2)}, u32[]{:S(2)}) collective-permute-start(bf16[4,512,256]{2,1,0:T(8,128)(2,1)S(1)} %get-tuple-element.85), channel_id=1, source_target_pairs={{0,16},{16,0},{32,48},{48,32},{64,80},{80,64},{96,112},{112,96},{1... | collective-permute-start | bytes 3145736 | tf_op jit(solution)/shard_map/ppermute | solution.py:19
  76.0 20.0 %collective-permute-start.20 = (bf16[3,256,512]{2,1,0:T(8,128)(2,1)S(1)}, bf16[3,256,512]{2,1,0:T(8,128)(2,1)S(1)}, u32[]{:S(2)}, u32[]{:S(2)}) collective-permute-start(bf16[3,256,512]{2,1,0:T(8,128)(2,1)S(1)} %get-tuple-element.76), channel_id=1, source_target_pairs={{0,32},{16,48},{32,0},{48,16},{64,96},{80,112},{96,64},{112,80},{1... | collective-permute-start | bytes 2359304 | tf_op jit(solution)/shard_map/ppermute | solution.py:19
  77.1 20.9 %collective-permute-start.22 = (bf16[3,256,512]{2,1,0:T(8,128)(2,1)S(1)}, bf16[3,256,512]{2,1,0:T(8,128)(2,1)S(1)}, u32[]{:S(2)}, u32[]{:S(2)}) collective-permute-start(bf16[3,256,512]{2,1,0:T(8,128)(2,1)S(1)} %get-tuple-element.78), channel_id=1, source_target_pairs={{0,96},{16,112},{32,64},{48,80},{64,32},{80,48},{96,0},{112,16},{1... | collective-permute-start | bytes 2359304 | tf_op jit(solution)/shard_map/ppermute | solution.py:19
  80.4 21.1 %collective-permute-start.17 = (bf16[2,16,8192]{2,1,0:T(8,128)(2,1)S(1)}, bf16[2,16,8192]{2,1,0:T(8,128)(2,1)S(1)}, u32[]{:S(2)}, u32[]{:S(2)}) collective-permute-start(bf16[2,16,8192]{2,1,0:T(8,128)(2,1)S(1)} %get-tuple-element.73), channel_id=1, source_target_pairs={{0,4},{1,5},{2,6},{3,7},{4,0},{5,1},{6,2},{7,3},{8,12},{9,13},{10,... | collective-permute-start | bytes 1572872 | tf_op jit(solution)/shard_map/ppermute | solution.py:19
  81.9 19.7 %collective-permute-start.19 = (bf16[2,16,8192]{2,1,0:T(8,128)(2,1)S(1)}, bf16[2,16,8192]{2,1,0:T(8,128)(2,1)S(1)}, u32[]{:S(2)}, u32[]{:S(2)}) collective-permute-start(bf16[2,16,8192]{2,1,0:T(8,128)(2,1)S(1)} %get-tuple-element.75), channel_id=1, source_target_pairs={{0,12},{1,13},{2,14},{3,15},{4,8},{5,9},{6,10},{7,11},{8,4},{9,5},... | collective-permute-start | bytes 1572872 | tf_op jit(solution)/shard_map/ppermute | solution.py:19
  96.0 5.6 %collective-permute-start.24 = (bf16[256,128]{1,0:T(8,128)(2,1)S(1)}, bf16[256,128]{1,0:T(8,128)(2,1)S(1)}, u32[]{:S(2)}, u32[]{:S(2)}) collective-permute-start(bf16[256,128]{1,0:T(8,128)(2,1)S(1)} %get-tuple-element.83), channel_id=1, source_target_pairs={{0,1},{1,0},{2,3},{3,2},{4,5},{5,4},{6,7},{7,6},{8,9},{9,8},{10,11... | collective-permute-start | bytes 196616 | tf_op jit(solution)/shard_map/ppermute | solution.py:19
  110.3 4.6 %collective-permute-start.27 = (bf16[8,16,8192]{2,1,0:T(8,128)(2,1)S(1)}, bf16[8,16,8192]{2,1,0:T(8,128)(2,1)S(1)}, u32[]{:S(2)}, u32[]{:S(2)}) collective-permute-start(bf16[8,16,8192]{2,1,0:T(8,128)(2,1)S(1)} %get-tuple-element.89.refs_2_), channel_id=1, source_target_pairs={{0,1},{1,0},{2,3},{3,2},{4,5},{5,4},{6,7},{7,6},{8,9},{9,8},{10,11... | collective-permute-start | bytes 6291464 | tf_op jit(solution)/shard_map/ppermute | solution.py:19
  110.4 22.1 %collective-permute-start.21 = (bf16[3,256,512]{2,1,0:T(8,128)(2,1)}, bf16[3,256,512]{2,1,0:T(8,128)(2,1)S(1)}, u32[]{:S(2)}, u32[]{:S(2)}) collective-permute-start(bf16[3,256,512]{2,1,0:T(8,128)(2,1)} %get-tuple-element.77), channel_id=1, source_target_pairs={{0,64},{16,80},{32,96},{48,112},{64,0},{80,16},{96,32},{112,48},{1... | collective-permute-start | bytes 2359304 | tf_op jit(solution)/shard_map/ppermute | solution.py:19
  111.7 20.8 %collective-permute-start.18 = (bf16[2,16,8192]{2,1,0:T(8,128)(2,1)}, bf16[2,16,8192]{2,1,0:T(8,128)(2,1)S(1)}, u32[]{:S(2)}, u32[]{:S(2)}) collective-permute-start(bf16[2,16,8192]{2,1,0:T(8,128)(2,1)} %get-tuple-element.74), channel_id=1, source_target_pairs={{0,8},{1,9},{2,10},{3,11},{4,12},{5,13},{6,14},{7,15},{8,0},{9,1},... | collective-permute-start | bytes 1572872 | tf_op jit(solution)/shard_map/ppermute | solution.py:19
  118.3 20.4 %collective-permute-start.28 = (bf16[2,16,8192]{2,1,0:T(8,128)(2,1)}, bf16[2,16,8192]{2,1,0:T(8,128)(2,1)S(1)}, u32[]{:S(2)}, u32[]{:S(2)}) collective-permute-start(bf16[2,16,8192]{2,1,0:T(8,128)(2,1)} %get-tuple-element.91), channel_id=1, source_target_pairs={{0,4},{1,5},{2,6},{3,7},{4,0},{5,1},{6,2},{7,3},{8,12},{9,13},{10,... | collective-permute-start | bytes 1572872 | tf_op jit(solution)/shard_map/ppermute | solution.py:19
  118.7 20.9 %collective-permute-start.29 = (bf16[2,16,8192]{2,1,0:T(8,128)(2,1)}, bf16[2,16,8192]{2,1,0:T(8,128)(2,1)}, u32[]{:S(2)}, u32[]{:S(2)}) collective-permute-start(bf16[2,16,8192]{2,1,0:T(8,128)(2,1)} %get-tuple-element.92), channel_id=1, source_target_pairs={{0,12},{1,13},{2,14},{3,15},{4,8},{5,9},{6,10},{7,11},{8,4},{9,5},... | collective-permute-start | bytes 1572872 | tf_op jit(solution)/shard_map/ppermute | solution.py:19
  120.8 11.7 %collective-permute-start.26 = (bf16[256,640]{1,0:T(8,128)(2,1)}, bf16[256,640]{1,0:T(8,128)(2,1)}, u32[]{:S(2)}, u32[]{:S(2)}) collective-permute-start(bf16[256,640]{1,0:T(8,128)(2,1)} %get-tuple-element.86), channel_id=1, source_target_pairs={{0,16},{16,0},{32,48},{48,32},{64,80},{80,64},{96,112},{112,96},{1... | collective-permute-start | bytes 983048 | tf_op jit(solution)/shard_map/ppermute | solution.py:19
  148.7 26.8 %collective-permute-start.32 = (bf16[8,256,512]{2,1,0:T(8,128)(2,1)S(1)}, bf16[8,256,512]{2,1,0:T(8,128)(2,1)}, u32[]{:S(2)}, u32[]{:S(2)}) collective-permute-start(bf16[8,256,512]{2,1,0:T(8,128)(2,1)S(1)} %get-tuple-element.94.refs_4_), channel_id=1, source_target_pairs={{0,1},{1,0},{2,3},{3,2},{4,5},{5,4},{6,7},{7,6},{8,9},{9,8},{10,11... | collective-permute-start | bytes 6291464 | tf_op jit(solution)/shard_map/ppermute | solution.py:19
  148.7 25.1 %collective-permute-start.33 = (bf16[2,256,640]{2,1,0:T(8,128)(2,1)S(1)}, bf16[2,256,640]{2,1,0:T(8,128)(2,1)S(1)}, u32[]{:S(2)}, u32[]{:S(2)}) collective-permute-start(bf16[2,256,640]{2,1,0:T(8,128)(2,1)S(1)} %stack_dqkv.1.refs_4_), channel_id=1, source_target_pairs={{0,32},{16,48},{32,0},{48,16},{64,96},{80,112},{96,64},{112,80},{1... | collective-permute-start | bytes 1966088 | tf_op jit(solution)/shard_map/ppermute | solution.py:19
  149.7 24.6 %collective-permute-start.34 = (bf16[2,256,640]{2,1,0:T(8,128)(2,1)S(1)}, bf16[2,256,640]{2,1,0:T(8,128)(2,1)}, u32[]{:S(2)}, u32[]{:S(2)}) collective-permute-start(bf16[2,256,640]{2,1,0:T(8,128)(2,1)S(1)} %stack_dqkv.1.refs_4_), channel_id=1, source_target_pairs={{0,96},{16,112},{32,64},{48,80},{64,32},{80,48},{96,0},{112,16},{1... | collective-permute-start | bytes 1966088 | tf_op jit(solution)/shard_map/ppermute | solution.py:19
  169.1 17.0 %collective-permute-start.30 = (bf16[16,8192]{1,0:T(8,128)(2,1)}, bf16[16,8192]{1,0:T(8,128)(2,1)}, u32[]{:S(2)}, u32[]{:S(2)}) collective-permute-start(bf16[16,8192]{1,0:T(8,128)(2,1)} %get-tuple-element.96), channel_id=1, source_target_pairs={{0,2},{1,3},{2,0},{3,1},{4,6},{5,7},{6,4},{7,5},{8,10},{9,11},{10,... | collective-permute-start | bytes 786440 | tf_op jit(solution)/shard_map/ppermute | solution.py:19
  173.8 19.8 %collective-permute-start.36 = (bf16[4,512,256]{2,1,0:T(8,128)(2,1)}, bf16[4,512,256]{2,1,0:T(8,128)(2,1)S(1)}, u32[]{:S(2)}, u32[]{:S(2)}) collective-permute-start(bf16[4,512,256]{2,1,0:T(8,128)(2,1)} %copy-done.5), channel_id=1, source_target_pairs={{0,1},{1,0},{2,3},{3,2},{4,5},{5,4},{6,7},{7,6},{8,9},{9,8},{10,11... | collective-permute-start | bytes 3145736 | tf_op jit(solution)/shard_map/ppermute | solution.py:19
  173.8 19.8 %collective-permute-start.37 = (bf16[4,512,256]{2,1,0:T(8,128)(2,1)}, bf16[4,512,256]{2,1,0:T(8,128)(2,1)S(1)}, u32[]{:S(2)}, u32[]{:S(2)}) collective-permute-start(bf16[4,512,256]{2,1,0:T(8,128)(2,1)} %copy-done.3), channel_id=1, source_target_pairs={{0,1},{1,0},{2,3},{3,2},{4,5},{5,4},{6,7},{7,6},{8,9},{9,8},{10,11... | collective-permute-start | bytes 3145736 | tf_op jit(solution)/shard_map/ppermute | solution.py:19
  174.3 15.6 %collective-permute-start.31 = (bf16[2,16,8192]{2,1,0:T(8,128)(2,1)}, bf16[2,16,8192]{2,1,0:T(8,128)(2,1)S(1)}, u32[]{:S(2)}, u32[]{:S(2)}) collective-permute-start(bf16[2,16,8192]{2,1,0:T(8,128)(2,1)} %copy-done.45), channel_id=1, source_target_pairs={{0,8},{1,9},{2,10},{3,11},{4,12},{5,13},{6,14},{7,15},{8,0},{9,1},... | collective-permute-start | bytes 1572872 | tf_op jit(solution)/shard_map/ppermute | solution.py:19
  175.5 18.2 %collective-permute-start.38 = (bf16[2,256,640]{2,1,0:T(8,128)(2,1)S(1)}, bf16[2,256,640]{2,1,0:T(8,128)(2,1)S(1)}, u32[]{:S(2)}, u32[]{:S(2)}) collective-permute-start(bf16[2,256,640]{2,1,0:T(8,128)(2,1)S(1)} %stack_dqkv.1.refs_4_), channel_id=1, source_target_pairs={{0,64},{16,80},{32,96},{48,112},{64,0},{80,16},{96,32},{112,48},{1... | collective-permute-start | bytes 1966088 | tf_op jit(solution)/shard_map/ppermute | solution.py:19
  186.1 26.2 %collective-permute-start.39 = (bf16[512,1024]{1,0:T(8,128)(2,1)S(1)}, bf16[512,1024]{1,0:T(8,128)(2,1)S(1)}, u32[]{:S(2)}, u32[]{:S(2)}) collective-permute-start(bf16[512,1024]{1,0:T(8,128)(2,1)S(1)} %get-tuple-element.99.refs_4_), channel_id=1, source_target_pairs={{0,16},{16,0},{32,48},{48,32},{64,80},{80,64},{96,112},{112,96},{1... | collective-permute-start | bytes 3145736 | tf_op jit(solution)/shard_map/ppermute | solution.py:19
  186.5 25.8 %copy-start.4 = (bf16[4,512,256]{2,1,0:T(8,128)(2,1)S(1)}, bf16[4,512,256]{2,1,0:T(8,128)(2,1)}, u32[]{:S(2)}) copy-start(bf16[4,512,256]{2,1,0:T(8,128)(2,1)} %copy-done.3) | copy-start | bytes 3145732
  186.5 25.8 %copy-start.6 = (bf16[4,512,256]{2,1,0:T(8,128)(2,1)S(1)}, bf16[4,512,256]{2,1,0:T(8,128)(2,1)}, u32[]{:S(2)}) copy-start(bf16[4,512,256]{2,1,0:T(8,128)(2,1)} %copy-done.5) | copy-start | bytes 3145732
  186.5 25.8 %copy-start.23 = (f32[1024,1]{1,0:T(8,128)S(1)}, f32[1024,1]{1,0:T(8,128)}, u32[]{:S(2)}) copy-start(f32[1024,1]{1,0:T(8,128)} %copy.17.refs_8_) | copy-start | bytes 12292
  192.7 29.9 %collective-permute-start.35 = (bf16[16,8192]{1,0:T(8,128)(2,1)S(1)}, bf16[16,8192]{1,0:T(8,128)(2,1)S(1)}, u32[]{:S(2)}, u32[]{:S(2)}) collective-permute-start(bf16[16,8192]{1,0:T(8,128)(2,1)S(1)} %get-tuple-element.101), channel_id=1, source_target_pairs={{0,2},{1,3},{2,0},{3,1},{4,6},{5,7},{6,4},{7,5},{8,10},{9,11},{10,... | collective-permute-start | bytes 786440 | tf_op jit(solution)/shard_map/ppermute | solution.py:19
  (41 other events, 131.4 us)

commit v3 on v2

--- a/solution.py
+++ b/solution.py
@@ -10,7 +10,8 @@
 theta = 500000.0
 f32 = jnp.float32
 bf16 = jnp.bfloat16
-VMEM = 20 * 1024 * 1024
+VMEM = 16 * 1024 * 1024
+LATE = 58 * 1024 * 1024
 ANY = pl.BlockSpec(memory_space=pl.ANY)
 T, CHIP, CORE, Y, X, Z, XL = range(7)
 
@@ -21,7 +22,7 @@
 
 class Order:
     def __init__(self, at):
-        self.at, self.last = at, []
+        self.at, self.last, self.vmem = at, [], VMEM
 
     def wait(self, *arrays):
         self.last = self.last + list(arrays)
@@ -29,11 +30,15 @@
 
 def call(kernel, name, order, operands, outputs, grid=(1,), scratch=()):
     arrays = [array for array, _ in operands]
-    after = [a for a in order.last if not any(a is b for b in arrays)]
-    count, extra = len(arrays), len(after)
+    after = order.last
+    count, extra, results = len(arrays), len(after), len(outputs)
 
     def body(at_ref, *refs):
-        kernel(at_ref, *refs[:count], *refs[count + extra :])
+        outs = refs[count + extra :]
+        outs[results][...] = jnp.zeros_like(outs[results])
+        kernel(at_ref, *refs[:count], *outs[:results], *outs[results + 1 :])
+
+    outputs = outputs + [whole_out((8, 128), f32)]
 
     results = pl.pallas_call(
         body,
@@ -45,11 +50,12 @@
             scratch_shapes=list(scratch),
         ),
         out_shape=[shape for shape, _ in outputs],
-        compiler_params=pltpu.CompilerParams(vmem_limit_bytes=VMEM),
+        compiler_params=pltpu.CompilerParams(vmem_limit_bytes=order.vmem),
         cost_estimate=pl.CostEstimate(flops=1, bytes_accessed=1, transcendentals=0),
         name=name,
     )(order.at, *arrays, *after)
-    order.last = [results[0]]
+    results = list(results)
+    order.last = [results.pop()]
     return results
 
 
@@ -519,92 +525,94 @@
     )[0]
 
 
-def out_terms(order, own, other, rows):
+def out_terms(name, order, own, other, rows, keep, *passed):
     _, length, width = own.shape
     total = rows.shape[2]
-
-    def kernel(at_ref, own_ref, other_ref, rows_ref, send_ref, keep_ref, acc, turned_ref):
+    count = len(passed)
+
+    def kernel(at_ref, own_ref, other_ref, rows_ref, *refs):
+        sources, out_ref, copies, turned_ref = refs[:count], refs[count], refs[count + 1 : -1], refs[-1]
         step = pl.program_id(0)
 
         @pl.when(step == 0)
         def _():
+            for source, target in zip(sources, copies):
+                target[...] = source[...]
             for k in range(4):
-                turned_ref[k] = rows_ref[k].T
-
-        def add(ref):
-            acc[...] = nn(turned_ref[0], ref[0, 0])
-            for k in range(1, 4):
-                acc[...] += nn(turned_ref[k], ref[k, 0])
-
-        pl.when(step % 2 == 0)(lambda: add(own_ref))
-        pl.when(step % 2 == 1)(lambda: add(other_ref))
-
-        @pl.when(step < 2)
-        def _():
-            send_ref[...] = acc[...].astype(bf16)
-
-        @pl.when(step >= 2)
-        def _():
-            keep_ref[...] = acc[...]
-
-    def x_of(i, at):
-        return jnp.where(i < 2, 1 - at[XL], at[XL])
+                turned_ref[:, k * length : (k + 1) * length] = rows_ref[k].T
+
+        def put(ref):
+            product = nn(turned_ref[...], ref[...].reshape(4 * length, width))
+            out_ref[...] = product.astype(out_ref.dtype)
+
+        pl.when(step == 0)(lambda: put(own_ref))
+        pl.when(step == 1)(lambda: put(other_ref))
 
     def side(half, at):
         return jnp.where(half == 0, at[CORE], 1 - at[CORE])
 
-    block = pl.BlockSpec((4, 1, length, width), lambda i, at: (0, x_of(i, at), 0, 0))
+    x_of = (lambda at: at[XL]) if keep else (lambda at: 1 - at[XL])
+    block = pl.BlockSpec((4, 1, length, width), lambda i, at: (0, x_of(at), 0, 0))
     dims = (4, 2, length, width)
     return call(
         kernel,
-        "out_terms",
-        order,
-        [(own.reshape(dims), block), (other.reshape(dims), block), whole(rows)],
+        name,
+        order,
+        [(own.reshape(dims), block), (other.reshape(dims), block), whole(rows)]
+        + [whole(p) for p in passed],
         [
             (
-                shape((total, 2 * width)),
-                pl.BlockSpec((total, width), lambda i, at: (0, side(jnp.minimum(i, 1), at))),
-            ),
-            (
-                shape((total, 2 * width), f32),
-                pl.BlockSpec((total, width), lambda i, at: (0, side(jnp.maximum(i - 2, 0), at))),
-            ),
-        ],
+                shape((total, 2 * width), f32 if keep else bf16),
+                pl.BlockSpec((total, width), lambda i, at: (0, side(i, at))),
+            )
+        ]
+        + [whole_out(p.shape, p.dtype) for p in passed],
+        grid=(2,),
+        scratch=[pltpu.VMEM((total, 4 * length), bf16)],
+    )
+
+
+def add_terms(order, keep, arrived):
+    rows, columns = keep.shape
+    block = pl.BlockSpec((rows // 4, columns), lambda i, at: (i, 0))
+
+    def kernel(at_ref, keep_ref, arrived_ref, out_ref):
+        out_ref[...] = keep_ref[...] + arrived_ref[...].astype(f32)
+
+    return call(
+        kernel,
+        "add_terms",
+        order,
+        [(keep, block), (arrived, block)],
+        [(shape((rows, columns), f32), block)],
         grid=(4,),
-        scratch=[pltpu.VMEM((total, width), f32), pltpu.VMEM((4, total, length), bf16)],
-    )
+    )[0]
 
 
 def q_gradient(order, own, other, rows, gain_column, q_width):
-    _, width, length = own[0].shape
-    total = rows[0].shape[2]
+    _, width, wide = own.shape
+    length, total = rows[0].shape[1:]
+    head = total - q_width
 
     def kernel(at_ref, *refs):
-        blocks, row_refs, gain_ref, q_ref, kv_ref, acc = refs[:4], refs[4:8], *refs[8:]
-        half, k = pl.program_id(0), pl.program_id(1)
-
-        def add(pair):
-            for number in range(4):
-
-                @pl.when(k == number)
-                def _():
-                    term = nn(pair[0][0], row_refs[number][0]) + nn(pair[1][0], row_refs[number][1])
-                    if number == 0:
-                        acc[...] = term
-                    else:
-                        acc[...] += term
-
-        pl.when(half == 0)(lambda: add(blocks[:2]))
-        pl.when(half == 1)(lambda: add(blocks[2:]))
-
-        @pl.when(k == 3)
+        own_ref, other_ref, row_refs, gain_ref = *refs[:2], refs[2:6], refs[6]
+        q_out, kv_out, acc, joined = refs[7:]
+        half = pl.program_id(0)
+
+        @pl.when(half == 0)
         def _():
-            product = acc[...] * gain_ref[...]
-            q_ref[...] = product[:, :q_width]
-            kv_ref[...] = product[:, q_width:]
-
-    first = pl.BlockSpec((1, width, length), lambda h, k, at: (jnp.where(h == 0, k, 3), 0, 0))
-    second = pl.BlockSpec((1, width, length), lambda h, k, at: (jnp.where(h == 0, 0, k), 0, 0))
+            for k in range(4):
+                for x in range(2):
+                    joined[x, k * length : (k + 1) * length, :] = row_refs[k][x]
+
+        def add(ref):
+            acc[...] = nn(ref[0], joined[0])
+            acc[...] += nn(ref[1], joined[1])
+
+        pl.when(half == 0)(lambda: add(own_ref))
+        pl.when(half == 1)(lambda: add(other_ref))
+        q_out[...] = acc[:, :q_width] * gain_ref[...]
+        kv_out[...] = acc[:, q_width:] * gain_ref[...]
 
     def side(h, at):
         return jnp.where(h == 0, at[CORE], 1 - at[CORE])
@@ -613,19 +621,20 @@
         kernel,
         "q_gradient",
         order,
-        [(a, first) for a in own]
-        + [(a, second) for a in other]
+        [whole(own), whole(other)]
         + [whole(a) for a in rows]
-        + [(gain_column, pl.BlockSpec((width, 1), lambda h, k, at: (side(h, at), 0)))],
+        + [
+            (gain_column, pl.BlockSpec((width, 1), lambda h, at: (side(h, at), 0))),
+        ],
         [
             (
                 shape((2 * width, size), f32),
-                pl.BlockSpec((width, size), lambda h, k, at: (side(h, at), 0)),
+                pl.BlockSpec((width, size), lambda h, at: (side(h, at), 0)),
             )
-            for size in (q_width, total - q_width)
+            for size in (q_width, head)
         ],
-        grid=(2, 4),
-        scratch=[pltpu.VMEM((width, total), f32)],
+        grid=(2,),
+        scratch=[pltpu.VMEM((width, total), f32), pltpu.VMEM((2, 4 * length, total), bf16)],
     )
 
 
@@ -645,15 +654,17 @@
 
 
 def split_x(name, order, parts):
+    _, width, length = parts[0].shape
+
     def plan(at_ref, ins, outs):
         pairs = []
         for k, ref in enumerate(ins):
-            pairs.append((ref.at[at_ref[XL]], outs[0].at[k]))
-            pairs.append((ref.at[1 - at_ref[XL]], outs[1].at[k]))
+            place = pl.ds(k * length, length)
+            pairs.append((ref.at[at_ref[XL]], outs[0].at[:, place]))
+            pairs.append((ref.at[1 - at_ref[XL]], outs[1].at[:, place]))
         return pairs
 
-    dims = (len(parts),) + parts[0].shape[1:]
-    return move(name, order, parts, [shape(dims)] * 2, plan)
+    return move(name, order, parts, [shape((width, len(parts) * length))] * 2, plan)
 
 
 def stack_b(order, parts):
@@ -743,55 +754,53 @@
     a_cross = partner(a_send, "dp", 1)
     out_parts = pair_sum(order, keep, arrived, 4, Y)
     out_near = y_near(out_parts)
-
     dattn, own_cot = out_gradient(order, cot_own, cot_other, o_weight)
     dq, dkv_keep, send = attend_gradient(order, dattn, probs, rot, kv_own, kv_other, tables)
-    b_far = far(cot_blocks)
     arrived = partner(send, "tensor", 1)
     order.wait(*b_near.values(), *out_near.values(), a_cross)
     dqkv, scaled = join_gradient(order, dq, dkv_keep, arrived, inverse, tables)
     scaled_other = partner(scaled, "dp", 1)
+    b_far = far(cot_blocks)
     out_far = y_far(out_parts)
-
     send, keep, gain_part = norm_gradient(order, dqkv, q_weight, kv_weight, normed, gain_row)
     arrived = partner(send, "tensor", 1)
     x_parts = pair_sum(order, keep, arrived, 4, Y)
     x_near = y_near(x_parts)
     gain_part = jnp.sum(lax.all_to_all(gain_part, "dp", 0, 0, tiled=True), axis=0)
-    order.wait(*b_far.values(), *out_far.values(), *x_near.values(), gain_part)
-    (pair,) = stack("stack_dqkv", order, [scaled, scaled_other])
-    dqkv_near = near([pair] * 4)
-    (b_own, attn_all) = stack_b(order, in_order({0: cot_blocks[0]}, b_near, b_far))
-    b_other = partner(b_own, "tensor", 1)
     gain_part = lax.all_to_all(
         jnp.broadcast_to(gain_part[None], (16, 1, 2 * width)), "tensor", 0, 0, tiled=True
     )
     gain_grad = jnp.sum(gain_part, axis=0)
+    order.wait(*b_far.values(), *out_far.values(), *x_near.values(), gain_grad)
+    pair, a_own = stack("stack_dqkv", order, [scaled, scaled_other], [a_keep, a_cross])
+    dqkv_near = near([pair] * 4)
+    b_own, attn_all = stack_b(order, in_order({0: cot_blocks[0]}, b_near, b_far))
+    b_other = partner(b_own, "tensor", 1)
     x_far = y_far(x_parts)
-    order.wait(gain_grad)
+    (keep,) = out_terms("out_keep", order, b_own, b_other, attn_all, True)
     out_keep, out_send = ring_sum(order, in_order({0: out_parts[0]}, out_near, out_far))
     out_arrived = partner(out_send, "tensor", 2)
-    a_other = [partner(a, "tensor", 1) for a in (a_keep, a_cross)]
-    order.wait(*dqkv_near.values())
-    send, keep = out_terms(order, b_own, b_other, attn_all)
-    dqkv_far = far([pair] * 4)
-    o_arrived = partner(send, "dp", 1)
-    result = (own_tokens.astype(f32) + (out_keep + out_arrived.astype(f32))).astype(bf16)
-
     x_keep, x_send = ring_sum(order, in_order({0: x_parts[0]}, x_near, x_far))
     x_arrived = partner(x_send, "tensor", 2)
-    o_grad = keep + o_arrived.astype(f32)
-
-    order.wait(o_arrived)
+    order.wait(*dqkv_near.values())
+    send, pair_copy = out_terms("out_send", order, b_own, b_other, attn_all, False, pair)
+    o_arrived = partner(send, "dp", 1)
+    dqkv_far = far([pair_copy] * 4)
+    a_other = partner(a_own, "tensor", 1)
+    result = (own_tokens.astype(f32) + (out_keep + out_arrived.astype(f32))).astype(bf16)
+    order.vmem = LATE
     q_grad, kv_grad = q_gradient(
         order,
-        [a_keep, a_cross],
+        a_own,
         a_other,
         in_order({0: pair}, dqkv_near, dqkv_far),
         gain_column,
         q_width,
     )
+    order.vmem = VMEM
+    order.wait(o_arrived)
     x_grad = input_gradient(order, x_keep, x_arrived, own_tokens, inverse, own_cot, gain_row)
+    o_grad = add_terms(order, keep, o_arrived)
     return (result[None], x_grad[None], gain_grad.reshape(-1), q_grad, kv_grad, o_grad)
 
 

time: 226 us -> 216 us (0.956)
  waiting for transfers between devices: 59.6 us -> 50.2 us
  Pallas kernels: 68.8 us -> 73.9 us
  local copies, waits for them, and re-layouts: 22.3 us -> 17.3 us
    ppermute x40 -> x39, waiting for transfers between devices: 59.6 us -> 50.2 us  [partner(): lax.ppermute(array, axis, [(i, i ^ bits) for i in range(lax.axis_size(axi...]
    pallas_call x23 -> x25, Pallas kernels: 68.8 us -> 73.9 us  [call(): pl.pallas_call(body, grid_spec=pltpu.PrefetchScalarGridSpec(num_scalar_pr...]
    unnamed x98 -> x104, local copies, waits for them, and re-layouts: 20.4 us -> 16.2 us
    ppermute x40 -> x39, starting transfers between devices: 46.5 us -> 48 us  [partner(): lax.ppermute(array, axis, [(i, i ^ bits) for i in range(lax.axis_size(axi...]
  transfers between devices with their start and end apart: 40 -> 39, of which waited for: 15 -> 15; matrix products, arithmetic and copies ran while one was open for 3% -> 1% of each run, Pallas kernels for 25% -> 26%
where the time goes in v3:
time: 216 us; the launch traced here: 215 us
  Pallas kernels  73.9 us (34%)
  waiting for transfers between devices  50.2 us (23%)
  starting transfers between devices  48 us (22%)
  blocking collectives  22.4 us (10%)
  local copies, waits for them, and re-layouts  17.3 us (8%)
    pallas_call x25, Pallas kernels, call(): pl.pallas_call(body, grid_spec=pltpu.PrefetchScalarGridSpec(num_scalar_pr...  73.9 us
    ppermute x39, waiting for transfers between devices, partner(): lax.ppermute(array, axis, [(i, i ^ bits) for i in range(lax.axis_size(axi...  50.2 us
    ppermute x39, starting transfers between devices, partner(): lax.ppermute(array, axis, [(i, i ^ bits) for i in range(lax.axis_size(axi...  48 us
    unnamed x104, local copies, waits for them, and re-layouts  16.2 us
    all_to_all x1, blocking collectives, on_device(): lax.all_to_all(jnp.broadcast_to(gain_part[None], (16, 1, 2 * width)), 'te...  11.2 us
    all_to_all x1, blocking collectives, on_device(): lax.all_to_all(gain_part, 'dp', 0, 0, tiled=True)  11.1 us
  transfers between devices with their start and end apart: 39, of which 15 were waited for; matrix products, arithmetic and copies ran while one was open for 1% of the time, Pallas kernels for 26%

profile of v3, /device:TPU:6, one launch (start us, length us, event | category | flops | bytes accessed | tf_op | source)
XLA Modules:
  0.0 215.0 jit_solution(3812983301793721875)
XLA Ops:
  2.1 1.6 collective-permute-start.1
  3.7 2.9 %collective-permute-start.3 = (bf16[256,512]{1,0:T(8,128)(2,1)}, bf16[256,512]{1,0:T(8,128)(2,1)S(1)}, u32[]{:S(2)}, u32[]{:S(2)}) collective-permute-start(bf16[256,512]{1,0:T(8,128)(2,1)} %bitcast.42), channel_id=1, source_target_pairs={{0,8},{1,9},{2,10},{3,11},{4,12},{5,13},{6,14},{7,15},{8,0},{9,1},... | collective-permute-start | bytes 786440 | tf_op jit(solution)/shard_map/ppermute | solution.py:20
  6.8 2.1 collective-permute-start.7
  8.9 2.0 collective-permute-done
  11.0 2.2 %collective-permute-start.2 = (bf16[256,512]{1,0:T(8,128)(2,1)S(1)}, bf16[256,512]{1,0:T(8,128)(2,1)S(1)}, u32[]{:S(2)}, u32[]{:S(2)}) collective-permute-start(bf16[256,512]{1,0:T(8,128)(2,1)S(1)} %collective-permute-done), channel_id=1, source_target_pairs={{0,4},{1,5},{2,6},{3,7},{4,0},{5,1},{6,2},{7,3},{8,12},{9,13},{10,... | collective-permute-start | bytes 786440 | tf_op jit(solution)/shard_map/ppermute | solution.py:20
  13.2 2.3 %collective-permute-start.4 = (bf16[256,512]{1,0:T(8,128)(2,1)S(1)}, bf16[256,512]{1,0:T(8,128)(2,1)S(1)}, u32[]{:S(2)}, u32[]{:S(2)}) collective-permute-start(bf16[256,512]{1,0:T(8,128)(2,1)S(1)} %collective-permute-done), channel_id=1, source_target_pairs={{0,8},{1,9},{2,10},{3,11},{4,12},{5,13},{6,14},{7,15},{8,0},{9,1},... | collective-permute-start | bytes 786440 | tf_op jit(solution)/shard_map/ppermute | solution.py:20
  15.5 4.2 %collective-permute-done.3 = bf16[256,512]{1,0:T(8,128)(2,1)S(1)} collective-permute-done((bf16[256,512]{1,0:T(8,128)(2,1)}, bf16[256,512]{1,0:T(8,128)(2,1)S(1)}, u32[]{:S(2)}, u32[]{:S(2)}) %collective-permute-start.3) | collective-permute-done | bytes 262176 | tf_op jit(solution)/shard_map/ppermute | solution.py:20
  21.0 1.9 collective-permute-done.2
  22.8 6.7 %collective-permute-done.4 = bf16[256,512]{1,0:T(8,128)(2,1)S(1)} collective-permute-done((bf16[256,512]{1,0:T(8,128)(2,1)S(1)}, bf16[256,512]{1,0:T(8,128)(2,1)S(1)}, u32[]{:S(2)}, u32[]{:S(2)}) %collective-permute-start.4) | collective-permute-done | bytes 262176 | tf_op jit(solution)/shard_map/ppermute | solution.py:20
  29.5 2.5 %collective-permute-done.6 = bf16[256,512]{1,0:T(8,128)(2,1)S(1)} collective-permute-done((bf16[256,512]{1,0:T(8,128)(2,1)S(1)}, bf16[256,512]{1,0:T(8,128)(2,1)S(1)}, u32[]{:S(2)}, u32[]{:S(2)}) %collective-permute-start.6) | collective-permute-done | bytes 262176 | tf_op jit(solution)/shard_map/ppermute | solution.py:20
  36.3 2.0 collective-permute-start.10
  38.3 2.5 %collective-permute-start.11 = (bf16[2,512,256]{2,1,0:T(8,128)(2,1)S(1)}, bf16[2,512,256]{2,1,0:T(8,128)(2,1)S(1)}, u32[]{:S(2)}, u32[]{:S(2)}) collective-permute-start(bf16[2,512,256]{2,1,0:T(8,128)(2,1)S(1)} %get-tuple-element.98), channel_id=1, source_target_pairs={{0,96},{16,112},{32,64},{48,80},{64,32},{80,48},{96,0},{112,16},{1... | collective-permute-start | bytes 1572872 | tf_op jit(solution)/shard_map/ppermute | solution.py:20
  41.2 3.7 %norm.1 = (bf16[256,8192]{1,0:T(8,128)(2,1)S(1)}, f32[256,1]{1,0:T(8,128)S(1)}, bf16[16,8192]{1,0:T(8,128)(2,1)S(1)}, f32[8,128]{1,0:T(8,128)S(1)}) custom-call(s32[7]{0:T(128)S(1)} %stack.31.at_ref, f32[1,8192]{1,0:T(1,128)S(1)} %bitcast.37, bf16[8,256,512]{2,1,0:T(8,128)(2,1)S(1)} %get-tuple-element.86.refs_0_.refs_1_, ...), custom_call_target="tpu_custom_call" | custom-call | flops 1 | bytes 1 | tf_op jit(solution)/shard_map/norm/pallas_call | solution.py:43
  45.0 1.7 copy-done.1
  46.8 5.9 %project.1 = (bf16[256,512]{1,0:T(8,128)(2,1)S(1)}, bf16[256,128]{1,0:T(8,128)(2,1)S(1)}, f32[8,128]{1,0:T(8,128)S(1)}) custom-call(s32[7]{0:T(128)S(1)} %stack.31.at_ref, bf16[256,8192]{1,0:T(8,128)(2,1)S(1)} %get-tuple-element.90.refs_0_.refs_3_, bf16[8192,512]{1,0:T(8,128)(2,1)S(1)} %copy-done, bf16[8192,128]{1,0:T(8,128)(2,1)S(1)} %copy-done.1, ...), custom_call_target="tpu_custom_call" | custom-call | flops 1 | bytes 1 | tf_op jit(solution)/shard_map/project/pallas_call | solution.py:43
  53.5 2.2 %collective-permute-start.15 = (bf16[2,512,256]{2,1,0:T(8,128)(2,1)S(1)}, bf16[2,512,256]{2,1,0:T(8,128)(2,1)S(1)}, u32[]{:S(2)}, u32[]{:S(2)}) collective-permute-start(bf16[2,512,256]{2,1,0:T(8,128)(2,1)S(1)} %get-tuple-element.104), channel_id=1, source_target_pairs={{0,64},{16,80},{32,96},{48,112},{64,0},{80,16},{96,32},{112,48},{1... | collective-permute-start | bytes 1572872 | tf_op jit(solution)/shard_map/ppermute | solution.py:20
  55.6 2.8 %collective-permute-start.16 = (bf16[2,256,512]{2,1,0:T(8,128)(2,1)S(1)}, bf16[2,256,512]{2,1,0:T(8,128)(2,1)S(1)}, u32[]{:S(2)}, u32[]{:S(2)}) collective-permute-start(bf16[2,256,512]{2,1,0:T(8,128)(2,1)S(1)} %get-tuple-element.105), channel_id=1, source_target_pairs={{0,8},{1,9},{2,10},{3,11},{4,12},{5,13},{6,14},{7,15},{8,0},{9,1},... | collective-permute-start | bytes 1572872 | tf_op jit(solution)/shard_map/ppermute | solution.py:20
  59.7 1.7 attend.1
  61.3 5.5 %mix.1 = (bf16[8,16,8192]{2,1,0:T(8,128)(2,1)S(1)}, bf16[8,16,8192]{2,1,0:T(8,128)(2,1)S(1)}, f32[8,128]{1,0:T(8,128)S(1)}) custom-call(s32[7]{0:T(128)S(1)} %stack.31.at_ref, bf16[256,512]{1,0:T(8,128)(2,1)S(1)} %get-tuple-element.99.refs_0_.refs_1_, bf16[512,8192]{1,0:T(8,128)(2,1)S(1)} %bitcast.30, f32[8,128]{1,0:T(8,128)S(1)} %get-tuple-element.100.refs_2_), custom_call_target="tpu_custom_call" | custom-call | flops 1 | bytes 1 | tf_op jit(solution)/shard_map/mix/pallas_call | solution.py:43
  68.5 2.3 %collective-permute-done.16.refs_2_ = bf16[2,256,512]{2,1,0:T(8,128)(2,1)S(1)} collective-permute-done((bf16[2,256,512]{2,1,0:T(8,128)(2,1)S(1)}, bf16[2,256,512]{2,1,0:T(8,128)(2,1)S(1)}, u32[]{:S(2)}, u32[]{:S(2)}) %collective-permute-start.16) | collective-permute-done | bytes 524320 | tf_op jit(solution)/shard_map/ppermute | solution.py:20
  72.0 2.1 pick_cot.1
  78.2 2.5 %pair_sum.2 = (bf16[2,16,8192]{2,1,0:T(8,128)(2,1)S(1)}, bf16[2,16,8192]{2,1,0:T(8,128)(2,1)S(1)}, bf16[2,16,8192]{2,1,0:T(8,128)(2,1)}, bf16[2,16,8192]{2,1,0:T(8,128)(2,1)S(1)}, f32[8,128]{1,0:T(8,128)S(1)}) custom-call(s32[7]{0:T(128)S(1)} %stack.31.at_ref, bf16[8,16,8192]{2,1,0:T(8,128)(2,1)S(1)} %get-tuple-element.101.refs_0_, ...), custom_call_target="tpu_custom_call" | custom-call | flops 1 | bytes 1 | tf_op jit(solution)/shard_map/pair_sum/pallas_call | solution.py:43
  82.2 2.3 %collective-permute-start.19 = (bf16[2,16,8192]{2,1,0:T(8,128)(2,1)S(1)}, bf16[2,16,8192]{2,1,0:T(8,128)(2,1)S(1)}, u32[]{:S(2)}, u32[]{:S(2)}) collective-permute-start(bf16[2,16,8192]{2,1,0:T(8,128)(2,1)S(1)} %get-tuple-element.114), channel_id=1, source_target_pairs={{0,12},{1,13},{2,14},{3,15},{4,8},{5,9},{6,10},{7,11},{8,4},{9,5},... | collective-permute-start | bytes 1572872 | tf_op jit(solution)/shard_map/ppermute | solution.py:20
  84.5 5.2 %out_gradient.1 = (bf16[256,512]{1,0:T(8,128)(2,1)S(1)}, bf16[16,8192]{1,0:T(8,128)(2,1)S(1)}, f32[8,128]{1,0:T(8,128)S(1)}) custom-call(s32[7]{0:T(128)S(1)} %stack.31.at_ref, bf16[8,256,512]{2,1,0:T(8,128)(2,1)S(1)} %get-tuple-element.107.refs_0_, bf16[8,256,512]{2,1,0:T(8,128)(2,1)S(1)} %collective-permute-done.23.refs_1_, ...), custom_call_target="tpu_custom_call" | custom-call | flops 1 | bytes 1 | tf_op jit(solution)/shard_map/out_gradient/pallas_call | solution.py:43
  89.8 2.3 %attend_gradient.1 = (bf16[256,512]{1,0:T(8,128)(2,1)S(1)}, f32[256,128]{1,0:T(8,128)S(1)}, bf16[256,128]{1,0:T(8,128)(2,1)S(1)}, f32[8,128]{1,0:T(8,128)S(1)}) custom-call(s32[7]{0:T(128)S(1)} %stack.31.at_ref, bf16[256,512]{1,0:T(8,128)(2,1)S(1)} %get-tuple-element.120.refs_0_, f32[4,256,256]{2,1,0:T(8,128)S(1)} %get-tuple-element.121.refs_1_, ...), custom_call_target="tpu_custom_call" | custom-call | flops 1 | bytes 1 | tf_op jit(solution)/shard_map/attend_gradient/pallas_call | solution.py:43
  92.1 4.4 %collective-permute-done.20.refs_7_.refs_1_ = bf16[3,256,512]{2,1,0:T(8,128)(2,1)S(1)} collective-permute-done((bf16[3,256,512]{2,1,0:T(8,128)(2,1)S(1)}, bf16[3,256,512]{2,1,0:T(8,128)(2,1)S(1)}, u32[]{:S(2)}, u32[]{:S(2)}) %collective-permute-start.20) | collective-permute-done | bytes 786464 | tf_op jit(solution)/shard_map/ppermute | solution.py:20
  96.4 1.9 collective-permute-done.22.refs_8_.refs_3_
  98.4 3.6 %collective-permute-done.25.refs_11_ = bf16[512,1024]{1,0:T(8,128)(2,1)S(1)} collective-permute-done((bf16[512,1024]{1,0:T(8,128)(2,1)S(1)}, bf16[512,1024]{1,0:T(8,128)(2,1)S(1)}, u32[]{:S(2)}, u32[]{:S(2)}) %collective-permute-start.25) | collective-permute-done | bytes 1048608 | tf_op jit(solution)/shard_map/ppermute | solution.py:20
  104.1 6.3 %norm_gradient.1 = (bf16[8,16,8192]{2,1,0:T(8,128)(2,1)S(1)}, bf16[8,16,8192]{2,1,0:T(8,128)(2,1)S(1)}, f32[8,1,1024]{2,1,0:T(1,128)S(1)}, f32[8,128]{1,0:T(8,128)S(1)}) custom-call(s32[7]{0:T(128)S(1)} %stack.31.at_ref, bf16[256,640]{1,0:T(8,128)(2,1)S(1)} %get-tuple-element.131.refs_0_, bf16[8192,512]{1,0:T(8,128)(2,1)S(1)} %copy-done, ...), custom_call_target="tpu_custom_call" | custom-call | flops 1 | bytes 1 | tf_op jit(solution)/shard_map/norm_gradient/pallas_call | solution.py:43
  111.6 3.2 %collective-permute-start.18 = (bf16[2,16,8192]{2,1,0:T(8,128)(2,1)}, bf16[2,16,8192]{2,1,0:T(8,128)(2,1)S(1)}, u32[]{:S(2)}, u32[]{:S(2)}) collective-permute-start(bf16[2,16,8192]{2,1,0:T(8,128)(2,1)} %get-tuple-element.113), channel_id=1, source_target_pairs={{0,8},{1,9},{2,10},{3,11},{4,12},{5,13},{6,14},{7,15},{8,0},{9,1},... | collective-permute-start | bytes 1572872 | tf_op jit(solution)/shard_map/ppermute | solution.py:20
  114.9 2.8 %pair_sum.3 = (bf16[2,16,8192]{2,1,0:T(8,128)(2,1)S(1)}, bf16[2,16,8192]{2,1,0:T(8,128)(2,1)}, bf16[2,16,8192]{2,1,0:T(8,128)(2,1)}, bf16[2,16,8192]{2,1,0:T(8,128)(2,1)}, f32[8,128]{1,0:T(8,128)S(1)}) custom-call(s32[7]{0:T(128)S(1)} %stack.31.at_ref, bf16[8,16,8192]{2,1,0:T(8,128)(2,1)S(1)} %get-tuple-element.133.refs_0_, ...), custom_call_target="tpu_custom_call" | custom-call | flops 1 | bytes 1 | tf_op jit(solution)/shard_map/pair_sum/pallas_call | solution.py:43
  118.9 2.1 collective-permute-start.29
  121.3 11.1 %all_to_all.10 = f32[8,1,1024]{2,1,0:T(1,128)S(1)} all-to-all(f32[8,1,1024]{2,1,0:T(1,128)S(1)} %get-tuple-element.139), channel_id=1, replica_groups=mesh['dp'=8,'tensor'=16] {'dp'}, dimensions={0} | all-to-all | bytes 65536 | tf_op jit(solution)/shard_map/all_to_all | solution.py:769
  132.5 11.2 %all_to_all.11 = f32[16,1,1024]{2,1,0:T(1,128)S(1)} all-to-all(f32[16,1,1024]{2,1,0:T(1,128)S(1)} %broadcast_in_dim.67), channel_id=1, replica_groups=mesh['dp'=8,'tensor'=16] {'tensor'}, dimensions={0} | all-to-all | bytes 131072 | tf_op jit(solution)/shard_map/all_to_all | solution.py:770
  144.0 2.0 copy-done.26
  146.0 3.6 %stack_dqkv.1 = (bf16[2,256,640]{2,1,0:T(8,128)(2,1)}, bf16[2,512,1024]{2,1,0:T(8,128)(2,1)}, f32[8,128]{1,0:T(8,128)S(1)}) custom-call(s32[7]{0:T(128)S(1)} %stack.31.at_ref, bf16[1,256,640]{2,1,0:T(8,128)(2,1)} %bitcast.18.refs_0_, bf16[1,256,640]{2,1,0:T(8,128)(2,1)} %bitcast.19.refs_1_, bf16[1,512,1024]{2,1,0:T(8,128)(2,1)S(1)} %bitcast.36, ...), custom_call_target="tpu_custom_call" | custom-call | flops 1 | bytes 1 | tf_op jit(solution)/shard_map/stack_dqkv/pallas_call | solution.py:43
  152.8 2.1 collective-permute-start.36
  156.3 2.4 %out_keep.1 = (f32[512,1024]{1,0:T(8,128)S(1)}, f32[8,128]{1,0:T(8,128)S(1)}) custom-call(s32[7]{0:T(128)S(1)} %stack.31.at_ref, bf16[4,2,256,512]{3,2,1,0:T(8,128)(2,1)S(1)} %bitcast.31, bf16[4,2,256,512]{3,2,1,0:T(8,128)(2,1)S(1)} %bitcast.33, bf16[4,256,512]{2,1,0:T(8,128)(2,1)S(1)} %get-tuple-element.142.refs_2_, f32[8,128]{1,0:T(8,128)S(1)} %get-tuple-element.143.refs_3_), custom_call_target="tpu_custom_call" | custom-call | flops 1 | bytes 1 | tf_op jit(solution)/shard_map/out_keep/pallas_call | solution.py:43
  160.0 2.2 %ring_sum.2 = (f32[16,8192]{1,0:T(8,128)S(1)}, bf16[16,8192]{1,0:T(8,128)(2,1)}, f32[8,128]{1,0:T(8,128)S(1)}) custom-call(s32[7]{0:T(128)S(1)} %stack.31.at_ref, bf16[2,16,8192]{2,1,0:T(8,128)(2,1)S(1)} %copy-done.32, bf16[2,16,8192]{2,1,0:T(8,128)(2,1)S(1)} %copy-done.14, bf16[2,16,8192]{2,1,0:T(8,128)(2,1)S(1)} %copy-done.22, ...), custom_call_target="tpu_custom_call" | custom-call | flops 1 | bytes 1 | tf_op jit(solution)/shard_map/ring_sum/pallas_call | solution.py:43
  163.0 2.9 %collective-permute-start.31 = (bf16[16,8192]{1,0:T(8,128)(2,1)}, bf16[16,8192]{1,0:T(8,128)(2,1)}, u32[]{:S(2)}, u32[]{:S(2)}) collective-permute-start(bf16[16,8192]{1,0:T(8,128)(2,1)} %get-tuple-element.146), channel_id=1, source_target_pairs={{0,2},{1,3},{2,0},{3,1},{4,6},{5,7},{6,4},{7,5},{8,10},{9,11},{10,... | collective-permute-start | bytes 786440 | tf_op jit(solution)/shard_map/ppermute | solution.py:20
  166.9 3.5 %collective-permute-done.32.refs_2_ = bf16[2,16,8192]{2,1,0:T(8,128)(2,1)} collective-permute-done((bf16[2,16,8192]{2,1,0:T(8,128)(2,1)}, bf16[2,16,8192]{2,1,0:T(8,128)(2,1)}, u32[]{:S(2)}, u32[]{:S(2)}) %collective-permute-start.32) | collective-permute-done | bytes 524320 | tf_op jit(solution)/shard_map/ppermute | solution.py:20
  173.5 2.7 %ring_sum.3 = (f32[16,8192]{1,0:T(8,128)S(1)}, bf16[16,8192]{1,0:T(8,128)(2,1)S(1)}, f32[8,128]{1,0:T(8,128)S(1)}) custom-call(s32[7]{0:T(128)S(1)} %stack.31.at_ref, bf16[2,16,8192]{2,1,0:T(8,128)(2,1)S(1)} %copy-done.34, bf16[2,16,8192]{2,1,0:T(8,128)(2,1)S(1)} %copy-done.18, bf16[2,16,8192]{2,1,0:T(8,128)(2,1)} %collective-permute-done.32.refs_2_, ...), custom_call_target="tpu_custom_call" | custom-call | flops 1 | bytes 1 | tf_op jit(solution)/shard_map/ring_sum/pallas_call | solution.py:43
  176.3 3.0 %collective-permute-start.33 = (bf16[16,8192]{1,0:T(8,128)(2,1)S(1)}, bf16[16,8192]{1,0:T(8,128)(2,1)S(1)}, u32[]{:S(2)}, u32[]{:S(2)}) collective-permute-start(bf16[16,8192]{1,0:T(8,128)(2,1)S(1)} %get-tuple-element.151), channel_id=1, source_target_pairs={{0,2},{1,3},{2,0},{3,1},{4,6},{5,7},{6,4},{7,5},{8,10},{9,11},{10,... | collective-permute-start | bytes 786440 | tf_op jit(solution)/shard_map/ppermute | solution.py:20
  179.3 4.2 %out_send.1 = (bf16[512,1024]{1,0:T(8,128)(2,1)}, bf16[2,256,640]{2,1,0:T(8,128)(2,1)S(1)}, f32[8,128]{1,0:T(8,128)S(1)}) custom-call(s32[7]{0:T(128)S(1)} %stack.31.at_ref, bf16[4,2,256,512]{3,2,1,0:T(8,128)(2,1)S(1)} %bitcast.32, bf16[4,2,256,512]{3,2,1,0:T(8,128)(2,1)S(1)} %bitcast.34, bf16[4,256,512]{2,1,0:T(8,128)(2,1)S(1)} %get-tuple-element.142.refs_2_, ...), custom_call_target="tpu_custom_call" | custom-call | flops 1 | bytes 1 | tf_op jit(solution)/shard_map/out_send/pallas_call | solution.py:43
  185.2 1.7 fusion
  187.0 13.4 %collective-permute-done.37.refs_4_ = bf16[2,256,640]{2,1,0:T(8,128)(2,1)S(1)} collective-permute-done((bf16[2,256,640]{2,1,0:T(8,128)(2,1)S(1)}, bf16[2,256,640]{2,1,0:T(8,128)(2,1)S(1)}, u32[]{:S(2)}, u32[]{:S(2)}) %collective-permute-start.37) | collective-permute-done | bytes 655392 | tf_op jit(solution)/shard_map/ppermute | solution.py:20
  201.2 8.9 %q_gradient.1 = (f32[1024,512]{1,0:T(8,128)}, f32[1024,128]{1,0:T(8,128)}, f32[8,128]{1,0:T(8,128)}) custom-call(s32[7]{0:T(128)} %copy-done.39, bf16[2,512,1024]{2,1,0:T(8,128)(2,1)} %get-tuple-element.153.refs_0_, bf16[2,512,1024]{2,1,0:T(8,128)(2,1)} %collective-permute-done.34.refs_1_, bf16[2,256,640]{2,1,0:T(8,128)(2,1)} %get-tuple-element.154.refs_3_.refs_2_, ...), custom_call_target="tpu_custom_call" | custom-call | flops 1 | bytes 1 | tf_op jit(solution)/shard_map/q_gradient/pallas_call | solution.py:43
  212.6 2.4 %add_terms.1 = (f32[512,1024]{1,0:T(8,128)}, f32[8,128]{1,0:T(8,128)}) custom-call(s32[7]{0:T(128)S(1)} %copy-done.40, f32[512,1024]{1,0:T(8,128)S(1)} %copy-done.12, bf16[512,1024]{1,0:T(8,128)(2,1)S(1)} %collective-permute-done.38.refs_7_.refs_1_, f32[8,128]{1,0:T(8,128)S(1)} %get-tuple-element.164.refs_2_), custom_call_target="tpu_custom_call" | custom-call | flops 1 | bytes 1 | tf_op jit(solution)/shard_map/add_terms/pallas_call | solution.py:43
  (170 shorter events, 38.9 us)
Async XLA Ops:
  0.6 10.3 %collective-permute-start = (bf16[256,512]{1,0:T(8,128)(2,1)}, bf16[256,512]{1,0:T(8,128)(2,1)S(1)}, u32[]{:S(2)}, u32[]{:S(2)}) collective-permute-start(bf16[256,512]{1,0:T(8,128)(2,1)} %bitcast.40), channel_id=1, source_target_pairs={{0,2},{1,3},{2,0},{3,1},{4,6},{5,7},{6,4},{7,5},{8,10},{9,11},{10,... | collective-permute-start | bytes 786440 | tf_op jit(solution)/shard_map/ppermute | solution.py:20
  2.1 11.1 %collective-permute-start.1 = (bf16[256,512]{1,0:T(8,128)(2,1)}, bf16[256,512]{1,0:T(8,128)(2,1)S(1)}, u32[]{:S(2)}, u32[]{:S(2)}) collective-permute-start(bf16[256,512]{1,0:T(8,128)(2,1)} %bitcast.41), channel_id=1, source_target_pairs={{0,4},{1,5},{2,6},{3,7},{4,0},{5,1},{6,2},{7,3},{8,12},{9,13},{10,... | collective-permute-start | bytes 786440 | tf_op jit(solution)/shard_map/ppermute | solution.py:20
  3.7 16.0 %collective-permute-start.3 = (bf16[256,512]{1,0:T(8,128)(2,1)}, bf16[256,512]{1,0:T(8,128)(2,1)S(1)}, u32[]{:S(2)}, u32[]{:S(2)}) collective-permute-start(bf16[256,512]{1,0:T(8,128)(2,1)} %bitcast.42), channel_id=1, source_target_pairs={{0,8},{1,9},{2,10},{3,11},{4,12},{5,13},{6,14},{7,15},{8,0},{9,1},... | collective-permute-start | bytes 786440 | tf_op jit(solution)/shard_map/ppermute | solution.py:20
  6.6 14.4 %collective-permute-start.5 = (bf16[256,512]{1,0:T(8,128)(2,1)}, bf16[256,512]{1,0:T(8,128)(2,1)S(1)}, u32[]{:S(2)}, u32[]{:S(2)}) collective-permute-start(bf16[256,512]{1,0:T(8,128)(2,1)} %bitcast.43), channel_id=1, source_target_pairs={{0,12},{1,13},{2,14},{3,15},{4,8},{5,9},{6,10},{7,11},{8,4},{9,5},... | collective-permute-start | bytes 786440 | tf_op jit(solution)/shard_map/ppermute | solution.py:20
  6.8 14.1 %collective-permute-start.7 = (bf16[256,512]{1,0:T(8,128)(2,1)}, bf16[256,512]{1,0:T(8,128)(2,1)S(1)}, u32[]{:S(2)}, u32[]{:S(2)}) collective-permute-start(bf16[256,512]{1,0:T(8,128)(2,1)} %bitcast.44), channel_id=1, source_target_pairs={{0,2},{1,3},{2,0},{3,1},{4,6},{5,7},{6,4},{7,5},{8,10},{9,11},{10,... | collective-permute-start | bytes 786440 | tf_op jit(solution)/shard_map/ppermute | solution.py:20
  11.0 11.9 %collective-permute-start.2 = (bf16[256,512]{1,0:T(8,128)(2,1)S(1)}, bf16[256,512]{1,0:T(8,128)(2,1)S(1)}, u32[]{:S(2)}, u32[]{:S(2)}) collective-permute-start(bf16[256,512]{1,0:T(8,128)(2,1)S(1)} %collective-permute-done), channel_id=1, source_target_pairs={{0,4},{1,5},{2,6},{3,7},{4,0},{5,1},{6,2},{7,3},{8,12},{9,13},{10,... | collective-permute-start | bytes 786440 | tf_op jit(solution)/shard_map/ppermute | solution.py:20
  13.2 16.3 %collective-permute-start.4 = (bf16[256,512]{1,0:T(8,128)(2,1)S(1)}, bf16[256,512]{1,0:T(8,128)(2,1)S(1)}, u32[]{:S(2)}, u32[]{:S(2)}) collective-permute-start(bf16[256,512]{1,0:T(8,128)(2,1)S(1)} %collective-permute-done), channel_id=1, source_target_pairs={{0,8},{1,9},{2,10},{3,11},{4,12},{5,13},{6,14},{7,15},{8,0},{9,1},... | collective-permute-start | bytes 786440 | tf_op jit(solution)/shard_map/ppermute | solution.py:20
  19.7 12.4 %collective-permute-start.6 = (bf16[256,512]{1,0:T(8,128)(2,1)S(1)}, bf16[256,512]{1,0:T(8,128)(2,1)S(1)}, u32[]{:S(2)}, u32[]{:S(2)}) collective-permute-start(bf16[256,512]{1,0:T(8,128)(2,1)S(1)} %collective-permute-done), channel_id=1, source_target_pairs={{0,12},{1,13},{2,14},{3,15},{4,8},{5,9},{6,10},{7,11},{8,4},{9,5},... | collective-permute-start | bytes 786440 | tf_op jit(solution)/shard_map/ppermute | solution.py:20
  19.9 20.9 %copy-start.49 = (bf16[8192]{0:T(1024)(128)(2,1)S(1)}, bf16[8192]{0:T(1024)(128)(2,1)}, u32[]{:S(2)}) copy-start(bf16[8192]{0:T(1024)(128)(2,1)} %param.9) | copy-start | bytes 49156
  20.0 159.3 %copy-start.39 = (s32[7]{0:T(128)}, s32[7]{0:T(128)S(1)}, u32[]{:S(2)}) copy-start(s32[7]{0:T(128)S(1)} %stack.31.at_ref) | copy-start | bytes 88
  34.0 11.0 %copy-start = (bf16[8192,512]{1,0:T(8,128)(2,1)S(1)}, bf16[8192,512]{1,0:T(8,128)(2,1)}, u32[]{:S(2)}) copy-start(bf16[8192,512]{1,0:T(8,128)(2,1)} %refs_1_.5) | copy-start | bytes 25165828
  35.2 6.0 %collective-permute-start.8 = (bf16[8,256,512]{2,1,0:T(8,128)(2,1)S(1)}, bf16[8,256,512]{2,1,0:T(8,128)(2,1)S(1)}, u32[]{:S(2)}, u32[]{:S(2)}) collective-permute-start(bf16[8,256,512]{2,1,0:T(8,128)(2,1)S(1)} %get-tuple-element.86.refs_0_.refs_1_), channel_id=1, source_target_pairs={{0,1},{1,0},{2,3},{3,2},{4,5},{5,4},{6,7},{7,6},{8,9},{9,8},{10,11... | collective-permute-start | bytes 6291464 | tf_op jit(solution)/shard_map/ppermute | solution.py:20
  36.3 19.3 %collective-permute-start.10 = (bf16[2,512,256]{2,1,0:T(8,128)(2,1)S(1)}, bf16[2,512,256]{2,1,0:T(8,128)(2,1)S(1)}, u32[]{:S(2)}, u32[]{:S(2)}) collective-permute-start(bf16[2,512,256]{2,1,0:T(8,128)(2,1)S(1)} %get-tuple-element.97), channel_id=1, source_target_pairs={{0,32},{16,48},{32,0},{48,16},{64,96},{80,112},{96,64},{112,80},{1... | collective-permute-start | bytes 1572872 | tf_op jit(solution)/shard_map/ppermute | solution.py:20
  38.3 20.1 %collective-permute-start.11 = (bf16[2,512,256]{2,1,0:T(8,128)(2,1)S(1)}, bf16[2,512,256]{2,1,0:T(8,128)(2,1)S(1)}, u32[]{:S(2)}, u32[]{:S(2)}) collective-permute-start(bf16[2,512,256]{2,1,0:T(8,128)(2,1)S(1)} %get-tuple-element.98), channel_id=1, source_target_pairs={{0,96},{16,112},{32,64},{48,80},{64,32},{80,48},{96,0},{112,16},{1... | collective-permute-start | bytes 1572872 | tf_op jit(solution)/shard_map/ppermute | solution.py:20
  40.8 17.6 %collective-permute-start.12 = (bf16[2,256,512]{2,1,0:T(8,128)(2,1)S(1)}, bf16[2,256,512]{2,1,0:T(8,128)(2,1)S(1)}, u32[]{:S(2)}, u32[]{:S(2)}) collective-permute-start(bf16[2,256,512]{2,1,0:T(8,128)(2,1)S(1)} %get-tuple-element.94.refs_1_.refs_0_), channel_id=1, source_target_pairs={{0,4},{1,5},{2,6},{3,7},{4,0},{5,1},{6,2},{7,3},{8,12},{9,13},{10,... | collective-permute-start | bytes 1572872 | tf_op jit(solution)/shard_map/ppermute | solution.py:20
  40.8 17.6 %collective-permute-start.13 = (bf16[2,256,512]{2,1,0:T(8,128)(2,1)S(1)}, bf16[2,256,512]{2,1,0:T(8,128)(2,1)S(1)}, u32[]{:S(2)}, u32[]{:S(2)}) collective-permute-start(bf16[2,256,512]{2,1,0:T(8,128)(2,1)S(1)} %get-tuple-element.94.refs_1_.refs_0_), channel_id=1, source_target_pairs={{0,12},{1,13},{2,14},{3,15},{4,8},{5,9},{6,10},{7,11},{8,4},{9,5},... | collective-permute-start | bytes 1572872 | tf_op jit(solution)/shard_map/ppermute | solution.py:20
  45.0 57.0 %copy-start.35 = (f32[256,1]{1,0:T(8,128)}, f32[256,1]{1,0:T(8,128)S(1)}, u32[]{:S(2)}) copy-start(f32[256,1]{1,0:T(8,128)S(1)} %get-tuple-element.126.refs_3_) | copy-start | bytes 3076
  45.0 16.3 %slice-start = ((s8[8388608]{0:T(1024)(128)(4,1)}), s8[4194304]{0:T(1024)(128)(4,1)S(1)}, s32[]{:S(2)}) async-start(s8[8388608]{0:T(1024)(128)(4,1)} %bitcast.29), calls=%async_computation.2 | async-start | bytes 8388608
  46.8 14.5 %slice-start.1 = ((s8[8388608]{0:T(1024)(128)(4,1)}), s8[4194304]{0:T(1024)(128)(4,1)S(1)}, s32[]{:S(2)}) async-start(s8[8388608]{0:T(1024)(128)(4,1)} %bitcast.29), calls=%async_computation.3 | async-start | bytes 8388608
  53.5 15.1 %collective-permute-start.15 = (bf16[2,512,256]{2,1,0:T(8,128)(2,1)S(1)}, bf16[2,512,256]{2,1,0:T(8,128)(2,1)S(1)}, u32[]{:S(2)}, u32[]{:S(2)}) collective-permute-start(bf16[2,512,256]{2,1,0:T(8,128)(2,1)S(1)} %get-tuple-element.104), channel_id=1, source_target_pairs={{0,64},{16,80},{32,96},{48,112},{64,0},{80,16},{96,32},{112,48},{1... | collective-permute-start | bytes 1572872 | tf_op jit(solution)/shard_map/ppermute | solution.py:20
  55.6 15.2 %collective-permute-start.16 = (bf16[2,256,512]{2,1,0:T(8,128)(2,1)S(1)}, bf16[2,256,512]{2,1,0:T(8,128)(2,1)S(1)}, u32[]{:S(2)}, u32[]{:S(2)}) collective-permute-start(bf16[2,256,512]{2,1,0:T(8,128)(2,1)S(1)} %get-tuple-element.105), channel_id=1, source_target_pairs={{0,8},{1,9},{2,10},{3,11},{4,12},{5,13},{6,14},{7,15},{8,0},{9,1},... | collective-permute-start | bytes 1572872 | tf_op jit(solution)/shard_map/ppermute | solution.py:20
  58.4 1.3 collective-permute-start.9
  66.9 11.3 %collective-permute-start.14 = (bf16[8,16,8192]{2,1,0:T(8,128)(2,1)S(1)}, bf16[8,16,8192]{2,1,0:T(8,128)(2,1)S(1)}, u32[]{:S(2)}, u32[]{:S(2)}) collective-permute-start(bf16[8,16,8192]{2,1,0:T(8,128)(2,1)S(1)} %get-tuple-element.102), channel_id=1, source_target_pairs={{0,1},{1,0},{2,3},{3,2},{4,5},{5,4},{6,7},{7,6},{8,9},{9,8},{10,11... | collective-permute-start | bytes 6291464 | tf_op jit(solution)/shard_map/ppermute | solution.py:20
  72.0 10.3 %collective-permute-start.23 = (bf16[8,256,512]{2,1,0:T(8,128)(2,1)S(1)}, bf16[8,256,512]{2,1,0:T(8,128)(2,1)S(1)}, u32[]{:S(2)}, u32[]{:S(2)}) collective-permute-start(bf16[8,256,512]{2,1,0:T(8,128)(2,1)S(1)} %get-tuple-element.107.refs_0_), channel_id=1, source_target_pairs={{0,1},{1,0},{2,3},{3,2},{4,5},{5,4},{6,7},{7,6},{8,9},{9,8},{10,11... | collective-permute-start | bytes 6291464 | tf_op jit(solution)/shard_map/ppermute | solution.py:20
  76.3 25.6 %collective-permute-start.25 = (bf16[512,1024]{1,0:T(8,128)(2,1)S(1)}, bf16[512,1024]{1,0:T(8,128)(2,1)S(1)}, u32[]{:S(2)}, u32[]{:S(2)}) collective-permute-start(bf16[512,1024]{1,0:T(8,128)(2,1)S(1)} %get-tuple-element.128), channel_id=1, source_target_pairs={{0,16},{16,0},{32,48},{48,32},{64,80},{80,64},{96,112},{112,96},{1... | collective-permute-start | bytes 3145736 | tf_op jit(solution)/shard_map/ppermute | solution.py:20
  76.4 20.0 %collective-permute-start.20 = (bf16[3,256,512]{2,1,0:T(8,128)(2,1)S(1)}, bf16[3,256,512]{2,1,0:T(8,128)(2,1)S(1)}, u32[]{:S(2)}, u32[]{:S(2)}) collective-permute-start(bf16[3,256,512]{2,1,0:T(8,128)(2,1)S(1)} %get-tuple-element.116), channel_id=1, source_target_pairs={{0,32},{16,48},{32,0},{48,16},{64,96},{80,112},{96,64},{112,80},{1... | collective-permute-start | bytes 2359304 | tf_op jit(solution)/shard_map/ppermute | solution.py:20
  77.5 20.9 %collective-permute-start.22 = (bf16[3,256,512]{2,1,0:T(8,128)(2,1)S(1)}, bf16[3,256,512]{2,1,0:T(8,128)(2,1)S(1)}, u32[]{:S(2)}, u32[]{:S(2)}) collective-permute-start(bf16[3,256,512]{2,1,0:T(8,128)(2,1)S(1)} %get-tuple-element.118), channel_id=1, source_target_pairs={{0,96},{16,112},{32,64},{48,80},{64,32},{80,48},{96,0},{112,16},{1... | collective-permute-start | bytes 2359304 | tf_op jit(solution)/shard_map/ppermute | solution.py:20
  80.7 21.2 %collective-permute-start.17 = (bf16[2,16,8192]{2,1,0:T(8,128)(2,1)S(1)}, bf16[2,16,8192]{2,1,0:T(8,128)(2,1)S(1)}, u32[]{:S(2)}, u32[]{:S(2)}) collective-permute-start(bf16[2,16,8192]{2,1,0:T(8,128)(2,1)S(1)} %get-tuple-element.112), channel_id=1, source_target_pairs={{0,4},{1,5},{2,6},{3,7},{4,0},{5,1},{6,2},{7,3},{8,12},{9,13},{10,... | collective-permute-start | bytes 1572872 | tf_op jit(solution)/shard_map/ppermute | solution.py:20
  82.2 19.8 %collective-permute-start.19 = (bf16[2,16,8192]{2,1,0:T(8,128)(2,1)S(1)}, bf16[2,16,8192]{2,1,0:T(8,128)(2,1)S(1)}, u32[]{:S(2)}, u32[]{:S(2)}) collective-permute-start(bf16[2,16,8192]{2,1,0:T(8,128)(2,1)S(1)} %get-tuple-element.114), channel_id=1, source_target_pairs={{0,12},{1,13},{2,14},{3,15},{4,8},{5,9},{6,10},{7,11},{8,4},{9,5},... | collective-permute-start | bytes 1572872 | tf_op jit(solution)/shard_map/ppermute | solution.py:20
  89.8 13.7 %copy-start.43 = (bf16[16,8192]{1,0:T(8,128)(2,1)}, bf16[16,8192]{1,0:T(8,128)(2,1)S(1)}, u32[]{:S(2)}) copy-start(bf16[16,8192]{1,0:T(8,128)(2,1)S(1)} %get-tuple-element.152.refs_4_) | copy-start | bytes 786436
  96.4 5.5 %collective-permute-start.24 = (bf16[256,128]{1,0:T(8,128)(2,1)S(1)}, bf16[256,128]{1,0:T(8,128)(2,1)S(1)}, u32[]{:S(2)}, u32[]{:S(2)}) collective-permute-start(bf16[256,128]{1,0:T(8,128)(2,1)S(1)} %get-tuple-element.125), channel_id=1, source_target_pairs={{0,1},{1,0},{2,3},{3,2},{4,5},{5,4},{6,7},{7,6},{8,9},{9,8},{10,11... | collective-permute-start | bytes 196616 | tf_op jit(solution)/shard_map/ppermute | solution.py:20
  110.4 4.5 %collective-permute-start.27 = (bf16[8,16,8192]{2,1,0:T(8,128)(2,1)S(1)}, bf16[8,16,8192]{2,1,0:T(8,128)(2,1)S(1)}, u32[]{:S(2)}, u32[]{:S(2)}) collective-permute-start(bf16[8,16,8192]{2,1,0:T(8,128)(2,1)S(1)} %get-tuple-element.134), channel_id=1, source_target_pairs={{0,1},{1,0},{2,3},{3,2},{4,5},{5,4},{6,7},{7,6},{8,9},{9,8},{10,11... | collective-permute-start | bytes 6291464 | tf_op jit(solution)/shard_map/ppermute | solution.py:20
  110.4 33.4 %collective-permute-start.21 = (bf16[3,256,512]{2,1,0:T(8,128)(2,1)}, bf16[3,256,512]{2,1,0:T(8,128)(2,1)S(1)}, u32[]{:S(2)}, u32[]{:S(2)}) collective-permute-start(bf16[3,256,512]{2,1,0:T(8,128)(2,1)} %get-tuple-element.117), channel_id=1, source_target_pairs={{0,64},{16,80},{32,96},{48,112},{64,0},{80,16},{96,32},{112,48},{1... | collective-permute-start | bytes 2359304 | tf_op jit(solution)/shard_map/ppermute | solution.py:20
  111.6 32.2 %collective-permute-start.18 = (bf16[2,16,8192]{2,1,0:T(8,128)(2,1)}, bf16[2,16,8192]{2,1,0:T(8,128)(2,1)S(1)}, u32[]{:S(2)}, u32[]{:S(2)}) collective-permute-start(bf16[2,16,8192]{2,1,0:T(8,128)(2,1)} %get-tuple-element.113), channel_id=1, source_target_pairs={{0,8},{1,9},{2,10},{3,11},{4,12},{5,13},{6,14},{7,15},{8,0},{9,1},... | collective-permute-start | bytes 1572872 | tf_op jit(solution)/shard_map/ppermute | solution.py:20
  118.5 25.4 %collective-permute-start.28 = (bf16[2,16,8192]{2,1,0:T(8,128)(2,1)}, bf16[2,16,8192]{2,1,0:T(8,128)(2,1)S(1)}, u32[]{:S(2)}, u32[]{:S(2)}) collective-permute-start(bf16[2,16,8192]{2,1,0:T(8,128)(2,1)} %get-tuple-element.137), channel_id=1, source_target_pairs={{0,4},{1,5},{2,6},{3,7},{4,0},{5,1},{6,2},{7,3},{8,12},{9,13},{10,... | collective-permute-start | bytes 1572872 | tf_op jit(solution)/shard_map/ppermute | solution.py:20
  118.9 25.0 %collective-permute-start.29 = (bf16[2,16,8192]{2,1,0:T(8,128)(2,1)}, bf16[2,16,8192]{2,1,0:T(8,128)(2,1)S(1)}, u32[]{:S(2)}, u32[]{:S(2)}) collective-permute-start(bf16[2,16,8192]{2,1,0:T(8,128)(2,1)} %get-tuple-element.138), channel_id=1, source_target_pairs={{0,12},{1,13},{2,14},{3,15},{4,8},{5,9},{6,10},{7,11},{8,4},{9,5},... | collective-permute-start | bytes 1572872 | tf_op jit(solution)/shard_map/ppermute | solution.py:20
  121.0 22.9 %collective-permute-start.26 = (bf16[256,640]{1,0:T(8,128)(2,1)}, bf16[256,640]{1,0:T(8,128)(2,1)}, u32[]{:S(2)}, u32[]{:S(2)}) collective-permute-start(bf16[256,640]{1,0:T(8,128)(2,1)} %get-tuple-element.129), channel_id=1, source_target_pairs={{0,16},{16,0},{32,48},{48,32},{64,80},{80,64},{96,112},{112,96},{1... | collective-permute-start | bytes 983048 | tf_op jit(solution)/shard_map/ppermute | solution.py:20
  152.1 4.2 %collective-permute-start.30 = (bf16[8,256,512]{2,1,0:T(8,128)(2,1)S(1)}, bf16[8,256,512]{2,1,0:T(8,128)(2,1)S(1)}, u32[]{:S(2)}, u32[]{:S(2)}) collective-permute-start(bf16[8,256,512]{2,1,0:T(8,128)(2,1)S(1)} %get-tuple-element.141), channel_id=1, source_target_pairs={{0,1},{1,0},{2,3},{3,2},{4,5},{5,4},{6,7},{7,6},{8,9},{9,8},{10,11... | collective-permute-start | bytes 6291464 | tf_op jit(solution)/shard_map/ppermute | solution.py:20
  152.2 27.0 %collective-permute-start.35 = (bf16[2,256,640]{2,1,0:T(8,128)(2,1)}, bf16[2,256,640]{2,1,0:T(8,128)(2,1)}, u32[]{:S(2)}, u32[]{:S(2)}) collective-permute-start(bf16[2,256,640]{2,1,0:T(8,128)(2,1)} %get-tuple-element.154.refs_3_.refs_2_), channel_id=1, source_target_pairs={{0,32},{16,48},{32,0},{48,16},{64,96},{80,112},{96,64},{112,80},{1... | collective-permute-start | bytes 1966088 | tf_op jit(solution)/shard_map/ppermute | solution.py:20
  152.8 26.4 %collective-permute-start.36 = (bf16[2,256,640]{2,1,0:T(8,128)(2,1)}, bf16[2,256,640]{2,1,0:T(8,128)(2,1)}, u32[]{:S(2)}, u32[]{:S(2)}) collective-permute-start(bf16[2,256,640]{2,1,0:T(8,128)(2,1)} %get-tuple-element.154.refs_3_.refs_2_), channel_id=1, source_target_pairs={{0,96},{16,112},{32,64},{48,80},{64,32},{80,48},{96,0},{112,16},{1... | collective-permute-start | bytes 1966088 | tf_op jit(solution)/shard_map/ppermute | solution.py:20
  154.9 15.5 %collective-permute-start.32 = (bf16[2,16,8192]{2,1,0:T(8,128)(2,1)}, bf16[2,16,8192]{2,1,0:T(8,128)(2,1)}, u32[]{:S(2)}, u32[]{:S(2)}) collective-permute-start(bf16[2,16,8192]{2,1,0:T(8,128)(2,1)} %get-tuple-element.148), channel_id=1, source_target_pairs={{0,8},{1,9},{2,10},{3,11},{4,12},{5,13},{6,14},{7,15},{8,0},{9,1},... | collective-permute-start | bytes 1572872 | tf_op jit(solution)/shard_map/ppermute | solution.py:20
  156.1 30.8 %collective-permute-start.34 = (bf16[2,512,1024]{2,1,0:T(8,128)(2,1)}, bf16[2,512,1024]{2,1,0:T(8,128)(2,1)}, u32[]{:S(2)}, u32[]{:S(2)}) collective-permute-start(bf16[2,512,1024]{2,1,0:T(8,128)(2,1)} %get-tuple-element.153.refs_0_), channel_id=1, source_target_pairs={{0,1},{1,0},{2,3},{3,2},{4,5},{5,4},{6,7},{7,6},{8,9},{9,8},{10,11... | collective-permute-start | bytes 6291464 | tf_op jit(solution)/shard_map/ppermute | solution.py:20
  163.0 22.2 %collective-permute-start.31 = (bf16[16,8192]{1,0:T(8,128)(2,1)}, bf16[16,8192]{1,0:T(8,128)(2,1)}, u32[]{:S(2)}, u32[]{:S(2)}) collective-permute-start(bf16[16,8192]{1,0:T(8,128)(2,1)} %get-tuple-element.146), channel_id=1, source_target_pairs={{0,2},{1,3},{2,0},{3,1},{4,6},{5,7},{6,4},{7,5},{8,10},{9,11},{10,... | collective-permute-start | bytes 786440 | tf_op jit(solution)/shard_map/ppermute | solution.py:20
  166.9 12.3 %copy-start.4 = (bf16[8,256,512]{2,1,0:T(8,128)(2,1)S(1)}, bf16[8,256,512]{2,1,0:T(8,128)(2,1)}, u32[]{:S(2)}) copy-start(bf16[8,256,512]{2,1,0:T(8,128)(2,1)} %copy-done.3) | copy-start | bytes 6291460
  176.3 33.9 %collective-permute-start.33 = (bf16[16,8192]{1,0:T(8,128)(2,1)S(1)}, bf16[16,8192]{1,0:T(8,128)(2,1)S(1)}, u32[]{:S(2)}, u32[]{:S(2)}) collective-permute-start(bf16[16,8192]{1,0:T(8,128)(2,1)S(1)} %get-tuple-element.151), channel_id=1, source_target_pairs={{0,2},{1,3},{2,0},{3,1},{4,6},{5,7},{6,4},{7,5},{8,10},{9,11},{10,... | collective-permute-start | bytes 786440 | tf_op jit(solution)/shard_map/ppermute | solution.py:20
  183.5 16.9 %copy-start.46 = (f32[8,128]{1,0:T(8,128)}, f32[8,128]{1,0:T(8,128)S(1)}, u32[]{:S(2)}) copy-start(f32[8,128]{1,0:T(8,128)S(1)} %get-tuple-element.157.refs_7_) | copy-start | bytes 12292
  183.5 16.9 %collective-permute-start.37 = (bf16[2,256,640]{2,1,0:T(8,128)(2,1)S(1)}, bf16[2,256,640]{2,1,0:T(8,128)(2,1)S(1)}, u32[]{:S(2)}, u32[]{:S(2)}) collective-permute-start(bf16[2,256,640]{2,1,0:T(8,128)(2,1)S(1)} %get-tuple-element.156), channel_id=1, source_target_pairs={{0,64},{16,80},{32,96},{48,112},{64,0},{80,16},{96,32},{112,48},{1... | collective-permute-start | bytes 1966088 | tf_op jit(solution)/shard_map/ppermute | solution.py:20
  184.9 25.2 %collective-permute-start.38 = (bf16[512,1024]{1,0:T(8,128)(2,1)}, bf16[512,1024]{1,0:T(8,128)(2,1)S(1)}, u32[]{:S(2)}, u32[]{:S(2)}) collective-permute-start(bf16[512,1024]{1,0:T(8,128)(2,1)} %get-tuple-element.159), channel_id=1, source_target_pairs={{0,16},{16,0},{32,48},{48,32},{64,80},{80,64},{96,112},{112,96},{1... | collective-permute-start | bytes 3145736 | tf_op jit(solution)/shard_map/ppermute | solution.py:20
  (43 other events, 159.4 us)

commit v4 on v3

--- a/solution.py
+++ b/solution.py
@@ -597,22 +597,27 @@
     def kernel(at_ref, *refs):
         own_ref, other_ref, row_refs, gain_ref = *refs[:2], refs[2:6], refs[6]
         q_out, kv_out, acc, joined = refs[7:]
-        half = pl.program_id(0)
-
-        @pl.when(half == 0)
+        half, x_at = pl.program_id(0), pl.program_id(1)
+
+        @pl.when((half == 0) & (x_at == 0))
         def _():
             for k in range(4):
                 for x in range(2):
                     joined[x, k * length : (k + 1) * length, :] = row_refs[k][x]
 
         def add(ref):
-            acc[...] = nn(ref[0], joined[0])
-            acc[...] += nn(ref[1], joined[1])
+            @pl.when(x_at == 0)
+            def _():
+                acc[...] = nn(ref[0], joined[0])
+
+            @pl.when(x_at == 1)
+            def _():
+                total = acc[...] + nn(ref[0], joined[1])
+                q_out[...] = total[:, :q_width] * gain_ref[...]
+                kv_out[...] = total[:, q_width:] * gain_ref[...]
 
         pl.when(half == 0)(lambda: add(own_ref))
         pl.when(half == 1)(lambda: add(other_ref))
-        q_out[...] = acc[:, :q_width] * gain_ref[...]
-        kv_out[...] = acc[:, q_width:] * gain_ref[...]
 
     def side(h, at):
         return jnp.where(h == 0, at[CORE], 1 - at[CORE])
@@ -621,19 +626,22 @@
         kernel,
         "q_gradient",
         order,
-        [whole(own), whole(other)]
+        [
+            (own, pl.BlockSpec((1, width, wide), lambda h, x, at: (jnp.where(h == 0, x, 1), 0, 0))),
+            (other, pl.BlockSpec((1, width, wide), lambda h, x, at: (jnp.where(h == 0, 0, x), 0, 0))),
+        ]
         + [whole(a) for a in rows]
         + [
-            (gain_column, pl.BlockSpec((width, 1), lambda h, at: (side(h, at), 0))),
+            (gain_column, pl.BlockSpec((width, 1), lambda h, x, at: (side(h, at), 0))),
         ],
         [
             (
                 shape((2 * width, size), f32),
-                pl.BlockSpec((width, size), lambda h, at: (side(h, at), 0)),
+                pl.BlockSpec((width, size), lambda h, x, at: (side(h, at), 0)),
             )
             for size in (q_width, head)
         ],
-        grid=(2,),
+        grid=(2, 2),
         scratch=[pltpu.VMEM((width, total), f32), pltpu.VMEM((2, 4 * length, total), bf16)],
     )
 

time: 216 us -> 216 us (level)
  no operation moved by 1% of the time
where the time goes in v4:
time: 216 us; the launch traced here: 215 us
  Pallas kernels  74.3 us (34%)
  waiting for transfers between devices  50.2 us (23%)
  starting transfers between devices  48 us (22%)
  blocking collectives  22.4 us (10%)
  local copies, waits for them, and re-layouts  17.3 us (8%)
    pallas_call x25, Pallas kernels, call(): pl.pallas_call(body, grid_spec=pltpu.PrefetchScalarGridSpec(num_scalar_pr...  74.3 us
    ppermute x39, waiting for transfers between devices, partner(): lax.ppermute(array, axis, [(i, i ^ bits) for i in range(lax.axis_size(axi...  50.2 us
    ppermute x39, starting transfers between devices, partner(): lax.ppermute(array, axis, [(i, i ^ bits) for i in range(lax.axis_size(axi...  48 us
    unnamed x104, local copies, waits for them, and re-layouts  16.2 us
    all_to_all x1, blocking collectives, on_device(): lax.all_to_all(jnp.broadcast_to(gain_part[None], (16, 1, 2 * width)), 'te...  11.2 us
    all_to_all x1, blocking collectives, on_device(): lax.all_to_all(gain_part, 'dp', 0, 0, tiled=True)  11.1 us
  transfers between devices with their start and end apart: 39, of which 15 were waited for; matrix products, arithmetic and copies ran while one was open for 1% of the time, Pallas kernels for 26%

profile of v4, /device:TPU:6, one launch (start us, length us, event | category | flops | bytes accessed | tf_op | source)
XLA Modules:
  0.0 215.3 jit_solution(2018934257244583854)
XLA Ops:
  2.1 1.6 collective-permute-start.1
  3.7 2.9 %collective-permute-start.3 = (bf16[256,512]{1,0:T(8,128)(2,1)}, bf16[256,512]{1,0:T(8,128)(2,1)S(1)}, u32[]{:S(2)}, u32[]{:S(2)}) collective-permute-start(bf16[256,512]{1,0:T(8,128)(2,1)} %bitcast.42), channel_id=1, source_target_pairs={{0,8},{1,9},{2,10},{3,11},{4,12},{5,13},{6,14},{7,15},{8,0},{9,1},... | collective-permute-start | bytes 786440 | tf_op jit(solution)/shard_map/ppermute | solution.py:20
  6.8 2.1 collective-permute-start.7
  8.9 2.0 collective-permute-done
  11.0 2.2 %collective-permute-start.2 = (bf16[256,512]{1,0:T(8,128)(2,1)S(1)}, bf16[256,512]{1,0:T(8,128)(2,1)S(1)}, u32[]{:S(2)}, u32[]{:S(2)}) collective-permute-start(bf16[256,512]{1,0:T(8,128)(2,1)S(1)} %collective-permute-done), channel_id=1, source_target_pairs={{0,4},{1,5},{2,6},{3,7},{4,0},{5,1},{6,2},{7,3},{8,12},{9,13},{10,... | collective-permute-start | bytes 786440 | tf_op jit(solution)/shard_map/ppermute | solution.py:20
  13.2 2.3 %collective-permute-start.4 = (bf16[256,512]{1,0:T(8,128)(2,1)S(1)}, bf16[256,512]{1,0:T(8,128)(2,1)S(1)}, u32[]{:S(2)}, u32[]{:S(2)}) collective-permute-start(bf16[256,512]{1,0:T(8,128)(2,1)S(1)} %collective-permute-done), channel_id=1, source_target_pairs={{0,8},{1,9},{2,10},{3,11},{4,12},{5,13},{6,14},{7,15},{8,0},{9,1},... | collective-permute-start | bytes 786440 | tf_op jit(solution)/shard_map/ppermute | solution.py:20
  15.5 4.2 %collective-permute-done.3 = bf16[256,512]{1,0:T(8,128)(2,1)S(1)} collective-permute-done((bf16[256,512]{1,0:T(8,128)(2,1)}, bf16[256,512]{1,0:T(8,128)(2,1)S(1)}, u32[]{:S(2)}, u32[]{:S(2)}) %collective-permute-start.3) | collective-permute-done | bytes 262176 | tf_op jit(solution)/shard_map/ppermute | solution.py:20
  21.0 1.9 collective-permute-done.2
  22.8 6.7 %collective-permute-done.4 = bf16[256,512]{1,0:T(8,128)(2,1)S(1)} collective-permute-done((bf16[256,512]{1,0:T(8,128)(2,1)S(1)}, bf16[256,512]{1,0:T(8,128)(2,1)S(1)}, u32[]{:S(2)}, u32[]{:S(2)}) %collective-permute-start.4) | collective-permute-done | bytes 262176 | tf_op jit(solution)/shard_map/ppermute | solution.py:20
  29.5 2.5 %collective-permute-done.6 = bf16[256,512]{1,0:T(8,128)(2,1)S(1)} collective-permute-done((bf16[256,512]{1,0:T(8,128)(2,1)S(1)}, bf16[256,512]{1,0:T(8,128)(2,1)S(1)}, u32[]{:S(2)}, u32[]{:S(2)}) %collective-permute-start.6) | collective-permute-done | bytes 262176 | tf_op jit(solution)/shard_map/ppermute | solution.py:20
  36.3 2.0 collective-permute-start.10
  38.3 2.5 %collective-permute-start.11 = (bf16[2,512,256]{2,1,0:T(8,128)(2,1)S(1)}, bf16[2,512,256]{2,1,0:T(8,128)(2,1)S(1)}, u32[]{:S(2)}, u32[]{:S(2)}) collective-permute-start(bf16[2,512,256]{2,1,0:T(8,128)(2,1)S(1)} %get-tuple-element.98), channel_id=1, source_target_pairs={{0,96},{16,112},{32,64},{48,80},{64,32},{80,48},{96,0},{112,16},{1... | collective-permute-start | bytes 1572872 | tf_op jit(solution)/shard_map/ppermute | solution.py:20
  41.2 3.7 %norm.1 = (bf16[256,8192]{1,0:T(8,128)(2,1)S(1)}, f32[256,1]{1,0:T(8,128)S(1)}, bf16[16,8192]{1,0:T(8,128)(2,1)S(1)}, f32[8,128]{1,0:T(8,128)S(1)}) custom-call(s32[7]{0:T(128)S(1)} %stack.31.at_ref, f32[1,8192]{1,0:T(1,128)S(1)} %bitcast.37, bf16[8,256,512]{2,1,0:T(8,128)(2,1)S(1)} %get-tuple-element.86.refs_0_.refs_1_, ...), custom_call_target="tpu_custom_call" | custom-call | flops 1 | bytes 1 | tf_op jit(solution)/shard_map/norm/pallas_call | solution.py:43
  45.0 1.7 copy-done.1
  46.8 5.9 %project.1 = (bf16[256,512]{1,0:T(8,128)(2,1)S(1)}, bf16[256,128]{1,0:T(8,128)(2,1)S(1)}, f32[8,128]{1,0:T(8,128)S(1)}) custom-call(s32[7]{0:T(128)S(1)} %stack.31.at_ref, bf16[256,8192]{1,0:T(8,128)(2,1)S(1)} %get-tuple-element.90.refs_0_.refs_3_, bf16[8192,512]{1,0:T(8,128)(2,1)S(1)} %copy-done, bf16[8192,128]{1,0:T(8,128)(2,1)S(1)} %copy-done.1, ...), custom_call_target="tpu_custom_call" | custom-call | flops 1 | bytes 1 | tf_op jit(solution)/shard_map/project/pallas_call | solution.py:43
  53.5 2.2 %collective-permute-start.15 = (bf16[2,512,256]{2,1,0:T(8,128)(2,1)S(1)}, bf16[2,512,256]{2,1,0:T(8,128)(2,1)S(1)}, u32[]{:S(2)}, u32[]{:S(2)}) collective-permute-start(bf16[2,512,256]{2,1,0:T(8,128)(2,1)S(1)} %get-tuple-element.104), channel_id=1, source_target_pairs={{0,64},{16,80},{32,96},{48,112},{64,0},{80,16},{96,32},{112,48},{1... | collective-permute-start | bytes 1572872 | tf_op jit(solution)/shard_map/ppermute | solution.py:20
  55.6 2.8 %collective-permute-start.16 = (bf16[2,256,512]{2,1,0:T(8,128)(2,1)S(1)}, bf16[2,256,512]{2,1,0:T(8,128)(2,1)S(1)}, u32[]{:S(2)}, u32[]{:S(2)}) collective-permute-start(bf16[2,256,512]{2,1,0:T(8,128)(2,1)S(1)} %get-tuple-element.105), channel_id=1, source_target_pairs={{0,8},{1,9},{2,10},{3,11},{4,12},{5,13},{6,14},{7,15},{8,0},{9,1},... | collective-permute-start | bytes 1572872 | tf_op jit(solution)/shard_map/ppermute | solution.py:20
  59.7 1.7 attend.1
  61.3 5.5 %mix.1 = (bf16[8,16,8192]{2,1,0:T(8,128)(2,1)S(1)}, bf16[8,16,8192]{2,1,0:T(8,128)(2,1)S(1)}, f32[8,128]{1,0:T(8,128)S(1)}) custom-call(s32[7]{0:T(128)S(1)} %stack.31.at_ref, bf16[256,512]{1,0:T(8,128)(2,1)S(1)} %get-tuple-element.99.refs_0_.refs_1_, bf16[512,8192]{1,0:T(8,128)(2,1)S(1)} %bitcast.30, f32[8,128]{1,0:T(8,128)S(1)} %get-tuple-element.100.refs_2_), custom_call_target="tpu_custom_call" | custom-call | flops 1 | bytes 1 | tf_op jit(solution)/shard_map/mix/pallas_call | solution.py:43
  68.5 2.3 %collective-permute-done.16.refs_2_ = bf16[2,256,512]{2,1,0:T(8,128)(2,1)S(1)} collective-permute-done((bf16[2,256,512]{2,1,0:T(8,128)(2,1)S(1)}, bf16[2,256,512]{2,1,0:T(8,128)(2,1)S(1)}, u32[]{:S(2)}, u32[]{:S(2)}) %collective-permute-start.16) | collective-permute-done | bytes 524320 | tf_op jit(solution)/shard_map/ppermute | solution.py:20
  72.0 2.1 pick_cot.1
  78.2 2.5 %pair_sum.2 = (bf16[2,16,8192]{2,1,0:T(8,128)(2,1)S(1)}, bf16[2,16,8192]{2,1,0:T(8,128)(2,1)S(1)}, bf16[2,16,8192]{2,1,0:T(8,128)(2,1)}, bf16[2,16,8192]{2,1,0:T(8,128)(2,1)S(1)}, f32[8,128]{1,0:T(8,128)S(1)}) custom-call(s32[7]{0:T(128)S(1)} %stack.31.at_ref, bf16[8,16,8192]{2,1,0:T(8,128)(2,1)S(1)} %get-tuple-element.101.refs_0_, ...), custom_call_target="tpu_custom_call" | custom-call | flops 1 | bytes 1 | tf_op jit(solution)/shard_map/pair_sum/pallas_call | solution.py:43
  82.2 2.3 %collective-permute-start.19 = (bf16[2,16,8192]{2,1,0:T(8,128)(2,1)S(1)}, bf16[2,16,8192]{2,1,0:T(8,128)(2,1)S(1)}, u32[]{:S(2)}, u32[]{:S(2)}) collective-permute-start(bf16[2,16,8192]{2,1,0:T(8,128)(2,1)S(1)} %get-tuple-element.114), channel_id=1, source_target_pairs={{0,12},{1,13},{2,14},{3,15},{4,8},{5,9},{6,10},{7,11},{8,4},{9,5},... | collective-permute-start | bytes 1572872 | tf_op jit(solution)/shard_map/ppermute | solution.py:20
  84.5 5.2 %out_gradient.1 = (bf16[256,512]{1,0:T(8,128)(2,1)S(1)}, bf16[16,8192]{1,0:T(8,128)(2,1)S(1)}, f32[8,128]{1,0:T(8,128)S(1)}) custom-call(s32[7]{0:T(128)S(1)} %stack.31.at_ref, bf16[8,256,512]{2,1,0:T(8,128)(2,1)S(1)} %get-tuple-element.107.refs_0_, bf16[8,256,512]{2,1,0:T(8,128)(2,1)S(1)} %collective-permute-done.23.refs_1_, ...), custom_call_target="tpu_custom_call" | custom-call | flops 1 | bytes 1 | tf_op jit(solution)/shard_map/out_gradient/pallas_call | solution.py:43
  89.8 2.3 %attend_gradient.1 = (bf16[256,512]{1,0:T(8,128)(2,1)S(1)}, f32[256,128]{1,0:T(8,128)S(1)}, bf16[256,128]{1,0:T(8,128)(2,1)S(1)}, f32[8,128]{1,0:T(8,128)S(1)}) custom-call(s32[7]{0:T(128)S(1)} %stack.31.at_ref, bf16[256,512]{1,0:T(8,128)(2,1)S(1)} %get-tuple-element.120.refs_0_, f32[4,256,256]{2,1,0:T(8,128)S(1)} %get-tuple-element.121.refs_1_, ...), custom_call_target="tpu_custom_call" | custom-call | flops 1 | bytes 1 | tf_op jit(solution)/shard_map/attend_gradient/pallas_call | solution.py:43
  92.1 4.4 %collective-permute-done.20.refs_7_.refs_1_ = bf16[3,256,512]{2,1,0:T(8,128)(2,1)S(1)} collective-permute-done((bf16[3,256,512]{2,1,0:T(8,128)(2,1)S(1)}, bf16[3,256,512]{2,1,0:T(8,128)(2,1)S(1)}, u32[]{:S(2)}, u32[]{:S(2)}) %collective-permute-start.20) | collective-permute-done | bytes 786464 | tf_op jit(solution)/shard_map/ppermute | solution.py:20
  96.4 1.9 collective-permute-done.22.refs_8_.refs_3_
  98.4 3.6 %collective-permute-done.25.refs_11_ = bf16[512,1024]{1,0:T(8,128)(2,1)S(1)} collective-permute-done((bf16[512,1024]{1,0:T(8,128)(2,1)S(1)}, bf16[512,1024]{1,0:T(8,128)(2,1)S(1)}, u32[]{:S(2)}, u32[]{:S(2)}) %collective-permute-start.25) | collective-permute-done | bytes 1048608 | tf_op jit(solution)/shard_map/ppermute | solution.py:20
  104.1 6.3 %norm_gradient.1 = (bf16[8,16,8192]{2,1,0:T(8,128)(2,1)S(1)}, bf16[8,16,8192]{2,1,0:T(8,128)(2,1)S(1)}, f32[8,1,1024]{2,1,0:T(1,128)S(1)}, f32[8,128]{1,0:T(8,128)S(1)}) custom-call(s32[7]{0:T(128)S(1)} %stack.31.at_ref, bf16[256,640]{1,0:T(8,128)(2,1)S(1)} %get-tuple-element.131.refs_0_, bf16[8192,512]{1,0:T(8,128)(2,1)S(1)} %copy-done, ...), custom_call_target="tpu_custom_call" | custom-call | flops 1 | bytes 1 | tf_op jit(solution)/shard_map/norm_gradient/pallas_call | solution.py:43
  111.6 3.2 %collective-permute-start.18 = (bf16[2,16,8192]{2,1,0:T(8,128)(2,1)}, bf16[2,16,8192]{2,1,0:T(8,128)(2,1)S(1)}, u32[]{:S(2)}, u32[]{:S(2)}) collective-permute-start(bf16[2,16,8192]{2,1,0:T(8,128)(2,1)} %get-tuple-element.113), channel_id=1, source_target_pairs={{0,8},{1,9},{2,10},{3,11},{4,12},{5,13},{6,14},{7,15},{8,0},{9,1},... | collective-permute-start | bytes 1572872 | tf_op jit(solution)/shard_map/ppermute | solution.py:20
  114.9 2.8 %pair_sum.3 = (bf16[2,16,8192]{2,1,0:T(8,128)(2,1)S(1)}, bf16[2,16,8192]{2,1,0:T(8,128)(2,1)}, bf16[2,16,8192]{2,1,0:T(8,128)(2,1)}, bf16[2,16,8192]{2,1,0:T(8,128)(2,1)}, f32[8,128]{1,0:T(8,128)S(1)}) custom-call(s32[7]{0:T(128)S(1)} %stack.31.at_ref, bf16[8,16,8192]{2,1,0:T(8,128)(2,1)S(1)} %get-tuple-element.133.refs_0_, ...), custom_call_target="tpu_custom_call" | custom-call | flops 1 | bytes 1 | tf_op jit(solution)/shard_map/pair_sum/pallas_call | solution.py:43
  118.9 2.1 collective-permute-start.29
  121.3 11.1 %all_to_all.10 = f32[8,1,1024]{2,1,0:T(1,128)S(1)} all-to-all(f32[8,1,1024]{2,1,0:T(1,128)S(1)} %get-tuple-element.139), channel_id=1, replica_groups=mesh['dp'=8,'tensor'=16] {'dp'}, dimensions={0} | all-to-all | bytes 65536 | tf_op jit(solution)/shard_map/all_to_all | solution.py:777
  132.5 11.2 %all_to_all.11 = f32[16,1,1024]{2,1,0:T(1,128)S(1)} all-to-all(f32[16,1,1024]{2,1,0:T(1,128)S(1)} %broadcast_in_dim.67), channel_id=1, replica_groups=mesh['dp'=8,'tensor'=16] {'tensor'}, dimensions={0} | all-to-all | bytes 131072 | tf_op jit(solution)/shard_map/all_to_all | solution.py:778
  144.0 2.0 copy-done.26
  146.0 3.6 %stack_dqkv.1 = (bf16[2,256,640]{2,1,0:T(8,128)(2,1)}, bf16[2,512,1024]{2,1,0:T(8,128)(2,1)}, f32[8,128]{1,0:T(8,128)S(1)}) custom-call(s32[7]{0:T(128)S(1)} %stack.31.at_ref, bf16[1,256,640]{2,1,0:T(8,128)(2,1)} %bitcast.18.refs_0_, bf16[1,256,640]{2,1,0:T(8,128)(2,1)} %bitcast.19.refs_1_, bf16[1,512,1024]{2,1,0:T(8,128)(2,1)S(1)} %bitcast.36, ...), custom_call_target="tpu_custom_call" | custom-call | flops 1 | bytes 1 | tf_op jit(solution)/shard_map/stack_dqkv/pallas_call | solution.py:43
  152.8 2.1 collective-permute-start.36
  156.3 2.4 %out_keep.1 = (f32[512,1024]{1,0:T(8,128)S(1)}, f32[8,128]{1,0:T(8,128)S(1)}) custom-call(s32[7]{0:T(128)S(1)} %stack.31.at_ref, bf16[4,2,256,512]{3,2,1,0:T(8,128)(2,1)S(1)} %bitcast.31, bf16[4,2,256,512]{3,2,1,0:T(8,128)(2,1)S(1)} %bitcast.33, bf16[4,256,512]{2,1,0:T(8,128)(2,1)S(1)} %get-tuple-element.142.refs_2_, f32[8,128]{1,0:T(8,128)S(1)} %get-tuple-element.143.refs_3_), custom_call_target="tpu_custom_call" | custom-call | flops 1 | bytes 1 | tf_op jit(solution)/shard_map/out_keep/pallas_call | solution.py:43
  160.0 2.2 %ring_sum.2 = (f32[16,8192]{1,0:T(8,128)S(1)}, bf16[16,8192]{1,0:T(8,128)(2,1)}, f32[8,128]{1,0:T(8,128)S(1)}) custom-call(s32[7]{0:T(128)S(1)} %stack.31.at_ref, bf16[2,16,8192]{2,1,0:T(8,128)(2,1)S(1)} %copy-done.32, bf16[2,16,8192]{2,1,0:T(8,128)(2,1)S(1)} %copy-done.14, bf16[2,16,8192]{2,1,0:T(8,128)(2,1)S(1)} %copy-done.22, ...), custom_call_target="tpu_custom_call" | custom-call | flops 1 | bytes 1 | tf_op jit(solution)/shard_map/ring_sum/pallas_call | solution.py:43
  163.0 2.9 %collective-permute-start.31 = (bf16[16,8192]{1,0:T(8,128)(2,1)}, bf16[16,8192]{1,0:T(8,128)(2,1)}, u32[]{:S(2)}, u32[]{:S(2)}) collective-permute-start(bf16[16,8192]{1,0:T(8,128)(2,1)} %get-tuple-element.146), channel_id=1, source_target_pairs={{0,2},{1,3},{2,0},{3,1},{4,6},{5,7},{6,4},{7,5},{8,10},{9,11},{10,... | collective-permute-start | bytes 786440 | tf_op jit(solution)/shard_map/ppermute | solution.py:20
  166.9 3.5 %collective-permute-done.32.refs_2_ = bf16[2,16,8192]{2,1,0:T(8,128)(2,1)} collective-permute-done((bf16[2,16,8192]{2,1,0:T(8,128)(2,1)}, bf16[2,16,8192]{2,1,0:T(8,128)(2,1)}, u32[]{:S(2)}, u32[]{:S(2)}) %collective-permute-start.32) | collective-permute-done | bytes 524320 | tf_op jit(solution)/shard_map/ppermute | solution.py:20
  173.5 2.7 %ring_sum.3 = (f32[16,8192]{1,0:T(8,128)S(1)}, bf16[16,8192]{1,0:T(8,128)(2,1)S(1)}, f32[8,128]{1,0:T(8,128)S(1)}) custom-call(s32[7]{0:T(128)S(1)} %stack.31.at_ref, bf16[2,16,8192]{2,1,0:T(8,128)(2,1)S(1)} %copy-done.34, bf16[2,16,8192]{2,1,0:T(8,128)(2,1)S(1)} %copy-done.18, bf16[2,16,8192]{2,1,0:T(8,128)(2,1)} %collective-permute-done.32.refs_2_, ...), custom_call_target="tpu_custom_call" | custom-call | flops 1 | bytes 1 | tf_op jit(solution)/shard_map/ring_sum/pallas_call | solution.py:43
  176.3 3.0 %collective-permute-start.33 = (bf16[16,8192]{1,0:T(8,128)(2,1)S(1)}, bf16[16,8192]{1,0:T(8,128)(2,1)S(1)}, u32[]{:S(2)}, u32[]{:S(2)}) collective-permute-start(bf16[16,8192]{1,0:T(8,128)(2,1)S(1)} %get-tuple-element.151), channel_id=1, source_target_pairs={{0,2},{1,3},{2,0},{3,1},{4,6},{5,7},{6,4},{7,5},{8,10},{9,11},{10,... | collective-permute-start | bytes 786440 | tf_op jit(solution)/shard_map/ppermute | solution.py:20
  179.3 4.2 %out_send.1 = (bf16[512,1024]{1,0:T(8,128)(2,1)}, bf16[2,256,640]{2,1,0:T(8,128)(2,1)S(1)}, f32[8,128]{1,0:T(8,128)S(1)}) custom-call(s32[7]{0:T(128)S(1)} %stack.31.at_ref, bf16[4,2,256,512]{3,2,1,0:T(8,128)(2,1)S(1)} %bitcast.32, bf16[4,2,256,512]{3,2,1,0:T(8,128)(2,1)S(1)} %bitcast.34, bf16[4,256,512]{2,1,0:T(8,128)(2,1)S(1)} %get-tuple-element.142.refs_2_, ...), custom_call_target="tpu_custom_call" | custom-call | flops 1 | bytes 1 | tf_op jit(solution)/shard_map/out_send/pallas_call | solution.py:43
  185.2 1.7 fusion
  187.0 13.4 %collective-permute-done.37.refs_4_ = bf16[2,256,640]{2,1,0:T(8,128)(2,1)S(1)} collective-permute-done((bf16[2,256,640]{2,1,0:T(8,128)(2,1)S(1)}, bf16[2,256,640]{2,1,0:T(8,128)(2,1)S(1)}, u32[]{:S(2)}, u32[]{:S(2)}) %collective-permute-start.37) | collective-permute-done | bytes 655392 | tf_op jit(solution)/shard_map/ppermute | solution.py:20
  201.2 9.3 %q_gradient.1 = (f32[1024,512]{1,0:T(8,128)}, f32[1024,128]{1,0:T(8,128)}, f32[8,128]{1,0:T(8,128)}) custom-call(s32[7]{0:T(128)} %copy-done.39, bf16[2,512,1024]{2,1,0:T(8,128)(2,1)} %get-tuple-element.153.refs_0_, bf16[2,512,1024]{2,1,0:T(8,128)(2,1)} %collective-permute-done.34.refs_1_, bf16[2,256,640]{2,1,0:T(8,128)(2,1)} %get-tuple-element.154.refs_3_.refs_2_, ...), custom_call_target="tpu_custom_call" | custom-call | flops 1 | bytes 1 | tf_op jit(solution)/shard_map/q_gradient/pallas_call | solution.py:43
  212.9 2.4 %add_terms.1 = (f32[512,1024]{1,0:T(8,128)}, f32[8,128]{1,0:T(8,128)}) custom-call(s32[7]{0:T(128)S(1)} %copy-done.40, f32[512,1024]{1,0:T(8,128)S(1)} %copy-done.12, bf16[512,1024]{1,0:T(8,128)(2,1)S(1)} %collective-permute-done.38.refs_7_.refs_1_, f32[8,128]{1,0:T(8,128)S(1)} %get-tuple-element.164.refs_2_), custom_call_target="tpu_custom_call" | custom-call | flops 1 | bytes 1 | tf_op jit(solution)/shard_map/add_terms/pallas_call | solution.py:43
  (170 shorter events, 38.9 us)
Async XLA Ops:
  0.6 10.3 %collective-permute-start = (bf16[256,512]{1,0:T(8,128)(2,1)}, bf16[256,512]{1,0:T(8,128)(2,1)S(1)}, u32[]{:S(2)}, u32[]{:S(2)}) collective-permute-start(bf16[256,512]{1,0:T(8,128)(2,1)} %bitcast.40), channel_id=1, source_target_pairs={{0,2},{1,3},{2,0},{3,1},{4,6},{5,7},{6,4},{7,5},{8,10},{9,11},{10,... | collective-permute-start | bytes 786440 | tf_op jit(solution)/shard_map/ppermute | solution.py:20
  2.1 11.1 %collective-permute-start.1 = (bf16[256,512]{1,0:T(8,128)(2,1)}, bf16[256,512]{1,0:T(8,128)(2,1)S(1)}, u32[]{:S(2)}, u32[]{:S(2)}) collective-permute-start(bf16[256,512]{1,0:T(8,128)(2,1)} %bitcast.41), channel_id=1, source_target_pairs={{0,4},{1,5},{2,6},{3,7},{4,0},{5,1},{6,2},{7,3},{8,12},{9,13},{10,... | collective-permute-start | bytes 786440 | tf_op jit(solution)/shard_map/ppermute | solution.py:20
  3.7 16.0 %collective-permute-start.3 = (bf16[256,512]{1,0:T(8,128)(2,1)}, bf16[256,512]{1,0:T(8,128)(2,1)S(1)}, u32[]{:S(2)}, u32[]{:S(2)}) collective-permute-start(bf16[256,512]{1,0:T(8,128)(2,1)} %bitcast.42), channel_id=1, source_target_pairs={{0,8},{1,9},{2,10},{3,11},{4,12},{5,13},{6,14},{7,15},{8,0},{9,1},... | collective-permute-start | bytes 786440 | tf_op jit(solution)/shard_map/ppermute | solution.py:20
  6.6 14.4 %collective-permute-start.5 = (bf16[256,512]{1,0:T(8,128)(2,1)}, bf16[256,512]{1,0:T(8,128)(2,1)S(1)}, u32[]{:S(2)}, u32[]{:S(2)}) collective-permute-start(bf16[256,512]{1,0:T(8,128)(2,1)} %bitcast.43), channel_id=1, source_target_pairs={{0,12},{1,13},{2,14},{3,15},{4,8},{5,9},{6,10},{7,11},{8,4},{9,5},... | collective-permute-start | bytes 786440 | tf_op jit(solution)/shard_map/ppermute | solution.py:20
  6.8 14.1 %collective-permute-start.7 = (bf16[256,512]{1,0:T(8,128)(2,1)}, bf16[256,512]{1,0:T(8,128)(2,1)S(1)}, u32[]{:S(2)}, u32[]{:S(2)}) collective-permute-start(bf16[256,512]{1,0:T(8,128)(2,1)} %bitcast.44), channel_id=1, source_target_pairs={{0,2},{1,3},{2,0},{3,1},{4,6},{5,7},{6,4},{7,5},{8,10},{9,11},{10,... | collective-permute-start | bytes 786440 | tf_op jit(solution)/shard_map/ppermute | solution.py:20
  11.0 11.9 %collective-permute-start.2 = (bf16[256,512]{1,0:T(8,128)(2,1)S(1)}, bf16[256,512]{1,0:T(8,128)(2,1)S(1)}, u32[]{:S(2)}, u32[]{:S(2)}) collective-permute-start(bf16[256,512]{1,0:T(8,128)(2,1)S(1)} %collective-permute-done), channel_id=1, source_target_pairs={{0,4},{1,5},{2,6},{3,7},{4,0},{5,1},{6,2},{7,3},{8,12},{9,13},{10,... | collective-permute-start | bytes 786440 | tf_op jit(solution)/shard_map/ppermute | solution.py:20
  13.2 16.3 %collective-permute-start.4 = (bf16[256,512]{1,0:T(8,128)(2,1)S(1)}, bf16[256,512]{1,0:T(8,128)(2,1)S(1)}, u32[]{:S(2)}, u32[]{:S(2)}) collective-permute-start(bf16[256,512]{1,0:T(8,128)(2,1)S(1)} %collective-permute-done), channel_id=1, source_target_pairs={{0,8},{1,9},{2,10},{3,11},{4,12},{5,13},{6,14},{7,15},{8,0},{9,1},... | collective-permute-start | bytes 786440 | tf_op jit(solution)/shard_map/ppermute | solution.py:20
  19.7 12.4 %collective-permute-start.6 = (bf16[256,512]{1,0:T(8,128)(2,1)S(1)}, bf16[256,512]{1,0:T(8,128)(2,1)S(1)}, u32[]{:S(2)}, u32[]{:S(2)}) collective-permute-start(bf16[256,512]{1,0:T(8,128)(2,1)S(1)} %collective-permute-done), channel_id=1, source_target_pairs={{0,12},{1,13},{2,14},{3,15},{4,8},{5,9},{6,10},{7,11},{8,4},{9,5},... | collective-permute-start | bytes 786440 | tf_op jit(solution)/shard_map/ppermute | solution.py:20
  19.9 20.9 %copy-start.49 = (bf16[8192]{0:T(1024)(128)(2,1)S(1)}, bf16[8192]{0:T(1024)(128)(2,1)}, u32[]{:S(2)}) copy-start(bf16[8192]{0:T(1024)(128)(2,1)} %param.9) | copy-start | bytes 49156
  20.0 159.3 %copy-start.39 = (s32[7]{0:T(128)}, s32[7]{0:T(128)S(1)}, u32[]{:S(2)}) copy-start(s32[7]{0:T(128)S(1)} %stack.31.at_ref) | copy-start | bytes 88
  34.0 11.0 %copy-start = (bf16[8192,512]{1,0:T(8,128)(2,1)S(1)}, bf16[8192,512]{1,0:T(8,128)(2,1)}, u32[]{:S(2)}) copy-start(bf16[8192,512]{1,0:T(8,128)(2,1)} %refs_1_.5) | copy-start | bytes 25165828
  35.2 6.0 %collective-permute-start.8 = (bf16[8,256,512]{2,1,0:T(8,128)(2,1)S(1)}, bf16[8,256,512]{2,1,0:T(8,128)(2,1)S(1)}, u32[]{:S(2)}, u32[]{:S(2)}) collective-permute-start(bf16[8,256,512]{2,1,0:T(8,128)(2,1)S(1)} %get-tuple-element.86.refs_0_.refs_1_), channel_id=1, source_target_pairs={{0,1},{1,0},{2,3},{3,2},{4,5},{5,4},{6,7},{7,6},{8,9},{9,8},{10,11... | collective-permute-start | bytes 6291464 | tf_op jit(solution)/shard_map/ppermute | solution.py:20
  36.3 19.3 %collective-permute-start.10 = (bf16[2,512,256]{2,1,0:T(8,128)(2,1)S(1)}, bf16[2,512,256]{2,1,0:T(8,128)(2,1)S(1)}, u32[]{:S(2)}, u32[]{:S(2)}) collective-permute-start(bf16[2,512,256]{2,1,0:T(8,128)(2,1)S(1)} %get-tuple-element.97), channel_id=1, source_target_pairs={{0,32},{16,48},{32,0},{48,16},{64,96},{80,112},{96,64},{112,80},{1... | collective-permute-start | bytes 1572872 | tf_op jit(solution)/shard_map/ppermute | solution.py:20
  38.3 20.1 %collective-permute-start.11 = (bf16[2,512,256]{2,1,0:T(8,128)(2,1)S(1)}, bf16[2,512,256]{2,1,0:T(8,128)(2,1)S(1)}, u32[]{:S(2)}, u32[]{:S(2)}) collective-permute-start(bf16[2,512,256]{2,1,0:T(8,128)(2,1)S(1)} %get-tuple-element.98), channel_id=1, source_target_pairs={{0,96},{16,112},{32,64},{48,80},{64,32},{80,48},{96,0},{112,16},{1... | collective-permute-start | bytes 1572872 | tf_op jit(solution)/shard_map/ppermute | solution.py:20
  40.8 17.6 %collective-permute-start.12 = (bf16[2,256,512]{2,1,0:T(8,128)(2,1)S(1)}, bf16[2,256,512]{2,1,0:T(8,128)(2,1)S(1)}, u32[]{:S(2)}, u32[]{:S(2)}) collective-permute-start(bf16[2,256,512]{2,1,0:T(8,128)(2,1)S(1)} %get-tuple-element.94.refs_1_.refs_0_), channel_id=1, source_target_pairs={{0,4},{1,5},{2,6},{3,7},{4,0},{5,1},{6,2},{7,3},{8,12},{9,13},{10,... | collective-permute-start | bytes 1572872 | tf_op jit(solution)/shard_map/ppermute | solution.py:20
  40.8 17.6 %collective-permute-start.13 = (bf16[2,256,512]{2,1,0:T(8,128)(2,1)S(1)}, bf16[2,256,512]{2,1,0:T(8,128)(2,1)S(1)}, u32[]{:S(2)}, u32[]{:S(2)}) collective-permute-start(bf16[2,256,512]{2,1,0:T(8,128)(2,1)S(1)} %get-tuple-element.94.refs_1_.refs_0_), channel_id=1, source_target_pairs={{0,12},{1,13},{2,14},{3,15},{4,8},{5,9},{6,10},{7,11},{8,4},{9,5},... | collective-permute-start | bytes 1572872 | tf_op jit(solution)/shard_map/ppermute | solution.py:20
  45.0 57.0 %copy-start.35 = (f32[256,1]{1,0:T(8,128)}, f32[256,1]{1,0:T(8,128)S(1)}, u32[]{:S(2)}) copy-start(f32[256,1]{1,0:T(8,128)S(1)} %get-tuple-element.126.refs_3_) | copy-start | bytes 3076
  45.0 16.3 %slice-start = ((s8[8388608]{0:T(1024)(128)(4,1)}), s8[4194304]{0:T(1024)(128)(4,1)S(1)}, s32[]{:S(2)}) async-start(s8[8388608]{0:T(1024)(128)(4,1)} %bitcast.29), calls=%async_computation.2 | async-start | bytes 8388608
  46.8 14.5 %slice-start.1 = ((s8[8388608]{0:T(1024)(128)(4,1)}), s8[4194304]{0:T(1024)(128)(4,1)S(1)}, s32[]{:S(2)}) async-start(s8[8388608]{0:T(1024)(128)(4,1)} %bitcast.29), calls=%async_computation.3 | async-start | bytes 8388608
  53.5 15.1 %collective-permute-start.15 = (bf16[2,512,256]{2,1,0:T(8,128)(2,1)S(1)}, bf16[2,512,256]{2,1,0:T(8,128)(2,1)S(1)}, u32[]{:S(2)}, u32[]{:S(2)}) collective-permute-start(bf16[2,512,256]{2,1,0:T(8,128)(2,1)S(1)} %get-tuple-element.104), channel_id=1, source_target_pairs={{0,64},{16,80},{32,96},{48,112},{64,0},{80,16},{96,32},{112,48},{1... | collective-permute-start | bytes 1572872 | tf_op jit(solution)/shard_map/ppermute | solution.py:20
  55.6 15.2 %collective-permute-start.16 = (bf16[2,256,512]{2,1,0:T(8,128)(2,1)S(1)}, bf16[2,256,512]{2,1,0:T(8,128)(2,1)S(1)}, u32[]{:S(2)}, u32[]{:S(2)}) collective-permute-start(bf16[2,256,512]{2,1,0:T(8,128)(2,1)S(1)} %get-tuple-element.105), channel_id=1, source_target_pairs={{0,8},{1,9},{2,10},{3,11},{4,12},{5,13},{6,14},{7,15},{8,0},{9,1},... | collective-permute-start | bytes 1572872 | tf_op jit(solution)/shard_map/ppermute | solution.py:20
  58.4 1.3 collective-permute-start.9
  66.9 11.3 %collective-permute-start.14 = (bf16[8,16,8192]{2,1,0:T(8,128)(2,1)S(1)}, bf16[8,16,8192]{2,1,0:T(8,128)(2,1)S(1)}, u32[]{:S(2)}, u32[]{:S(2)}) collective-permute-start(bf16[8,16,8192]{2,1,0:T(8,128)(2,1)S(1)} %get-tuple-element.102), channel_id=1, source_target_pairs={{0,1},{1,0},{2,3},{3,2},{4,5},{5,4},{6,7},{7,6},{8,9},{9,8},{10,11... | collective-permute-start | bytes 6291464 | tf_op jit(solution)/shard_map/ppermute | solution.py:20
  72.0 10.3 %collective-permute-start.23 = (bf16[8,256,512]{2,1,0:T(8,128)(2,1)S(1)}, bf16[8,256,512]{2,1,0:T(8,128)(2,1)S(1)}, u32[]{:S(2)}, u32[]{:S(2)}) collective-permute-start(bf16[8,256,512]{2,1,0:T(8,128)(2,1)S(1)} %get-tuple-element.107.refs_0_), channel_id=1, source_target_pairs={{0,1},{1,0},{2,3},{3,2},{4,5},{5,4},{6,7},{7,6},{8,9},{9,8},{10,11... | collective-permute-start | bytes 6291464 | tf_op jit(solution)/shard_map/ppermute | solution.py:20
  76.3 25.6 %collective-permute-start.25 = (bf16[512,1024]{1,0:T(8,128)(2,1)S(1)}, bf16[512,1024]{1,0:T(8,128)(2,1)S(1)}, u32[]{:S(2)}, u32[]{:S(2)}) collective-permute-start(bf16[512,1024]{1,0:T(8,128)(2,1)S(1)} %get-tuple-element.128), channel_id=1, source_target_pairs={{0,16},{16,0},{32,48},{48,32},{64,80},{80,64},{96,112},{112,96},{1... | collective-permute-start | bytes 3145736 | tf_op jit(solution)/shard_map/ppermute | solution.py:20
  76.4 20.0 %collective-permute-start.20 = (bf16[3,256,512]{2,1,0:T(8,128)(2,1)S(1)}, bf16[3,256,512]{2,1,0:T(8,128)(2,1)S(1)}, u32[]{:S(2)}, u32[]{:S(2)}) collective-permute-start(bf16[3,256,512]{2,1,0:T(8,128)(2,1)S(1)} %get-tuple-element.116), channel_id=1, source_target_pairs={{0,32},{16,48},{32,0},{48,16},{64,96},{80,112},{96,64},{112,80},{1... | collective-permute-start | bytes 2359304 | tf_op jit(solution)/shard_map/ppermute | solution.py:20
  77.5 20.9 %collective-permute-start.22 = (bf16[3,256,512]{2,1,0:T(8,128)(2,1)S(1)}, bf16[3,256,512]{2,1,0:T(8,128)(2,1)S(1)}, u32[]{:S(2)}, u32[]{:S(2)}) collective-permute-start(bf16[3,256,512]{2,1,0:T(8,128)(2,1)S(1)} %get-tuple-element.118), channel_id=1, source_target_pairs={{0,96},{16,112},{32,64},{48,80},{64,32},{80,48},{96,0},{112,16},{1... | collective-permute-start | bytes 2359304 | tf_op jit(solution)/shard_map/ppermute | solution.py:20
  80.7 21.2 %collective-permute-start.17 = (bf16[2,16,8192]{2,1,0:T(8,128)(2,1)S(1)}, bf16[2,16,8192]{2,1,0:T(8,128)(2,1)S(1)}, u32[]{:S(2)}, u32[]{:S(2)}) collective-permute-start(bf16[2,16,8192]{2,1,0:T(8,128)(2,1)S(1)} %get-tuple-element.112), channel_id=1, source_target_pairs={{0,4},{1,5},{2,6},{3,7},{4,0},{5,1},{6,2},{7,3},{8,12},{9,13},{10,... | collective-permute-start | bytes 1572872 | tf_op jit(solution)/shard_map/ppermute | solution.py:20
  82.2 19.8 %collective-permute-start.19 = (bf16[2,16,8192]{2,1,0:T(8,128)(2,1)S(1)}, bf16[2,16,8192]{2,1,0:T(8,128)(2,1)S(1)}, u32[]{:S(2)}, u32[]{:S(2)}) collective-permute-start(bf16[2,16,8192]{2,1,0:T(8,128)(2,1)S(1)} %get-tuple-element.114), channel_id=1, source_target_pairs={{0,12},{1,13},{2,14},{3,15},{4,8},{5,9},{6,10},{7,11},{8,4},{9,5},... | collective-permute-start | bytes 1572872 | tf_op jit(solution)/shard_map/ppermute | solution.py:20
  89.8 13.7 %copy-start.43 = (bf16[16,8192]{1,0:T(8,128)(2,1)}, bf16[16,8192]{1,0:T(8,128)(2,1)S(1)}, u32[]{:S(2)}) copy-start(bf16[16,8192]{1,0:T(8,128)(2,1)S(1)} %get-tuple-element.152.refs_4_) | copy-start | bytes 786436
  96.4 5.5 %collective-permute-start.24 = (bf16[256,128]{1,0:T(8,128)(2,1)S(1)}, bf16[256,128]{1,0:T(8,128)(2,1)S(1)}, u32[]{:S(2)}, u32[]{:S(2)}) collective-permute-start(bf16[256,128]{1,0:T(8,128)(2,1)S(1)} %get-tuple-element.125), channel_id=1, source_target_pairs={{0,1},{1,0},{2,3},{3,2},{4,5},{5,4},{6,7},{7,6},{8,9},{9,8},{10,11... | collective-permute-start | bytes 196616 | tf_op jit(solution)/shard_map/ppermute | solution.py:20
  110.4 4.5 %collective-permute-start.27 = (bf16[8,16,8192]{2,1,0:T(8,128)(2,1)S(1)}, bf16[8,16,8192]{2,1,0:T(8,128)(2,1)S(1)}, u32[]{:S(2)}, u32[]{:S(2)}) collective-permute-start(bf16[8,16,8192]{2,1,0:T(8,128)(2,1)S(1)} %get-tuple-element.134), channel_id=1, source_target_pairs={{0,1},{1,0},{2,3},{3,2},{4,5},{5,4},{6,7},{7,6},{8,9},{9,8},{10,11... | collective-permute-start | bytes 6291464 | tf_op jit(solution)/shard_map/ppermute | solution.py:20
  110.4 33.4 %collective-permute-start.21 = (bf16[3,256,512]{2,1,0:T(8,128)(2,1)}, bf16[3,256,512]{2,1,0:T(8,128)(2,1)S(1)}, u32[]{:S(2)}, u32[]{:S(2)}) collective-permute-start(bf16[3,256,512]{2,1,0:T(8,128)(2,1)} %get-tuple-element.117), channel_id=1, source_target_pairs={{0,64},{16,80},{32,96},{48,112},{64,0},{80,16},{96,32},{112,48},{1... | collective-permute-start | bytes 2359304 | tf_op jit(solution)/shard_map/ppermute | solution.py:20
  111.6 32.2 %collective-permute-start.18 = (bf16[2,16,8192]{2,1,0:T(8,128)(2,1)}, bf16[2,16,8192]{2,1,0:T(8,128)(2,1)S(1)}, u32[]{:S(2)}, u32[]{:S(2)}) collective-permute-start(bf16[2,16,8192]{2,1,0:T(8,128)(2,1)} %get-tuple-element.113), channel_id=1, source_target_pairs={{0,8},{1,9},{2,10},{3,11},{4,12},{5,13},{6,14},{7,15},{8,0},{9,1},... | collective-permute-start | bytes 1572872 | tf_op jit(solution)/shard_map/ppermute | solution.py:20
  118.5 25.4 %collective-permute-start.28 = (bf16[2,16,8192]{2,1,0:T(8,128)(2,1)}, bf16[2,16,8192]{2,1,0:T(8,128)(2,1)S(1)}, u32[]{:S(2)}, u32[]{:S(2)}) collective-permute-start(bf16[2,16,8192]{2,1,0:T(8,128)(2,1)} %get-tuple-element.137), channel_id=1, source_target_pairs={{0,4},{1,5},{2,6},{3,7},{4,0},{5,1},{6,2},{7,3},{8,12},{9,13},{10,... | collective-permute-start | bytes 1572872 | tf_op jit(solution)/shard_map/ppermute | solution.py:20
  118.9 25.0 %collective-permute-start.29 = (bf16[2,16,8192]{2,1,0:T(8,128)(2,1)}, bf16[2,16,8192]{2,1,0:T(8,128)(2,1)S(1)}, u32[]{:S(2)}, u32[]{:S(2)}) collective-permute-start(bf16[2,16,8192]{2,1,0:T(8,128)(2,1)} %get-tuple-element.138), channel_id=1, source_target_pairs={{0,12},{1,13},{2,14},{3,15},{4,8},{5,9},{6,10},{7,11},{8,4},{9,5},... | collective-permute-start | bytes 1572872 | tf_op jit(solution)/shard_map/ppermute | solution.py:20
  121.0 22.9 %collective-permute-start.26 = (bf16[256,640]{1,0:T(8,128)(2,1)}, bf16[256,640]{1,0:T(8,128)(2,1)}, u32[]{:S(2)}, u32[]{:S(2)}) collective-permute-start(bf16[256,640]{1,0:T(8,128)(2,1)} %get-tuple-element.129), channel_id=1, source_target_pairs={{0,16},{16,0},{32,48},{48,32},{64,80},{80,64},{96,112},{112,96},{1... | collective-permute-start | bytes 983048 | tf_op jit(solution)/shard_map/ppermute | solution.py:20
  152.1 4.2 %collective-permute-start.30 = (bf16[8,256,512]{2,1,0:T(8,128)(2,1)S(1)}, bf16[8,256,512]{2,1,0:T(8,128)(2,1)S(1)}, u32[]{:S(2)}, u32[]{:S(2)}) collective-permute-start(bf16[8,256,512]{2,1,0:T(8,128)(2,1)S(1)} %get-tuple-element.141), channel_id=1, source_target_pairs={{0,1},{1,0},{2,3},{3,2},{4,5},{5,4},{6,7},{7,6},{8,9},{9,8},{10,11... | collective-permute-start | bytes 6291464 | tf_op jit(solution)/shard_map/ppermute | solution.py:20
  152.2 27.0 %collective-permute-start.35 = (bf16[2,256,640]{2,1,0:T(8,128)(2,1)}, bf16[2,256,640]{2,1,0:T(8,128)(2,1)}, u32[]{:S(2)}, u32[]{:S(2)}) collective-permute-start(bf16[2,256,640]{2,1,0:T(8,128)(2,1)} %get-tuple-element.154.refs_3_.refs_2_), channel_id=1, source_target_pairs={{0,32},{16,48},{32,0},{48,16},{64,96},{80,112},{96,64},{112,80},{1... | collective-permute-start | bytes 1966088 | tf_op jit(solution)/shard_map/ppermute | solution.py:20
  152.8 26.4 %collective-permute-start.36 = (bf16[2,256,640]{2,1,0:T(8,128)(2,1)}, bf16[2,256,640]{2,1,0:T(8,128)(2,1)}, u32[]{:S(2)}, u32[]{:S(2)}) collective-permute-start(bf16[2,256,640]{2,1,0:T(8,128)(2,1)} %get-tuple-element.154.refs_3_.refs_2_), channel_id=1, source_target_pairs={{0,96},{16,112},{32,64},{48,80},{64,32},{80,48},{96,0},{112,16},{1... | collective-permute-start | bytes 1966088 | tf_op jit(solution)/shard_map/ppermute | solution.py:20
  154.9 15.5 %collective-permute-start.32 = (bf16[2,16,8192]{2,1,0:T(8,128)(2,1)}, bf16[2,16,8192]{2,1,0:T(8,128)(2,1)}, u32[]{:S(2)}, u32[]{:S(2)}) collective-permute-start(bf16[2,16,8192]{2,1,0:T(8,128)(2,1)} %get-tuple-element.148), channel_id=1, source_target_pairs={{0,8},{1,9},{2,10},{3,11},{4,12},{5,13},{6,14},{7,15},{8,0},{9,1},... | collective-permute-start | bytes 1572872 | tf_op jit(solution)/shard_map/ppermute | solution.py:20
  156.1 30.8 %collective-permute-start.34 = (bf16[2,512,1024]{2,1,0:T(8,128)(2,1)}, bf16[2,512,1024]{2,1,0:T(8,128)(2,1)}, u32[]{:S(2)}, u32[]{:S(2)}) collective-permute-start(bf16[2,512,1024]{2,1,0:T(8,128)(2,1)} %get-tuple-element.153.refs_0_), channel_id=1, source_target_pairs={{0,1},{1,0},{2,3},{3,2},{4,5},{5,4},{6,7},{7,6},{8,9},{9,8},{10,11... | collective-permute-start | bytes 6291464 | tf_op jit(solution)/shard_map/ppermute | solution.py:20
  163.0 22.2 %collective-permute-start.31 = (bf16[16,8192]{1,0:T(8,128)(2,1)}, bf16[16,8192]{1,0:T(8,128)(2,1)}, u32[]{:S(2)}, u32[]{:S(2)}) collective-permute-start(bf16[16,8192]{1,0:T(8,128)(2,1)} %get-tuple-element.146), channel_id=1, source_target_pairs={{0,2},{1,3},{2,0},{3,1},{4,6},{5,7},{6,4},{7,5},{8,10},{9,11},{10,... | collective-permute-start | bytes 786440 | tf_op jit(solution)/shard_map/ppermute | solution.py:20
  166.9 12.3 %copy-start.4 = (bf16[8,256,512]{2,1,0:T(8,128)(2,1)S(1)}, bf16[8,256,512]{2,1,0:T(8,128)(2,1)}, u32[]{:S(2)}) copy-start(bf16[8,256,512]{2,1,0:T(8,128)(2,1)} %copy-done.3) | copy-start | bytes 6291460
  176.3 34.3 %collective-permute-start.33 = (bf16[16,8192]{1,0:T(8,128)(2,1)S(1)}, bf16[16,8192]{1,0:T(8,128)(2,1)S(1)}, u32[]{:S(2)}, u32[]{:S(2)}) collective-permute-start(bf16[16,8192]{1,0:T(8,128)(2,1)S(1)} %get-tuple-element.151), channel_id=1, source_target_pairs={{0,2},{1,3},{2,0},{3,1},{4,6},{5,7},{6,4},{7,5},{8,10},{9,11},{10,... | collective-permute-start | bytes 786440 | tf_op jit(solution)/shard_map/ppermute | solution.py:20
  183.5 16.9 %copy-start.46 = (f32[8,128]{1,0:T(8,128)}, f32[8,128]{1,0:T(8,128)S(1)}, u32[]{:S(2)}) copy-start(f32[8,128]{1,0:T(8,128)S(1)} %get-tuple-element.157.refs_7_) | copy-start | bytes 12292
  183.5 16.9 %collective-permute-start.37 = (bf16[2,256,640]{2,1,0:T(8,128)(2,1)S(1)}, bf16[2,256,640]{2,1,0:T(8,128)(2,1)S(1)}, u32[]{:S(2)}, u32[]{:S(2)}) collective-permute-start(bf16[2,256,640]{2,1,0:T(8,128)(2,1)S(1)} %get-tuple-element.156), channel_id=1, source_target_pairs={{0,64},{16,80},{32,96},{48,112},{64,0},{80,16},{96,32},{112,48},{1... | collective-permute-start | bytes 1966088 | tf_op jit(solution)/shard_map/ppermute | solution.py:20
  184.9 25.6 %collective-permute-start.38 = (bf16[512,1024]{1,0:T(8,128)(2,1)}, bf16[512,1024]{1,0:T(8,128)(2,1)S(1)}, u32[]{:S(2)}, u32[]{:S(2)}) collective-permute-start(bf16[512,1024]{1,0:T(8,128)(2,1)} %get-tuple-element.159), channel_id=1, source_target_pairs={{0,16},{16,0},{32,48},{48,32},{64,80},{80,64},{96,112},{112,96},{1... | collective-permute-start | bytes 3145736 | tf_op jit(solution)/shard_map/ppermute | solution.py:20
  (43 other events, 160.5 us)
